TPU v7x, 32 devices: a whole 2x2x4 slice. The times are simulated.
32 devices in a mesh: seq: 8 (over z, y), tp: 4 (over x, core).
Axes of the slice: x: 2, y: 2, z: 4, core: 2. Of those that a mesh axis runs over, the one named last changes fastest.
Arguments:
- tokens: bfloat16 [2, 3072, 1536], P(None, 'seq'), may hold values from -6 to 6
- mix_gain: float32 [1536], replicated, may hold values from 0.1 to 1.9
- proj_b: bfloat16 [1536, 1536], P(None, 'tp'), may hold values from -0.15625 to 0.15625
- proj_c: bfloat16 [1536, 1536], P(None, 'tp'), may hold values from -0.15625 to 0.15625
- proj_x: bfloat16 [1536, 1536], P(None, 'tp'), may hold values from -0.15625 to 0.15625
- conv_taps: bfloat16 [3, 1536], P(None, 'tp'), may hold values from -3.5 to 3.5
- proj_out: bfloat16 [1536, 1536], P('tp'), may hold values from -0.15625 to 0.15625
- ffn_gain: float32 [1536], replicated, may hold values from 0.1 to 1.9
- w_gate: bfloat16 [1536, 6912], P(None, 'tp'), may hold values from -0.15625 to 0.15625
- w_up: bfloat16 [1536, 6912], P(None, 'tp'), may hold values from -0.15625 to 0.15625
- w_down: bfloat16 [6912, 1536], P('tp'), may hold values from -0.109375 to 0.109375
- cotangent: bfloat16 [2, 3072, 1536], P(None, 'seq'), may hold values from -6 to 6
- seq_lengths: int32 [2, 6], replicated, may hold values from 1 to 2048, 3072 in all within a row
- span_order: int32 [2, 24], replicated, may hold values from 0 to 23, as said below
- keep_mask: int32 [2, 3072], P(None, 'seq'), may hold values 0 or 1
Outputs:
- block_out: bfloat16 [2, 3072, 1536], P(None, 'seq')
- d_tokens: bfloat16 [2, 3072, 1536], P(None, 'seq')
- d_mixgain: float32 [1536], replicated
- d_projb: float32 [1536, 1536], P('seq', 'tp')
- d_projc: float32 [1536, 1536], P('seq', 'tp')
- d_projx: float32 [1536, 1536], P('seq', 'tp')
- d_convtaps: float32 [3, 1536], P(None, 'tp')
- d_projout: float32 [1536, 1536], P('tp', 'seq')
- d_ffngain: float32 [1536], replicated
- d_gate: float32 [1536, 6912], P('seq', 'tp')
- d_up: float32 [1536, 6912], P('seq', 'tp')
- d_down: float32 [6912, 1536], P('tp', 'seq')
Inputs may be any that keep to these rules, and one draw needn't show every extreme that they name: Each row of seq_lengths sums to 3072; its longest sequence has exactly 2048 tokens. `span_order`: each row is a permutation of the 24 stream blocks; slot s lies on index s // 3 of seq, and stream block c + 1 always lies on the seq index after that of block c, cyclically.
All inputs are finite; a program needn't handle non-finite values. No bound on the sum of `keep_mask` on one device may be relied on, other than what follows from the above.
Results may differ from a plain program's by a relative error of at most 0.011.
Values may be sent and summed in bfloat16 or wider, within the bound.
A program may use at most 192 MiB of HBM per device.

v0:
```python
import jax
import jax.numpy as jnp
from jax import lax
from jax.sharding import PartitionSpec as P

SPAN = 128
MICRO = 2


EPSILON = 1e-05


def passed_along(block, axis, distance):
    devices = range(lax.axis_size(axis))
    route = [((i - distance) % len(devices), i) for i in devices]
    return lax.ppermute(block, axis, route)


def body(
    tokens,
    mix_gain,
    proj_b,
    proj_c,
    proj_x,
    conv_taps,
    proj_out,
    ffn_gain,
    w_gate,
    w_up,
    w_down,
    cotangent,
    seq_lengths,
    span_order,
    keep_mask,
):
    f32 = jnp.float32
    bf16 = jnp.bfloat16
    seq_count = lax.axis_size("seq")
    device = lax.axis_index("seq")
    tok_local = tokens.shape[1]
    per_device = tok_local // SPAN
    chan_local = proj_b.shape[1]
    taps = conv_taps.astype(f32)
    gain_one = jnp.zeros(mix_gain.shape, f32)
    gain_two = jnp.zeros(ffn_gain.shape, f32)
    taps_grad = jnp.zeros(taps.shape, f32)
    pending = None
    sharded = None
    outputs = []
    input_grads = []
    for batch_idx in range(MICRO):
        order = span_order[batch_idx]
        mine = lax.dynamic_slice_in_dim(order, device * per_device, per_device)
        lengths = seq_lengths[batch_idx]
        starts = jnp.cumsum(lengths) - lengths
        position = mine[:, None] * SPAN + jnp.arange(SPAN, dtype=jnp.int32)[None, :]
        doc_start = jnp.max(
            jnp.where(starts[None, None, :] <= position[:, :, None], starts[None, None, :], 0),
            axis=2,
        )
        offset = position - doc_start
        valid_far = (offset >= 2).astype(f32)[:, :, None]
        valid_near = (offset >= 1).astype(f32)[:, :, None]
        inputs = tokens[batch_idx].astype(f32)
        scale_one = lax.rsqrt(jnp.mean(inputs * inputs, axis=-1, keepdims=True) + EPSILON)
        normal_one = inputs * scale_one
        normed = (normal_one * mix_gain).astype(bf16)
        gate_b = jnp.dot(normed, proj_b, preferred_element_type=f32)
        gate_c = jnp.dot(normed, proj_c, preferred_element_type=f32)
        values = jnp.dot(normed, proj_x, preferred_element_type=f32)
        product = (gate_b * values).astype(bf16).reshape(per_device, SPAN, chan_local)
        tails = product[:, SPAN - 2 :, :]
        before = passed_along(tails, "seq", 1)
        left_order = lax.dynamic_slice_in_dim(
            order, jnp.mod(device - 1, seq_count) * per_device, per_device
        )
        select = (left_order[None, :] == (mine - 1)[:, None]).astype(bf16)
        prior = jnp.einsum("ak,kjc->ajc", select, before, preferred_element_type=f32).astype(bf16)
        extended = jnp.concatenate([prior, product], axis=1).astype(f32)
        far_term = extended[:, :-2] * valid_far
        near_term = extended[:, 1:-1] * valid_near
        here_term = extended[:, 2:]
        convolved = (taps[0] * far_term + taps[1] * near_term + taps[2] * here_term).reshape(
            tok_local, chan_local
        )
        mixed = (gate_c * convolved).astype(bf16)
        branch_terms = jnp.dot(mixed, proj_out, preferred_element_type=f32)
        middle = inputs + lax.psum(branch_terms, "tp")
        scale_two = lax.rsqrt(jnp.mean(middle * middle, axis=-1, keepdims=True) + EPSILON)
        normal_two = middle * scale_two
        second_rows = (normal_two * ffn_gain).astype(bf16)
        gate_h = jnp.dot(second_rows, w_gate, preferred_element_type=f32)
        up_h = jnp.dot(second_rows, w_up, preferred_element_type=f32)
        sigma = jax.nn.sigmoid(gate_h)
        silu_h = gate_h * sigma
        hidden = (silu_h * up_h).astype(bf16)
        feed_terms = jnp.dot(hidden, w_down, preferred_element_type=f32)
        outputs.append((middle + lax.psum(feed_terms, "tp")).astype(bf16))
        grad_out = cotangent[batch_idx] * keep_mask[batch_idx].astype(bf16)[:, None]
        grad_down = jnp.einsum("tf,td->fd", hidden, grad_out, preferred_element_type=f32)
        grad_hidden = jnp.einsum("td,fd->tf", grad_out, w_down, preferred_element_type=f32)
        grad_gate = (grad_hidden * up_h * sigma * (1.0 + gate_h * (1.0 - sigma))).astype(bf16)
        grad_up = (grad_hidden * silu_h).astype(bf16)
        grad_wgate = jnp.einsum("td,tf->df", second_rows, grad_gate, preferred_element_type=f32)
        grad_wup = jnp.einsum("td,tf->df", second_rows, grad_up, preferred_element_type=f32)
        partial_second = jnp.einsum(
            "tf,df->td", grad_gate, w_gate, preferred_element_type=f32
        ) + jnp.einsum("tf,df->td", grad_up, w_up, preferred_element_type=f32)
        grad_second = lax.psum(partial_second, "tp")
        out_rows = grad_out.astype(f32)
        gain_two = gain_two + jnp.sum(grad_second * normal_two, axis=0)
        weighted_two = grad_second * ffn_gain
        grad_middle = out_rows + scale_two * (
            weighted_two - normal_two * jnp.mean(weighted_two * normal_two, axis=-1, keepdims=True)
        )
        branch_rows = grad_middle.astype(bf16)
        grad_wout = jnp.einsum("tc,td->cd", mixed, branch_rows, preferred_element_type=f32)
        grad_mixed = jnp.einsum("td,cd->tc", branch_rows, proj_out, preferred_element_type=f32)
        grad_c = (grad_mixed * convolved).astype(bf16)
        grad_conv = (grad_mixed * gate_c).reshape(per_device, SPAN, chan_local)
        taps_grad = taps_grad + jnp.stack(
            [
                jnp.sum(grad_conv * far_term, axis=(0, 1)),
                jnp.sum(grad_conv * near_term, axis=(0, 1)),
                jnp.sum(grad_conv * here_term, axis=(0, 1)),
            ]
        )
        grad_ext = (
            jnp.pad(taps[0] * valid_far * grad_conv, ((0, 0), (0, 2), (0, 0)))
            + jnp.pad(taps[1] * valid_near * grad_conv, ((0, 0), (1, 1), (0, 0)))
            + jnp.pad(taps[2] * grad_conv, ((0, 0), (2, 0), (0, 0)))
        )
        outgoing = grad_ext[:, :2, :]
        arrived = passed_along(outgoing, "seq", -1)
        right_order = lax.dynamic_slice_in_dim(
            order, jnp.mod(device + 1, seq_count) * per_device, per_device
        )
        route = (right_order[None, :] == (mine + 1)[:, None]).astype(f32)
        incoming = jnp.einsum(
            "ak,kjc->ajc",
            route,
            arrived,
            precision=lax.Precision.HIGHEST,
            preferred_element_type=f32,
        )
        grad_product = (
            grad_ext[:, 2:, :] + jnp.pad(incoming, ((0, 0), (SPAN - 2, 0), (0, 0)))
        ).reshape(tok_local, chan_local)
        grad_b = (grad_product * values).astype(bf16)
        grad_x = (grad_product * gate_b).astype(bf16)
        grad_wb = jnp.einsum("td,tc->dc", normed, grad_b, preferred_element_type=f32)
        grad_wc = jnp.einsum("td,tc->dc", normed, grad_c, preferred_element_type=f32)
        grad_wx = jnp.einsum("td,tc->dc", normed, grad_x, preferred_element_type=f32)
        partial_first = (
            jnp.einsum("tc,dc->td", grad_b, proj_b, preferred_element_type=f32)
            + jnp.einsum("tc,dc->td", grad_c, proj_c, preferred_element_type=f32)
            + jnp.einsum("tc,dc->td", grad_x, proj_x, preferred_element_type=f32)
        )
        grad_first = lax.psum(partial_first, "tp")
        gain_one = gain_one + jnp.sum(grad_first * normal_one, axis=0)
        weighted_one = grad_first * mix_gain
        grad_input = grad_middle + scale_one * (
            weighted_one - normal_one * jnp.mean(weighted_one * normal_one, axis=-1, keepdims=True)
        )
        input_rows = grad_input.astype(bf16)
        input_grads.append(input_rows)
        local_grads = (grad_wb, grad_wc, grad_wx, grad_wout, grad_wgate, grad_wup, grad_down)
        pending = (
            local_grads
            if pending is None
            else jax.tree.map(lambda left, right: left + right, pending, local_grads)
        )
    sharded = (
        lax.psum_scatter(pending[0], "seq", scatter_dimension=0, tiled=True),
        lax.psum_scatter(pending[1], "seq", scatter_dimension=0, tiled=True),
        lax.psum_scatter(pending[2], "seq", scatter_dimension=0, tiled=True),
        lax.psum_scatter(pending[3], "seq", scatter_dimension=1, tiled=True),
        lax.psum_scatter(pending[4], "seq", scatter_dimension=0, tiled=True),
        lax.psum_scatter(pending[5], "seq", scatter_dimension=0, tiled=True),
        lax.psum_scatter(pending[6], "seq", scatter_dimension=1, tiled=True),
    )
    small = lax.psum((gain_one, gain_two, taps_grad), "seq")
    return (
        jnp.stack(outputs),
        jnp.stack(input_grads),
        small[0],
        sharded[0],
        sharded[1],
        sharded[2],
        small[2],
        sharded[3],
        small[1],
        sharded[4],
        sharded[5],
        sharded[6],
    )


def solution(mesh):
    placed = (
        P(None, "seq", None),
        P(),
        P(None, "tp"),
        P(None, "tp"),
        P(None, "tp"),
        P(None, "tp"),
        P("tp", None),
        P(),
        P(None, "tp"),
        P(None, "tp"),
        P("tp", None),
        P(None, "seq", None),
        P(),
        P(),
        P(None, "seq"),
    )
    return jax.shard_map(
        body,
        mesh=mesh,
        in_specs=placed,
        out_specs=(
            P(None, "seq", None),
            P(None, "seq", None),
            P(),
            P("seq", "tp"),
            P("seq", "tp"),
            P("seq", "tp"),
            P(None, "tp"),
            P("tp", "seq"),
            P(),
            P("seq", "tp"),
            P("seq", "tp"),
            P("tp", "seq"),
        ),
        check_vma=False,
    )
```

profile of v0, /device:TPU:0, one launch (start us, length us, event | category | flops | bytes accessed | tf_op | source)
XLA Modules:
  0.0 1353.6 jit_solution(7254905157921798664)
XLA Ops:
  7.3 2.3 fusion.17
  9.7 2.2 fusion.83
  14.2 3.0 collective-permute-start.1
  44.5 2.2 fusion.102
  46.7 2.2 fusion.106
  50.2 93.3 %all-reduce.20.cloned.1.call-done = (f32[384,1536]{1,0:T(8,128)}, f32[384,1536]{1,0:T(8,128)}) async-done(((f32[384,1536]{1,0:T(8,128)}, f32[384,1536]{1,0:T(8,128)}), (f32[384,1536]{1,0:T(8,128)}, f32[384,1536]{1,0:T(8,128)})) %all-reduce.20.cloned.1.call-update) | async-done | bytes 4718608 | tf_op jit(solution)/shard_map/psum | solution.py:88
  143.5 3.1 multiply_reduce_fusion.5
  149.0 8.4 fusion.103
  157.4 4.4 fusion.104
  161.8 3.1 fusion.107
  164.9 3.1 fusion.108
  168.1 7.2 multiply_convert_fusion.2
  175.3 2.3 fusion.110
  177.6 5.0 multiply_convert_fusion
  182.6 2.3 fusion.112
  185.0 3.8 convolution_add_fusion.12
  188.8 3.8 convolution_add_fusion.11
  192.9 6.8 fusion.105
  199.6 6.2 fusion.109
  205.9 81.3 %all-reduce.18.cloned.1.call-done = (f32[384,1536]{1,0:T(8,128)}, f32[384,1536]{1,0:T(8,128)}) async-done(((f32[384,1536]{1,0:T(8,128)}, f32[384,1536]{1,0:T(8,128)}), (f32[384,1536]{1,0:T(8,128)}, f32[384,1536]{1,0:T(8,128)})) %all-reduce.18.cloned.1.call-update) | async-done | bytes 4718608 | tf_op jit(solution)/shard_map/psum | solution.py:109
  287.2 5.7 multiply_reduce_fusion.1
  293.7 3.0 multiply_add_fusion.1
  299.5 4.3 collective-permute-start.2
  307.3 2.4 collective-permute-done.3
  314.5 2.2 convolution_add_fusion.9
  317.6 2.2 convolution_add_fusion.7
  320.7 2.7 fusion.46
  323.5 2.4 convolution_add_fusion.3
  327.9 2.4 convolution_add_fusion.5
  332.3 2.5 convolution_add_fusion.4
  336.8 2.4 convolution_add_fusion.6
  339.8 4.9 fusion.114
  344.7 5.8 convolution_add_fusion.2
  350.6 4.9 fusion.115
  355.6 6.0 convolution_add_fusion.1
  362.2 5.2 fusion.30
  367.5 5.9 convolution_add_fusion
  374.2 116.3 %all-reduce.16.cloned.1.call-done = (f32[384,1536]{1,0:T(8,128)}, f32[384,1536]{1,0:T(8,128)}, f32[384,1536]{1,0:T(8,128)}, f32[384,1536]{1,0:T(8,128)}) async-done(((f32[384,1536]{1,0:T(8,128)}, f32[384,1536]{1,0:T(8,128)}, f32[384,1536]{1,0:T(8,128)}, f32[384,1536]{1,0:T(8,128)}), (f32[384,1536]{1,0:T(8,128)}, f32[384,1536]{1,0:T(8,128)}, f32[384,1536]{1,0:T(8,128)}, ...) | async-done | bytes 9437200 | tf_op jit(solution)/shard_map/psum | solution.py:98
  490.5 3.6 fusion.16
  494.1 38.0 %all-reduce.8 = (f32[1536]{0:T(1024)}, f32[3,384]{1,0:T(4,128)}, f32[1536]{0:T(1024)}) all-reduce(f32[1536]{0:T(1024)S(1)} %add.350, f32[3,384]{1,0:T(4,128)S(1)} %maximum_add_fusion, f32[1536]{0:T(1024)S(1)} %add.356), channel_id=1, replica_groups=mesh['seq'=8,'tp'=4] {'seq'}, use_global_device_ids=true, to_apply=%region_22.23 | all-reduce | flops 4224 | bytes 33792 | tf_op jit(solution)/shard_map/psum | solution.py:182
  532.0 4.5 fusion.29
  544.4 19.5 %reduce-scatter.14.cloned.1.call-done = f32[384,192]{0,1:T(8,128)} async-done(((f32[384,1536]{0,1:T(8,128)}), f32[384,192]{0,1:T(8,128)}) %reduce-scatter.14.cloned.1.call-update) | async-done | bytes 294928 | tf_op jit(solution)/shard_map/reduce_scatter | solution.py:177
  563.9 72.2 %reduce-scatter.10.cloned.1.call-done = f32[192,384]{1,0:T(8,128)} async-done(((f32[1536,384]{1,0:T(8,128)}), f32[192,384]{1,0:T(8,128)}) %reduce-scatter.10.cloned.1.call-update) | async-done | bytes 294928 | tf_op jit(solution)/shard_map/reduce_scatter | solution.py:175
  636.1 72.2 %reduce-scatter.12.cloned.1.call-done = f32[192,384]{1,0:T(8,128)} async-done(((f32[1536,384]{1,0:T(8,128)}), f32[192,384]{1,0:T(8,128)}) %reduce-scatter.12.cloned.1.call-update) | async-done | bytes 294928 | tf_op jit(solution)/shard_map/reduce_scatter | solution.py:176
  708.3 72.3 %reduce-scatter.8.cloned.1.call-done = f32[192,384]{1,0:T(8,128)} async-done(((f32[1536,384]{1,0:T(8,128)}), f32[192,384]{1,0:T(8,128)}) %reduce-scatter.8.cloned.1.call-update) | async-done | bytes 294928 | tf_op jit(solution)/shard_map/reduce_scatter | solution.py:174
  780.6 188.7 %reduce-scatter.16.cloned.1.call-done = f32[192,1728]{1,0:T(8,128)} async-done(((f32[1536,1728]{1,0:T(8,128)}), f32[192,1728]{1,0:T(8,128)}) %reduce-scatter.16.cloned.1.call-update) | async-done | bytes 1327120 | tf_op jit(solution)/shard_map/reduce_scatter | solution.py:178
  969.3 188.7 %reduce-scatter.18.cloned.1.call-done = f32[192,1728]{1,0:T(8,128)} async-done(((f32[1536,1728]{1,0:T(8,128)}), f32[192,1728]{1,0:T(8,128)}) %reduce-scatter.18.cloned.1.call-update) | async-done | bytes 1327120 | tf_op jit(solution)/shard_map/reduce_scatter | solution.py:179
  1158.0 188.6 %reduce-scatter.20.cloned.1.call-done = f32[1728,192]{0,1:T(8,128)} async-done(((f32[1728,1536]{0,1:T(8,128)}), f32[1728,192]{0,1:T(8,128)}) %reduce-scatter.20.cloned.1.call-update) | async-done | bytes 1327120 | tf_op jit(solution)/shard_map/reduce_scatter | solution.py:180
  (342 shorter events, 62.3 us)
Async XLA Ops:
  7.2 37.3 %copy-start = (bf16[384,1536]{1,0:T(8,128)(2,1)S(1)}, bf16[384,1536]{1,0:T(8,128)(2,1)}, u32[]{:S(2)}) copy-start(bf16[384,1536]{1,0:T(8,128)(2,1)} %param.21) | copy-start | bytes 3538948
  7.2 136.3 %all-reduce.20.cloned.1.call-start = ((), (), s32[]{:S(2)}) async-start(), calls=%async_computation.16 | async-start | bytes 9437184 | tf_op jit(solution)/shard_map/psum | solution.py:88
  9.6 30.9 %copy-start.93 = (f32[384]{0:T(512)}, f32[384]{0:T(512)S(1)}, u32[]{:S(2)}) copy-start(f32[384]{0:T(512)S(1)} %get-tuple-element.113) | copy-start | bytes 4612
  9.6 33.2 %copy-start.71 = (f32[384]{0:T(512)}, f32[384]{0:T(512)S(1)}, u32[]{:S(2)}) copy-start(f32[384]{0:T(512)S(1)} %get-tuple-element.112) | copy-start | bytes 4612
  11.9 5.3 copy-start.35
  13.5 6.1 copy-start.68
  14.2 21.5 %collective-permute-start.1 = (bf16[3,2,384]{2,1,0:T(2,128)(2,1)}, bf16[3,2,384]{2,1,0:T(2,128)(2,1)}, u32[]{:S(2)}, u32[]{:S(2)}) collective-permute-start(bf16[3,2,384]{2,1,0:T(2,128)(2,1)} %slice.118), channel_id=1, source_target_pairs={{28,0},{0,4},{4,8},{8,12},{12,16},{16,20},{20,24},{24,28},{29,1},{... | collective-permute-start | bytes 13832 | tf_op jit(solution)/shard_map/ppermute | solution.py:16
  21.0 16.6 %collective-permute-start = (bf16[3,2,384]{2,1,0:T(2,128)(2,1)}, bf16[3,2,384]{2,1,0:T(2,128)(2,1)}, u32[]{:S(2)}, u32[]{:S(2)}) collective-permute-start(bf16[3,2,384]{2,1,0:T(2,128)(2,1)} %slice.112), channel_id=1, source_target_pairs={{28,0},{0,4},{4,8},{8,12},{12,16},{16,20},{20,24},{24,28},{29,1},{... | collective-permute-start | bytes 13832 | tf_op jit(solution)/shard_map/ppermute | solution.py:16
  34.1 6.1 copy-start.89
  34.1 6.1 copy-start.91
  34.9 5.3 copy-start.85
  34.9 5.3 copy-start.87
  48.9 238.3 %all-reduce.18.cloned.1.call-start = ((), (), s32[]{:S(2)}) async-start(), calls=%async_computation.15 | async-start | bytes 9437184 | tf_op jit(solution)/shard_map/psum | solution.py:109
  146.6 10.7 slice-start.4
  148.9 8.4 copy-start.20
  148.9 16.0 %copy-start.16 = (bf16[384,1536]{1,0:T(8,128)(2,1)}, bf16[384,1536]{1,0:T(8,128)(2,1)S(1)}, u32[]{:S(2)}) copy-start(bf16[384,1536]{1,0:T(8,128)(2,1)S(1)} %get-tuple-element.79) | copy-start | bytes 3538948
  148.9 8.4 slice-start.5
  149.0 12.9 slice-start
  161.8 6.2 slice-start.2
  175.3 9.7 copy-start.30
  182.6 6.2 copy-start.28
  192.6 297.8 %all-reduce.16.cloned.1.call-start = ((), (), s32[]{:S(2)}) async-start(), calls=%async_computation.14 | async-start | bytes 18874368 | tf_op jit(solution)/shard_map/psum | solution.py:98
  192.9 6.8 copy-start.18
  287.2 5.8 copy-start.4
  287.2 5.8 copy-start.7
  287.2 5.9 copy-start.22
  287.2 6.5 copy-start.24
  287.2 6.5 copy-start.82
  287.2 6.5 copy-start.84
  287.2 6.5 copy-start.96
  287.2 6.5 copy-start.99
  296.8 7.0 copy-start.10
  298.1 14.5 %copy-start.49 = (bf16[384,384]{1,0:T(8,128)(2,1)}, bf16[384,384]{1,0:T(8,128)(2,1)S(1)}, u32[]{:S(2)}) copy-start(bf16[384,384]{1,0:T(8,128)(2,1)S(1)} %get-tuple-element.70) | copy-start | bytes 884740
  299.5 7.6 collective-permute-start.2
  304.6 12.1 copy-start.37
  306.0 3.7 collective-permute-start.3
  311.7 5.8 copy-start.39
  319.8 244.1 %reduce-scatter.14.cloned.1.call-start = ((), (), s32[]{:S(2)}) async-start(), calls=%async_computation.10 | async-start | bytes 2654208 | tf_op jit(solution)/shard_map/reduce_scatter | solution.py:177
  326.0 310.2 %reduce-scatter.10.cloned.1.call-start = ((), (), s32[]{:S(2)}) async-start(), calls=%async_computation.8 | async-start | bytes 2654208 | tf_op jit(solution)/shard_map/reduce_scatter | solution.py:175
  330.4 377.9 %reduce-scatter.12.cloned.1.call-start = ((), (), s32[]{:S(2)}) async-start(), calls=%async_computation.9 | async-start | bytes 2654208 | tf_op jit(solution)/shard_map/reduce_scatter | solution.py:176
  334.9 445.8 %reduce-scatter.8.cloned.1.call-start = ((), (), s32[]{:S(2)}) async-start(), calls=%async_computation.7 | async-start | bytes 2654208 | tf_op jit(solution)/shard_map/reduce_scatter | solution.py:174
  339.3 5.4 copy-start.17
  339.3 630.0 %reduce-scatter.16.cloned.1.call-start = ((), (), s32[]{:S(2)}) async-start(), calls=%async_computation.11 | async-start | bytes 12386304 | tf_op jit(solution)/shard_map/reduce_scatter | solution.py:178
  350.5 807.5 %reduce-scatter.18.cloned.1.call-start = ((), (), s32[]{:S(2)}) async-start(), calls=%async_computation.12 | async-start | bytes 12386304 | tf_op jit(solution)/shard_map/reduce_scatter | solution.py:179
  361.6 5.9 copy-start.97
  361.6 985.0 %reduce-scatter.20.cloned.1.call-start = ((), (), s32[]{:S(2)}) async-start(), calls=%async_computation.13 | async-start | bytes 12386304 | tf_op jit(solution)/shard_map/reduce_scatter | solution.py:180
  362.2 5.2 copy-start.23
  542.2 804.4 %copy-start.1 = (bf16[384,1536]{1,0:T(8,128)(2,1)S(1)}, bf16[384,1536]{1,0:T(8,128)(2,1)}, u32[]{:S(2)}) copy-start(bf16[384,1536]{1,0:T(8,128)(2,1)} %param.21) | copy-start | bytes 3538948
  (86 other events, 187.1 us)
Sparse Core Ops, SparseCore 0:
  49.0 94.4 all-reduce.19
  192.8 94.3 all-reduce.17
  319.9 170.5 all-reduce.15
  494.4 69.4 reduce-scatter.13
  567.8 68.2 reduce-scatter.9
  640.0 68.2 reduce-scatter.11
  712.4 68.1 reduce-scatter.7
  784.8 184.4 reduce-scatter.15
  973.5 184.4 reduce-scatter.17
  1162.1 184.4 reduce-scatter.19
where the time goes:
time: 1360 us; the launch traced here: 1350 us
  waiting for transfers between devices  1100 us (81%)
  matrix products  130 us (10%)
  other arithmetic  42.5 us (3%)
  blocking collectives  38 us (3%)
  local copies, waits for them, and re-layouts  19.9 us (1%)
  between operations  15.7 us (1%)
    reduce_scatter x1, waiting for transfers between devices, body(): lax.psum_scatter(pending[5], 'seq', scatter_dimension=0, tiled=True)  189 us
    reduce_scatter x1, waiting for transfers between devices, body(): lax.psum_scatter(pending[4], 'seq', scatter_dimension=0, tiled=True)  189 us
    reduce_scatter x1, waiting for transfers between devices, body(): lax.psum_scatter(pending[6], 'seq', scatter_dimension=1, tiled=True)  189 us
    psum x1, waiting for transfers between devices, body(): outputs.append((middle + lax.psum(feed_terms, 'tp')).astype(bf16))  116 us
    psum x1, waiting for transfers between devices, body(): middle = inputs + lax.psum(branch_terms, 'tp')  93.3 us
    psum x1, waiting for transfers between devices, body(): grad_second = lax.psum(partial_second, 'tp')  81.3 us
    reduce_scatter x1, waiting for transfers between devices, body(): lax.psum_scatter(pending[0], 'seq', scatter_dimension=0, tiled=True)  72.3 us
    reduce_scatter x1, waiting for transfers between devices, body(): lax.psum_scatter(pending[2], 'seq', scatter_dimension=0, tiled=True)  72.2 us
  transfers between devices with their start and end apart: 14, of which 11 were waited for; matrix products, arithmetic and copies ran while one was open for 7% of the time, Pallas kernels for 0%

commit v1 on v0

--- a/solution.py
+++ b/solution.py
@@ -85,7 +85,7 @@
         )
         mixed = (gate_c * convolved).astype(bf16)
         branch_terms = jnp.dot(mixed, proj_out, preferred_element_type=f32)
-        middle = inputs + lax.psum(branch_terms, "tp")
+        middle = inputs + lax.psum(branch_terms.astype(bf16), "tp").astype(f32)
         scale_two = lax.rsqrt(jnp.mean(middle * middle, axis=-1, keepdims=True) + EPSILON)
         normal_two = middle * scale_two
         second_rows = (normal_two * ffn_gain).astype(bf16)
@@ -95,7 +95,7 @@
         silu_h = gate_h * sigma
         hidden = (silu_h * up_h).astype(bf16)
         feed_terms = jnp.dot(hidden, w_down, preferred_element_type=f32)
-        outputs.append((middle + lax.psum(feed_terms, "tp")).astype(bf16))
+        outputs.append((middle + lax.psum(feed_terms.astype(bf16), "tp").astype(f32)).astype(bf16))
         grad_out = cotangent[batch_idx] * keep_mask[batch_idx].astype(bf16)[:, None]
         grad_down = jnp.einsum("tf,td->fd", hidden, grad_out, preferred_element_type=f32)
         grad_hidden = jnp.einsum("td,fd->tf", grad_out, w_down, preferred_element_type=f32)
@@ -106,7 +106,7 @@
         partial_second = jnp.einsum(
             "tf,df->td", grad_gate, w_gate, preferred_element_type=f32
         ) + jnp.einsum("tf,df->td", grad_up, w_up, preferred_element_type=f32)
-        grad_second = lax.psum(partial_second, "tp")
+        grad_second = lax.psum(partial_second.astype(bf16), "tp").astype(f32)
         out_rows = grad_out.astype(f32)
         gain_two = gain_two + jnp.sum(grad_second * normal_two, axis=0)
         weighted_two = grad_second * ffn_gain
@@ -156,7 +156,7 @@
             + jnp.einsum("tc,dc->td", grad_c, proj_c, preferred_element_type=f32)
             + jnp.einsum("tc,dc->td", grad_x, proj_x, preferred_element_type=f32)
         )
-        grad_first = lax.psum(partial_first, "tp")
+        grad_first = lax.psum(partial_first.astype(bf16), "tp").astype(f32)
         gain_one = gain_one + jnp.sum(grad_first * normal_one, axis=0)
         weighted_one = grad_first * mix_gain
         grad_input = grad_middle + scale_one * (
@@ -171,13 +171,13 @@
             else jax.tree.map(lambda left, right: left + right, pending, local_grads)
         )
     sharded = (
-        lax.psum_scatter(pending[0], "seq", scatter_dimension=0, tiled=True),
-        lax.psum_scatter(pending[1], "seq", scatter_dimension=0, tiled=True),
-        lax.psum_scatter(pending[2], "seq", scatter_dimension=0, tiled=True),
-        lax.psum_scatter(pending[3], "seq", scatter_dimension=1, tiled=True),
-        lax.psum_scatter(pending[4], "seq", scatter_dimension=0, tiled=True),
-        lax.psum_scatter(pending[5], "seq", scatter_dimension=0, tiled=True),
-        lax.psum_scatter(pending[6], "seq", scatter_dimension=1, tiled=True),
+        lax.psum_scatter(pending[0].astype(bf16), "seq", scatter_dimension=0, tiled=True).astype(f32),
+        lax.psum_scatter(pending[1].astype(bf16), "seq", scatter_dimension=0, tiled=True).astype(f32),
+        lax.psum_scatter(pending[2].astype(bf16), "seq", scatter_dimension=0, tiled=True).astype(f32),
+        lax.psum_scatter(pending[3].astype(bf16), "seq", scatter_dimension=1, tiled=True).astype(f32),
+        lax.psum_scatter(pending[4].astype(bf16), "seq", scatter_dimension=0, tiled=True).astype(f32),
+        lax.psum_scatter(pending[5].astype(bf16), "seq", scatter_dimension=0, tiled=True).astype(f32),
+        lax.psum_scatter(pending[6].astype(bf16), "seq", scatter_dimension=1, tiled=True).astype(f32),
     )
     small = lax.psum((gain_one, gain_two, taps_grad), "seq")
     return (

time: 1360 us -> 918 us (0.68)
  waiting for transfers between devices: 1100 us -> 654 us
  other arithmetic: 42.5 us -> 57.6 us
    reduce_scatter x7, waiting for transfers between devices: 802 us -> 461 us  [the longest x1 108 us: body(): lax.psum_scatter(pending[5].astype(bf16), 'seq', scatter_dimension=0, til...]
    psum x3, waiting for transfers between devices: 291 us -> 193 us  [the longest x1 94.4 us: body(): lax.psum(feed_terms.astype(bf16), 'tp').astype(f32)]
  transfers between devices with their start and end apart: 14 -> 14, of which waited for: 11 -> 9; matrix products, arithmetic and copies ran while one was open for 7% -> 12% of each run, Pallas kernels for 0% -> 0%
where the time goes in v1:
time: 918 us; the launch traced here: 912 us
  waiting for transfers between devices  654 us (71%)
  matrix products  123 us (13%)
  other arithmetic  57.6 us (6%)
  blocking collectives  37.4 us (4%)
  between operations  16.1 us (2%)
  local copies, waits for them, and re-layouts  12.6 us (1%)
  starting transfers between devices  10.9 us (1%)
    reduce_scatter x1, waiting for transfers between devices, body(): lax.psum_scatter(pending[5].astype(bf16), 'seq', scatter_dimension=0, til...  108 us
    reduce_scatter x1, waiting for transfers between devices, body(): lax.psum_scatter(pending[4].astype(bf16), 'seq', scatter_dimension=0, til...  107 us
    psum x1, waiting for transfers between devices, body(): lax.psum(feed_terms.astype(bf16), 'tp').astype(f32)  94.4 us
    reduce_scatter x1, waiting for transfers between devices, body(): lax.psum_scatter(pending[0].astype(bf16), 'seq', scatter_dimension=0, til...  64.7 us
    reduce_scatter x1, waiting for transfers between devices, body(): lax.psum_scatter(pending[2].astype(bf16), 'seq', scatter_dimension=0, til...  63.1 us
    reduce_scatter x1, waiting for transfers between devices, body(): lax.psum_scatter(pending[6].astype(bf16), 'seq', scatter_dimension=1, til...  60.4 us
    reduce_scatter x1, waiting for transfers between devices, body(): lax.psum_scatter(pending[1].astype(bf16), 'seq', scatter_dimension=0, til...  57.6 us
    psum x1, waiting for transfers between devices, body(): middle = inputs + lax.psum(branch_terms.astype(bf16), 'tp').astype(f32)  55.4 us
  transfers between devices with their start and end apart: 14, of which 9 were waited for; matrix products, arithmetic and copies ran while one was open for 12% of the time, Pallas kernels for 0%

profile of v1, /device:TPU:0, one launch (start us, length us, event | category | flops | bytes accessed | tf_op | source)
XLA Modules:
  0.0 912.1 jit_solution(3146030273833121987)
XLA Ops:
  7.3 2.3 fusion.41
  9.7 2.2 fusion.117
  14.2 3.0 collective-permute-start
  39.9 1.8 convolution_convert_fusion.2
  44.3 55.4 %all-reduce.20.cloned.1.call-done = (bf16[384,1536]{1,0:T(8,128)(2,1)}, bf16[384,1536]{1,0:T(8,128)(2,1)}) async-done(((bf16[384,1536]{1,0:T(8,128)(2,1)}, bf16[384,1536]{1,0:T(8,128)(2,1)}), (bf16[384,1536]{1,0:T(8,128)(2,1)}, bf16[384,1536]{1,0:T(8,128)(2,1)})) %all-reduce.20.cloned.1.call-update) | async-done | bytes 2359312 | tf_op jit(solution)/shard_map/psum | solution.py:88
  99.7 2.6 multiply_reduce_fusion.1
  103.3 8.2 fusion.125
  111.5 4.4 fusion.124
  116.0 3.1 fusion.127
  119.1 3.1 fusion.126
  122.2 6.9 multiply_convert_fusion.2
  129.1 2.3 fusion.128
  131.5 5.0 multiply_convert_fusion
  136.5 2.3 fusion.130
  138.9 3.4 fusion.20
  142.3 3.4 fusion.21
  146.2 6.4 convolution_convert_fusion.1
  152.6 5.9 convolution_convert_fusion
  158.4 43.4 %all-reduce.18.cloned.1.call-done = (bf16[384,1536]{1,0:T(8,128)(2,1)}, bf16[384,1536]{1,0:T(8,128)(2,1)}) async-done(((bf16[384,1536]{1,0:T(8,128)(2,1)}, bf16[384,1536]{1,0:T(8,128)(2,1)}), (bf16[384,1536]{1,0:T(8,128)(2,1)}, bf16[384,1536]{1,0:T(8,128)(2,1)})) %all-reduce.18.cloned.1.call-update) | async-done | bytes 2359312 | tf_op jit(solution)/shard_map/psum | solution.py:109
  201.9 4.8 fusion.36
  206.8 2.2 fusion.35
  211.2 2.0 fusion.19
  213.3 2.8 fusion.62
  217.8 4.2 collective-permute-start.2
  228.4 2.1 fusion.17
  239.7 1.9 fusion.15
  242.4 1.9 fusion.14
  246.3 2.1 fusion.18
  249.6 2.1 fusion.16
  252.0 5.0 fusion.52
  257.1 5.3 add_convert_fusion
  263.6 4.7 fusion.133
  268.3 4.9 add_convert_fusion.1
  273.5 4.6 fusion.132
  278.2 4.9 add_convert_fusion.2
  286.1 57.6 %reduce-scatter.10.cloned.1.call-done = bf16[192,384]{1,0:T(8,128)(2,1)} async-done(((bf16[1536,384]{1,0:T(8,128)(2,1)}), bf16[192,384]{1,0:T(8,128)(2,1)}) %reduce-scatter.10.cloned.1.call-update) | async-done | bytes 147472 | tf_op jit(solution)/shard_map/reduce_scatter | solution.py:175
  345.4 94.4 %all-reduce.16.cloned.1.call-done = (bf16[384,1536]{1,0:T(8,128)(2,1)}, bf16[384,1536]{1,0:T(8,128)(2,1)}, bf16[384,1536]{1,0:T(8,128)(2,1)}, bf16[384,1536]{1,0:T(8,128)(2,1)}) async-done(((bf16[384,1536]{1,0:T(8,128)(2,1)}, bf16[384,1536]{1,0:T(8,128)(2,1)}, bf16[384,1536]{1,0:T(8,128)(2,1)}, bf16[384,1536]{1,0:T(8,128)(2,1)}), (bf16[384,1536]{1,0:T(8,128)(2,1)}, bf16[384,1536]{1,0:T(8,128)(2,1)}, ...) | async-done | bytes 4718608 | tf_op jit(solution)/shard_map/psum | solution.py:98
  439.8 3.8 fusion.40
  444.2 63.1 %reduce-scatter.12.cloned.1.call-done = bf16[192,384]{1,0:T(8,128)(2,1)} async-done(((bf16[1536,384]{1,0:T(8,128)(2,1)}), bf16[192,384]{1,0:T(8,128)(2,1)}) %reduce-scatter.12.cloned.1.call-update) | async-done | bytes 147472 | tf_op jit(solution)/shard_map/reduce_scatter | solution.py:176
  508.9 64.7 %reduce-scatter.8.cloned.1.call-done = bf16[192,384]{1,0:T(8,128)(2,1)} async-done(((bf16[1536,384]{1,0:T(8,128)(2,1)}), bf16[192,384]{1,0:T(8,128)(2,1)}) %reduce-scatter.8.cloned.1.call-update) | async-done | bytes 147472 | tf_op jit(solution)/shard_map/reduce_scatter | solution.py:174
  575.3 37.4 %all-reduce.8 = (f32[1536]{0:T(1024)}, f32[3,384]{1,0:T(4,128)}, f32[1536]{0:T(1024)}) all-reduce(f32[1536]{0:T(1024)} %add.350, f32[3,384]{1,0:T(4,128)} %maximum_add_fusion, f32[1536]{0:T(1024)S(1)} %add.356), channel_id=1, replica_groups=mesh['seq'=8,'tp'=4] {'seq'}, use_global_device_ids=true, to_apply=%region_22.23 | all-reduce | flops 4224 | bytes 33792 | tf_op jit(solution)/shard_map/psum | solution.py:182
  614.0 5.3 fusion.50
  622.6 60.4 %reduce-scatter.20.cloned.1.call-done = bf16[1728,192]{0,1:T(8,128)(2,1)} async-done(((bf16[1728,1536]{0,1:T(8,128)(2,1)}), bf16[1728,192]{0,1:T(8,128)(2,1)}) %reduce-scatter.20.cloned.1.call-update) | async-done | bytes 663568 | tf_op jit(solution)/shard_map/reduce_scatter | solution.py:180
  682.9 2.4 convert_element_type.333
  685.3 107.7 %reduce-scatter.18.cloned.1.call-done = bf16[192,1728]{1,0:T(8,128)(2,1)} async-done(((bf16[1536,1728]{1,0:T(8,128)(2,1)}), bf16[192,1728]{1,0:T(8,128)(2,1)}) %reduce-scatter.18.cloned.1.call-update) | async-done | bytes 663568 | tf_op jit(solution)/shard_map/reduce_scatter | solution.py:179
  793.1 2.3 convert_element_type.331
  795.3 107.2 %reduce-scatter.16.cloned.1.call-done = bf16[192,1728]{1,0:T(8,128)(2,1)} async-done(((bf16[1536,1728]{1,0:T(8,128)(2,1)}), bf16[192,1728]{1,0:T(8,128)(2,1)}) %reduce-scatter.16.cloned.1.call-update) | async-done | bytes 663568 | tf_op jit(solution)/shard_map/reduce_scatter | solution.py:178
  902.6 2.3 convert_element_type.329
  (335 shorter events, 66.9 us)
Async XLA Ops:
  7.2 32.7 %copy-start = (bf16[384,1536]{1,0:T(8,128)(2,1)S(1)}, bf16[384,1536]{1,0:T(8,128)(2,1)}, u32[]{:S(2)}) copy-start(bf16[384,1536]{1,0:T(8,128)(2,1)} %param.21) | copy-start | bytes 3538948
  7.2 92.5 %all-reduce.20.cloned.1.call-start = ((), (), s32[]{:S(2)}) async-start(), calls=%async_computation.16 | async-start | bytes 4718592 | tf_op jit(solution)/shard_map/psum | solution.py:88
  9.6 8.4 copy-start.85
  11.9 5.3 copy-start.31
  13.5 6.2 copy-start.65
  14.2 16.2 %collective-permute-start = (bf16[3,2,384]{2,1,0:T(2,128)(2,1)}, bf16[3,2,384]{2,1,0:T(2,128)(2,1)}, u32[]{:S(2)}, u32[]{:S(2)}) collective-permute-start(bf16[3,2,384]{2,1,0:T(2,128)(2,1)} %slice.112), channel_id=1, source_target_pairs={{28,0},{0,4},{4,8},{8,12},{12,16},{16,20},{20,24},{24,28},{29,1},{... | collective-permute-start | bytes 13832 | tf_op jit(solution)/shard_map/ppermute | solution.py:16
  21.0 11.3 %collective-permute-start.1 = (bf16[3,2,384]{2,1,0:T(2,128)(2,1)}, bf16[3,2,384]{2,1,0:T(2,128)(2,1)}, u32[]{:S(2)}, u32[]{:S(2)}) collective-permute-start(bf16[3,2,384]{2,1,0:T(2,128)(2,1)} %slice.118), channel_id=1, source_target_pairs={{28,0},{0,4},{4,8},{8,12},{12,16},{16,20},{20,24},{24,28},{29,1},{... | collective-permute-start | bytes 13832 | tf_op jit(solution)/shard_map/ppermute | solution.py:16
  29.6 5.2 copy-start.77
  29.6 5.3 copy-start.79
  29.7 5.2 copy-start.81
  29.7 5.2 copy-start.83
  43.5 158.4 %all-reduce.18.cloned.1.call-start = ((), (), s32[]{:S(2)}) async-start(), calls=%async_computation.15 | async-start | bytes 4718592 | tf_op jit(solution)/shard_map/psum | solution.py:109
  102.4 9.1 %slice-start = ((s8[5308416]{0:T(1024)(128)(4,1)}), s8[4194304]{0:T(1024)(128)(4,1)S(1)}, s32[]{:S(2)}) async-start(s8[5308416]{0:T(1024)(128)(4,1)} %bitcast.210), calls=%async_computation.17 | async-start | bytes 8388608
  103.3 8.2 copy-start.15
  103.3 15.8 %copy-start.17 = (bf16[384,1536]{1,0:T(8,128)(2,1)}, bf16[384,1536]{1,0:T(8,128)(2,1)S(1)}, u32[]{:S(2)}) copy-start(bf16[384,1536]{1,0:T(8,128)(2,1)S(1)} %get-tuple-element.61) | copy-start | bytes 3538948
  103.3 8.2 slice-start.1
  103.3 12.7 %slice-start.2 = ((s8[5308416]{0:T(1024)(128)(4,1)}), s8[4194304]{0:T(1024)(128)(4,1)S(1)}, s32[]{:S(2)}) async-start(s8[5308416]{0:T(1024)(128)(4,1)} %bitcast.212), calls=%async_computation.19 | async-start | bytes 8388608
  116.0 6.2 slice-start.4
  129.1 9.7 %copy-start.24 = (bf16[384,1728]{0,1:T(8,128)(2,1)}, bf16[384,1728]{0,1:T(8,128)(2,1)S(1)}, u32[]{:S(2)}) copy-start(bf16[384,1728]{0,1:T(8,128)(2,1)S(1)} %get-tuple-element.50) | copy-start | bytes 3981316
  136.5 5.8 copy-start.27
  145.7 138.8 %reduce-scatter.14.cloned.1.call-start = ((), (), s32[]{:S(2)}) async-start(), calls=%async_computation.10 | async-start | bytes 1327104 | tf_op jit(solution)/shard_map/reduce_scatter | solution.py:177
  146.2 6.4 copy-start.41
  201.8 4.9 copy-start.29
  201.8 4.9 copy-start.30
  201.8 4.9 copy-start.74
  201.8 4.9 copy-start.76
  201.9 4.9 copy-start.92
  201.9 4.9 copy-start.95
  213.2 130.5 %reduce-scatter.10.cloned.1.call-start = ((), (), s32[]{:S(2)}) async-start(), calls=%async_computation.8 | async-start | bytes 1327104 | tf_op jit(solution)/shard_map/reduce_scatter | solution.py:175
  216.1 11.2 %copy-start.43 = (bf16[384,384]{1,0:T(8,128)(2,1)}, bf16[384,384]{1,0:T(8,128)(2,1)S(1)}, u32[]{:S(2)}) copy-start(bf16[384,384]{1,0:T(8,128)(2,1)S(1)} %get-tuple-element.72) | copy-start | bytes 884740
  216.2 5.9 copy-start.5
  216.2 5.8 copy-start.39
  216.2 5.8 copy-start.63
  217.8 12.8 %collective-permute-start.2 = (f32[3,2,384]{2,1,0:T(2,128)}, f32[3,2,384]{2,1,0:T(2,128)}, u32[]{:S(2)}, u32[]{:S(2)}) collective-permute-start(f32[3,2,384]{2,1,0:T(2,128)} %pad_add_fusion.3), channel_id=1, source_target_pairs={{4,0},{8,4},{12,8},{16,12},{20,16},{24,20},{28,24},{0,28},{5,1},{9... | collective-permute-start | bytes 27656 | tf_op jit(solution)/shard_map/ppermute | solution.py:16
  222.9 5.5 copy-start.45
  224.7 6.8 collective-permute-start.3
  230.6 209.2 %all-reduce.16.cloned.1.call-start = ((), (), s32[]{:S(2)}) async-start(), calls=%async_computation.14 | async-start | bytes 9437184 | tf_op jit(solution)/shard_map/psum | solution.py:98
  234.0 8.4 copy-start.47
  244.3 262.9 %reduce-scatter.12.cloned.1.call-start = ((), (), s32[]{:S(2)}) async-start(), calls=%async_computation.9 | async-start | bytes 1327104 | tf_op jit(solution)/shard_map/reduce_scatter | solution.py:176
  248.5 325.2 %reduce-scatter.8.cloned.1.call-start = ((), (), s32[]{:S(2)}) async-start(), calls=%async_computation.7 | async-start | bytes 1327104 | tf_op jit(solution)/shard_map/reduce_scatter | solution.py:174
  251.7 5.3 copy-start.93
  251.7 431.2 %reduce-scatter.20.cloned.1.call-start = ((), (), s32[]{:S(2)}) async-start(), calls=%async_computation.13 | async-start | bytes 6193152 | tf_op jit(solution)/shard_map/reduce_scatter | solution.py:180
  252.0 5.1 copy-start.22
  252.0 5.1 copy-start.42
  262.4 530.7 %reduce-scatter.18.cloned.1.call-start = ((), (), s32[]{:S(2)}) async-start(), calls=%async_computation.12 | async-start | bytes 6193152 | tf_op jit(solution)/shard_map/reduce_scatter | solution.py:179
  273.2 629.3 %reduce-scatter.16.cloned.1.call-start = ((), (), s32[]{:S(2)}) async-start(), calls=%async_computation.11 | async-start | bytes 6193152 | tf_op jit(solution)/shard_map/reduce_scatter | solution.py:178
  439.8 174.2 %copy-start.8 = (bf16[384,1536]{1,0:T(8,128)(2,1)S(1)}, bf16[384,1536]{1,0:T(8,128)(2,1)}, u32[]{:S(2)}) copy-start(bf16[384,1536]{1,0:T(8,128)(2,1)} %get-tuple-element.48) | copy-start | bytes 3538948
  682.9 221.9 %copy-start.1 = (bf16[384,1536]{1,0:T(8,128)(2,1)S(1)}, bf16[384,1536]{1,0:T(8,128)(2,1)}, u32[]{:S(2)}) copy-start(bf16[384,1536]{1,0:T(8,128)(2,1)} %param.21) | copy-start | bytes 3538948
  (80 other events, 184.0 us)
Sparse Core Ops, SparseCore 0:
  43.6 56.0 all-reduce.19
  145.8 55.9 all-reduce.17
  213.3 64.0 reduce-scatter.13
  280.7 62.9 reduce-scatter.9
  346.2 93.5 all-reduce.15
  443.0 64.2 reduce-scatter.11
  510.7 62.9 reduce-scatter.7
  577.2 105.6 reduce-scatter.19
  687.0 106.0 reduce-scatter.17
  796.5 106.0 reduce-scatter.15

commit v2 on v1

--- a/solution.py
+++ b/solution.py
@@ -1,13 +1,471 @@
+import functools
 import jax
 import jax.numpy as jnp
 from jax import lax
+from jax.experimental import pallas as pl
+from jax.experimental.pallas import tpu as pltpu
 from jax.sharding import PartitionSpec as P
 
 SPAN = 128
 MICRO = 2
-
-
 EPSILON = 1e-05
+MESH = pl.DeviceIdType.MESH
+TILE = 256
+f32 = jnp.float32
+bf16 = jnp.bfloat16
+
+
+def dot_nn(a, b):
+    return jnp.dot(a, b, preferred_element_type=f32)
+
+
+def dot_nt(a, b):
+    return lax.dot_general(a, b, (((1,), (1,)), ((), ())), preferred_element_type=f32)
+
+
+def dot_tn(a, b):
+    return lax.dot_general(a, b, (((0,), (0,)), ((), ())), preferred_element_type=f32)
+
+
+def send_to(src, dst, send_sem, recv_sem, device):
+    return pltpu.make_async_remote_copy(
+        src_ref=src,
+        dst_ref=dst,
+        send_sem=send_sem,
+        recv_sem=recv_sem,
+        device_id=device,
+        device_id_type=MESH,
+    )
+
+
+class Scatter:
+    def __init__(self, n_tiles, line, rows, ffn_tiles, refs):
+        self.n = n_tiles
+        self.line = line
+        self.rows = rows
+        self.ffn_tiles = ffn_tiles
+        (
+            self.sbuf,
+            self.obuf,
+            self.out,
+            self.stage,
+            self.yrecv,
+            self.zup,
+            self.zdn,
+            self.fetch,
+            self.final,
+            self.stage_sem,
+            self.ysend_sem,
+            self.yrecv_sem,
+            self.zsend_sem,
+            self.zup_sem,
+            self.zdn_sem,
+            self.fetch_sem,
+            self.final_sem,
+        ) = refs
+        self.slots = self.zup.shape[0]
+        s = lax.axis_index("seq")
+        self.t = lax.axis_index("tp")
+        self.a = lax.div(s, 2)
+        self.b = lax.rem(s, 2)
+        self.pair = (self.a * 2 + 1 - self.b, self.t)
+        self.up = (lax.rem(self.a + 1, line) * 2 + self.b, self.t)
+        self.down = (lax.rem(self.a + line - 1, line) * 2 + self.b, self.t)
+
+    @staticmethod
+    def scratch(n_tiles, line, rows):
+        slots = min(n_tiles, line + 2)
+        return [
+            pltpu.VMEM((2, 2, line, rows, TILE), bf16),
+            pltpu.VMEM((n_tiles, line, rows, TILE), bf16),
+            pltpu.VMEM((slots, line, rows, TILE), bf16),
+            pltpu.VMEM((slots, line, rows, TILE), bf16),
+            pltpu.VMEM((3, line, rows, TILE), bf16),
+            pltpu.VMEM((2, rows, TILE), f32),
+            pltpu.SemaphoreType.DMA((2, 2)),
+            pltpu.SemaphoreType.DMA((n_tiles,)),
+            pltpu.SemaphoreType.DMA((n_tiles,)),
+            pltpu.SemaphoreType.DMA((3, line)),
+            pltpu.SemaphoreType.DMA((slots, line)),
+            pltpu.SemaphoreType.DMA((slots, line)),
+            pltpu.SemaphoreType.DMA((3, line)),
+            pltpu.SemaphoreType.DMA((2,)),
+        ]
+
+    def local(self, k):
+        slot = lax.rem(k, 2)
+        return (
+            pltpu.make_async_copy(
+                self.stage.at[slot, 1 - self.b], self.sbuf.at[k], self.stage_sem.at[slot, 0]
+            ),
+            pltpu.make_async_copy(
+                self.stage.at[slot, self.b], self.obuf.at[k], self.stage_sem.at[slot, 1]
+            ),
+        )
+
+    def swap(self, k):
+        return send_to(
+            self.sbuf.at[k], self.yrecv.at[k], self.ysend_sem.at[k], self.yrecv_sem.at[k], self.pair
+        )
+
+    def flush(self, k):
+        for copy in self.local(k):
+            copy.wait()
+        self.swap(k).start()
+
+    def produce(self, k, parts):
+        @pl.when(k >= 1)
+        def _():
+            self.flush(k - 1)
+
+        slot = lax.rem(k, 2)
+        for offset, value in parts:
+            width = value.shape[1]
+            for c in range(self.line):
+                for half in range(2):
+                    row = (2 * c + half) * self.rows
+                    self.stage[slot, half, c, :, offset : offset + width] = value[
+                        row : row + self.rows
+                    ].astype(bf16)
+        for copy in self.local(k):
+            copy.start()
+
+    def lag(self, c):
+        return jnp.where(
+            c > self.a, self.a, jnp.where(c < self.a, self.line - 1 - self.a, self.line - 1)
+        )
+
+    def fetching(self, i, c):
+        slot = lax.rem(i, 3)
+        k = jnp.clip(i - self.lag(c), 0, self.n - 1)
+        return pltpu.make_async_copy(
+            self.obuf.at[k, c], self.fetch.at[slot, c], self.fetch_sem.at[slot, c]
+        )
+
+    def onward(self, i, c, upward):
+        slot = lax.rem(i, 3)
+        k = jnp.clip(i - self.lag(c), 0, self.n - 1)
+        zslot = lax.rem(k, self.slots)
+        inbox, sem, device = (
+            (self.zup, self.zup_sem, self.up) if upward else (self.zdn, self.zdn_sem, self.down)
+        )
+        return send_to(
+            self.fetch.at[slot, c],
+            inbox.at[zslot, c],
+            self.zsend_sem.at[slot, c],
+            sem.at[zslot, c],
+            device,
+        )
+
+    def valid(self, i, c):
+        k = i - self.lag(c)
+        return jnp.logical_and(k >= 0, k < self.n)
+
+    def prefetch(self, i):
+        @pl.loop(0, self.line)
+        def _(c):
+            @pl.when(self.valid(i, c))
+            def _():
+                self.fetching(i, c).start()
+
+    def drain(self, i):
+        @pl.loop(0, self.line)
+        def _(c):
+            @pl.when(jnp.logical_and(self.valid(i, c), c != self.a))
+            def _():
+                self.onward(i, c, True).wait_send()
+
+    def storing(self, k):
+        slot = lax.rem(k, 2)
+        ffn = k < self.ffn_tiles
+        kind = jnp.where(ffn, lax.rem(k, 3), 3)
+        column = jnp.where(ffn, lax.div(k, 3), k - self.ffn_tiles)
+        return pltpu.make_async_copy(
+            self.final.at[slot],
+            self.out.at[kind, :, pl.ds(pl.multiple_of(column * TILE, TILE), TILE)],
+            self.final_sem.at[slot],
+        )
+
+    def advance(self, i):
+        line, a = self.line, self.a
+
+        @pl.when(i >= 2)
+        def _():
+            self.drain(i - 2)
+
+        self.prefetch(i + 1)
+        first = i - jnp.minimum(a, line - 1 - a)
+
+        @pl.when(jnp.logical_and(first >= 0, first < self.n))
+        def _():
+            self.swap(first).wait_recv()
+
+        slot = lax.rem(i, 3)
+
+        @pl.loop(0, line)
+        def _(c):
+            @pl.when(self.valid(i, c))
+            def _():
+                k = i - self.lag(c)
+                zslot = lax.rem(k, self.slots)
+                below = jnp.logical_and(c >= a, a > 0)
+                above = jnp.logical_and(c <= a, a < line - 1)
+                self.fetching(i, c).wait()
+
+                @pl.when(below)
+                def _():
+                    send_to(
+                        self.fetch.at[slot, c],
+                        self.zup.at[zslot, c],
+                        self.zsend_sem.at[slot, c],
+                        self.zup_sem.at[zslot, c],
+                        self.down,
+                    ).wait_recv()
+
+                @pl.when(above)
+                def _():
+                    send_to(
+                        self.fetch.at[slot, c],
+                        self.zdn.at[zslot, c],
+                        self.zsend_sem.at[slot, c],
+                        self.zdn_sem.at[zslot, c],
+                        self.up,
+                    ).wait_recv()
+
+                def base():
+                    return self.fetch[slot, c].astype(f32) + self.yrecv[k, c].astype(f32)
+
+                @pl.when(c != a)
+                def _():
+                    @pl.when(jnp.logical_and(c > a, a > 0))
+                    def _():
+                        self.fetch[slot, c] = (base() + self.zup[zslot, c].astype(f32)).astype(bf16)
+
+                    @pl.when(jnp.logical_and(c < a, a < line - 1))
+                    def _():
+                        self.fetch[slot, c] = (base() + self.zdn[zslot, c].astype(f32)).astype(bf16)
+
+                    @pl.when(
+                        jnp.logical_or(
+                            jnp.logical_and(c > a, a == 0),
+                            jnp.logical_and(c < a, a == line - 1),
+                        )
+                    )
+                    def _():
+                        self.fetch[slot, c] = base().astype(bf16)
+
+                    @pl.when(c > a)
+                    def _():
+                        self.onward(i, c, True).start()
+
+                    @pl.when(c < a)
+                    def _():
+                        self.onward(i, c, False).start()
+
+                @pl.when(c == a)
+                def _():
+                    fslot = lax.rem(k, 2)
+
+                    @pl.when(k >= 2)
+                    def _():
+                        self.storing(k - 2).wait()
+
+                    @pl.when(jnp.logical_and(a > 0, a < line - 1))
+                    def _():
+                        self.final[fslot] = (
+                            base() + self.zup[zslot, c].astype(f32) + self.zdn[zslot, c].astype(f32)
+                        )
+
+                    @pl.when(a == 0)
+                    def _():
+                        self.final[fslot] = base() + self.zdn[zslot, c].astype(f32)
+
+                    @pl.when(a == line - 1)
+                    def _():
+                        self.final[fslot] = base() + self.zup[zslot, c].astype(f32)
+
+                    self.storing(k).start()
+
+    def finish(self):
+        steps = self.n + self.line - 1
+        self.drain(steps - 2)
+        self.drain(steps - 1)
+        self.storing(self.n - 2).wait()
+        self.storing(self.n - 1).wait()
+
+        @pl.loop(0, self.n)
+        def _(k):
+            self.swap(k).wait_send()
+
+
+def ffn_kernel(
+    line,
+    rows,
+    n_ffn,
+    n2,
+    g,
+    wg,
+    wu,
+    wd,
+    wg_rest,
+    wu_rest,
+    o_out,
+    d_out,
+    grads,
+    sbuf,
+    obuf,
+    oacc,
+    dacc,
+    wgb,
+    wub,
+    wdb,
+    gs,
+    us,
+    ds,
+    hb,
+    dgb,
+    dub,
+    wsem,
+    *rs_refs,
+):
+    units = wd.shape[0]
+    full = units // TILE
+    rest = units - full * TILE
+    rs = Scatter(3 * n_ffn, line, rows, 3 * n_ffn, (sbuf, obuf, grads) + rs_refs)
+
+    barrier = pltpu.get_barrier_semaphore()
+    for device in (rs.pair, rs.up, rs.down):
+        pl.semaphore_signal(barrier, inc=1, device_id=device, device_id_type=MESH)
+
+    def weights(j, slot):
+        cols = pl.ds(pl.multiple_of(j * TILE, TILE), TILE)
+        return (
+            pltpu.make_async_copy(wg.at[:, cols], wgb.at[slot], wsem.at[slot, 0]),
+            pltpu.make_async_copy(wu.at[:, cols], wub.at[slot], wsem.at[slot, 1]),
+            pltpu.make_async_copy(wd.at[cols, :], wdb.at[slot], wsem.at[slot, 2]),
+        )
+
+    def rest_weights(slot):
+        return (
+            pltpu.make_async_copy(wg_rest, wgb.at[slot], wsem.at[slot, 0]),
+            pltpu.make_async_copy(wu_rest, wub.at[slot], wsem.at[slot, 1]),
+            pltpu.make_async_copy(
+                wd.at[full * TILE :, :], wdb.at[slot, 0:rest, :], wsem.at[slot, 2]
+            ),
+        )
+
+    for copy in weights(0, 0):
+        copy.start()
+    oacc[...] = jnp.zeros_like(oacc)
+    dacc[...] = jnp.zeros_like(dacc)
+    pl.semaphore_wait(barrier, 3)
+
+    @pl.loop(0, n_ffn)
+    def _(j):
+        slot = lax.rem(j, 2)
+
+        @pl.when(j < full)
+        def _():
+            for copy in weights(j, slot):
+                copy.wait()
+
+        if rest:
+
+            @pl.when(j == full)
+            def _():
+                for copy in rest_weights(full % 2):
+                    copy.wait()
+
+        @pl.when(j + 1 < full)
+        def _():
+            for copy in weights(j + 1, 1 - slot):
+                copy.start()
+
+        if rest:
+
+            @pl.when(j + 1 == full)
+            def _():
+                wdb[full % 2, rest:, :] = jnp.zeros((TILE - rest, wdb.shape[2]), bf16)
+                for copy in rest_weights(full % 2):
+                    copy.start()
+
+        gs[...] = dot_nn(n2[...], wgb[slot])
+        us[...] = dot_nn(n2[...], wub[slot])
+        ds[...] = dot_nt(g[...], wdb[slot])
+
+        @pl.loop(0, gs.shape[0] // 64)
+        def _(r):
+            at = pl.ds(pl.multiple_of(r * 64, 64), 64)
+            gate, up, back = gs[at, :], us[at, :], ds[at, :]
+            sigma = jax.nn.sigmoid(gate)
+            silu = gate * sigma
+            hb[at, :] = (silu * up).astype(bf16)
+            dgb[at, :] = (back * up * sigma * (1.0 + gate * (1.0 - sigma))).astype(bf16)
+            dub[at, :] = (back * silu).astype(bf16)
+
+        rs.produce(3 * j, [(0, dot_tn(g[...], hb[...]))])
+        rs.produce(3 * j + 1, [(0, dot_tn(n2[...], dgb[...]))])
+        rs.produce(3 * j + 2, [(0, dot_tn(n2[...], dub[...]))])
+        oacc[...] += dot_nn(hb[...], wdb[slot])
+        dacc[...] += dot_nt(dgb[...], wgb[slot])
+        dacc[...] += dot_nt(dub[...], wub[slot])
+
+    rs.flush(rs.n - 1)
+    o_out[...] = oacc[...].astype(bf16)
+    d_out[...] = dacc[...].astype(bf16)
+    rs.prefetch(0)
+
+    @pl.loop(0, rs.n + line - 1)
+    def _(i):
+        rs.advance(i)
+
+    rs.finish()
+
+
+def ffn(n2, g, w_gate, w_up, w_down, seq_count):
+    tokens, width = n2.shape
+    units = w_gate.shape[1]
+    n_ffn = pl.cdiv(units, TILE)
+    full = units // TILE
+    line = seq_count // 2
+    rows = width // seq_count
+    n_tiles = 3 * n_ffn
+
+    def tail(w):
+        return jnp.pad(w[:, full * TILE :], ((0, 0), (0, n_ffn * TILE - units)))
+
+    vmem = pl.BlockSpec(memory_space=pltpu.VMEM)
+    hbm = pl.BlockSpec(memory_space=pl.ANY)
+    return pl.pallas_call(
+        functools.partial(ffn_kernel, line, rows, n_ffn),
+        out_shape=(
+            jax.ShapeDtypeStruct((tokens, width), bf16),
+            jax.ShapeDtypeStruct((tokens, width), bf16),
+            jax.ShapeDtypeStruct((4, rows, n_ffn * TILE), f32),
+            jax.ShapeDtypeStruct((n_tiles, line, rows, TILE), bf16),
+            jax.ShapeDtypeStruct((n_tiles, line, rows, TILE), bf16),
+        ),
+        in_specs=[vmem, vmem, hbm, hbm, hbm, hbm, hbm],
+        out_specs=(vmem, vmem, hbm, hbm, hbm),
+        scratch_shapes=[
+            pltpu.VMEM((tokens, width), f32),
+            pltpu.VMEM((tokens, width), f32),
+            pltpu.VMEM((2, width, TILE), bf16),
+            pltpu.VMEM((2, width, TILE), bf16),
+            pltpu.VMEM((2, TILE, width), bf16),
+            pltpu.VMEM((tokens, TILE), f32),
+            pltpu.VMEM((tokens, TILE), f32),
+            pltpu.VMEM((tokens, TILE), f32),
+            pltpu.VMEM((tokens, TILE), bf16),
+            pltpu.VMEM((tokens, TILE), bf16),
+            pltpu.VMEM((tokens, TILE), bf16),
+            pltpu.SemaphoreType.DMA((2, 3)),
+        ]
+        + Scatter.scratch(n_tiles, line, rows),
+        compiler_params=pltpu.CompilerParams(
+            collective_id=0, has_side_effects=True, vmem_limit_bytes=60 * 2**20
+        ),
+    )(n2, g, w_gate, w_up, w_down, tail(w_gate), tail(w_up))[:3]
 
 
 def passed_along(block, axis, distance):
@@ -33,8 +491,6 @@
     span_order,
     keep_mask,
 ):
-    f32 = jnp.float32
-    bf16 = jnp.bfloat16
     seq_count = lax.axis_size("seq")
     device = lax.axis_index("seq")
     tok_local = tokens.shape[1]
@@ -47,6 +503,7 @@
     pending = None
     sharded = None
     outputs = []
+    saved = []
     input_grads = []
     for batch_idx in range(MICRO):
         order = span_order[batch_idx]
@@ -89,24 +546,29 @@
         scale_two = lax.rsqrt(jnp.mean(middle * middle, axis=-1, keepdims=True) + EPSILON)
         normal_two = middle * scale_two
         second_rows = (normal_two * ffn_gain).astype(bf16)
-        gate_h = jnp.dot(second_rows, w_gate, preferred_element_type=f32)
-        up_h = jnp.dot(second_rows, w_up, preferred_element_type=f32)
-        sigma = jax.nn.sigmoid(gate_h)
-        silu_h = gate_h * sigma
-        hidden = (silu_h * up_h).astype(bf16)
-        feed_terms = jnp.dot(hidden, w_down, preferred_element_type=f32)
-        outputs.append((middle + lax.psum(feed_terms.astype(bf16), "tp").astype(f32)).astype(bf16))
         grad_out = cotangent[batch_idx] * keep_mask[batch_idx].astype(bf16)[:, None]
-        grad_down = jnp.einsum("tf,td->fd", hidden, grad_out, preferred_element_type=f32)
-        grad_hidden = jnp.einsum("td,fd->tf", grad_out, w_down, preferred_element_type=f32)
-        grad_gate = (grad_hidden * up_h * sigma * (1.0 + gate_h * (1.0 - sigma))).astype(bf16)
-        grad_up = (grad_hidden * silu_h).astype(bf16)
-        grad_wgate = jnp.einsum("td,tf->df", second_rows, grad_gate, preferred_element_type=f32)
-        grad_wup = jnp.einsum("td,tf->df", second_rows, grad_up, preferred_element_type=f32)
-        partial_second = jnp.einsum(
-            "tf,df->td", grad_gate, w_gate, preferred_element_type=f32
-        ) + jnp.einsum("tf,df->td", grad_up, w_up, preferred_element_type=f32)
-        grad_second = lax.psum(partial_second.astype(bf16), "tp").astype(f32)
+        saved.append(
+            (
+                inputs, scale_one, normal_one, normed, gate_b, gate_c, values, valid_far, valid_near,
+                far_term, near_term, here_term, convolved, mixed, middle, scale_two, normal_two,
+                second_rows, grad_out, order, mine,
+            )
+        )
+    second_all = jnp.concatenate([one[17] for one in saved])
+    grad_all = jnp.concatenate([one[18] for one in saved])
+    feed_all, partial_all, ffn_grads = ffn(second_all, grad_all, w_gate, w_up, w_down, seq_count)
+    feed_all = lax.psum(feed_all, "tp").astype(f32)
+    partial_all = lax.psum(partial_all, "tp").astype(f32)
+    units = w_gate.shape[1]
+    for batch_idx in range(MICRO):
+        (
+            inputs, scale_one, normal_one, normed, gate_b, gate_c, values, valid_far, valid_near,
+            far_term, near_term, here_term, convolved, mixed, middle, scale_two, normal_two,
+            second_rows, grad_out, order, mine,
+        ) = saved[batch_idx]
+        part = slice(batch_idx * tok_local, (batch_idx + 1) * tok_local)
+        outputs.append((middle + feed_all[part]).astype(bf16))
+        grad_second = partial_all[part]
         out_rows = grad_out.astype(f32)
         gain_two = gain_two + jnp.sum(grad_second * normal_two, axis=0)
         weighted_two = grad_second * ffn_gain
@@ -164,7 +626,7 @@
         )
         input_rows = grad_input.astype(bf16)
         input_grads.append(input_rows)
-        local_grads = (grad_wb, grad_wc, grad_wx, grad_wout, grad_wgate, grad_wup, grad_down)
+        local_grads = (grad_wb, grad_wc, grad_wx, grad_wout)
         pending = (
             local_grads
             if pending is None
@@ -175,9 +637,6 @@
         lax.psum_scatter(pending[1].astype(bf16), "seq", scatter_dimension=0, tiled=True).astype(f32),
         lax.psum_scatter(pending[2].astype(bf16), "seq", scatter_dimension=0, tiled=True).astype(f32),
         lax.psum_scatter(pending[3].astype(bf16), "seq", scatter_dimension=1, tiled=True).astype(f32),
-        lax.psum_scatter(pending[4].astype(bf16), "seq", scatter_dimension=0, tiled=True).astype(f32),
-        lax.psum_scatter(pending[5].astype(bf16), "seq", scatter_dimension=0, tiled=True).astype(f32),
-        lax.psum_scatter(pending[6].astype(bf16), "seq", scatter_dimension=1, tiled=True).astype(f32),
     )
     small = lax.psum((gain_one, gain_two, taps_grad), "seq")
     return (
@@ -190,9 +649,9 @@
         small[2],
         sharded[3],
         small[1],
-        sharded[4],
-        sharded[5],
-        sharded[6],
+        ffn_grads[1, :, :units],
+        ffn_grads[2, :, :units],
+        ffn_grads[0, :, :units].T,
     )
 
 

time: 918 us -> 779 us (0.85)
  waiting for transfers between devices: 654 us -> 347 us
  Pallas kernels: 0 us -> 229 us
  matrix products: 123 us -> 39.5 us
  local copies, waits for them, and re-layouts: 12.6 us -> 37.4 us
    reduce_scatter x3 -> x0, waiting for transfers between devices: 275 us -> none  [the longest x1 108 us: body(): lax.psum_scatter(pending[5].astype(bf16), 'seq', scatter_dimension=0, til...]
    pallas_call x0 -> x1, Pallas kernels: none -> 229 us  [ffn(): pl.pallas_call(functools.partial(ffn_kernel, line, rows, n_ffn), out_shap...]
    dot_general x18 -> x0, matrix products: 83.8 us -> none  [the longest x2 12.2 us: body(): feed_terms = jnp.dot(hidden, w_down, preferred_element_type=f32)]
    reduce_scatter x1, waiting for transfers between devices: 64.7 us -> 18.5 us  [body(): lax.psum_scatter(pending[0].astype(bf16), 'seq', scatter_dimension=0, til...]
    psum x1, waiting for transfers between devices: 55.4 us -> 31.1 us  [body(): middle = inputs + lax.psum(branch_terms.astype(bf16), 'tp').astype(f32)]
    reduce_scatter x1, waiting for transfers between devices: 0.01 us -> 20.7 us  [body(): lax.psum_scatter(pending[3].astype(bf16), 'seq', scatter_dimension=1, til...]
    unnamed x228 -> x186, local copies, waits for them, and re-layouts: 8.6 us -> 24.4 us
    psum x2, waiting for transfers between devices: 138 us -> 151 us  [the longest x1 94 us: body(): feed_all = lax.psum(feed_all, 'tp').astype(f32)]
  transfers between devices with their start and end apart: 14 -> 11, of which waited for: 9 -> 7; matrix products, arithmetic and copies ran while one was open for 12% -> 12% of each run, Pallas kernels for 0% -> 0%
where the time goes in v2:
time: 779 us; the launch traced here: 772 us
  waiting for transfers between devices  347 us (45%)
  Pallas kernels  229 us (29%)
  other arithmetic  57.9 us (7%)
  matrix products  39.5 us (5%)
  local copies, waits for them, and re-layouts  37.4 us (5%)
  blocking collectives  35.9 us (5%)
  between operations  15.8 us (2%)
  starting transfers between devices  10.2 us (1%)
    pallas_call x1, Pallas kernels, ffn(): pl.pallas_call(functools.partial(ffn_kernel, line, rows, n_ffn), out_shap...  229 us
    psum x1, waiting for transfers between devices, body(): feed_all = lax.psum(feed_all, 'tp').astype(f32)  94 us
    reduce_scatter x1, waiting for transfers between devices, body(): lax.psum_scatter(pending[1].astype(bf16), 'seq', scatter_dimension=0, til...  64.7 us
    reduce_scatter x1, waiting for transfers between devices, body(): lax.psum_scatter(pending[2].astype(bf16), 'seq', scatter_dimension=0, til...  60.2 us
    psum x1, waiting for transfers between devices, body(): partial_all = lax.psum(partial_all, 'tp').astype(f32)  57.4 us
    psum x1, blocking collectives, body(): small = lax.psum((gain_one, gain_two, taps_grad), 'seq')  35.9 us
    psum x1, waiting for transfers between devices, body(): middle = inputs + lax.psum(branch_terms.astype(bf16), 'tp').astype(f32)  31.1 us
    unnamed x186, local copies, waits for them, and re-layouts  24.4 us
  transfers between devices with their start and end apart: 11, of which 7 were waited for; matrix products, arithmetic and copies ran while one was open for 12% of the time, Pallas kernels for 0%

profile of v2, /device:TPU:0, one launch (start us, length us, event | category | flops | bytes accessed | tf_op | source)
XLA Modules:
  0.0 772.0 jit_solution(12126895544523434522)
XLA Ops:
  7.3 2.3 fusion.25
  9.7 2.2 fusion.96
  11.9 1.6 multiply_convert_fusion.3
  14.2 3.0 collective-permute-start
  18.0 1.7 multiply_convert_fusion.2
  21.0 1.5 collective-permute-start.1
  35.8 1.6 fusion.44
  37.5 1.6 fusion.42
  39.8 1.8 convolution_convert_fusion
  41.6 1.8 convolution_convert_fusion.1
  43.7 8.1 %copy.87.wg = bf16[1536,1728]{1,0:T(8,128)(2,1)} copy(bf16[1536,1728]{0,1:T(8,128)(2,1)} %param.23) | data formatting | bytes 10616832 | tf_op args[8]
  51.7 2.1 slice.160
  53.8 8.2 %copy.88.wu = bf16[1536,1728]{1,0:T(8,128)(2,1)} copy(bf16[1536,1728]{0,1:T(8,128)(2,1)} %param.24) | data formatting | bytes 10616832 | tf_op args[9]
  62.0 2.3 pad.35.wg_rest
  67.0 1.6 pad_maximum_fusion.1.g
  68.5 31.1 %all-reduce.21.cloned.1.call-done = (bf16[384,1536]{1,0:T(8,128)(2,1)}, bf16[384,1536]{1,0:T(8,128)(2,1)}) async-done(((bf16[384,1536]{1,0:T(8,128)(2,1)}, bf16[384,1536]{1,0:T(8,128)(2,1)}), (bf16[384,1536]{1,0:T(8,128)(2,1)}, bf16[384,1536]{1,0:T(8,128)(2,1)})) %all-reduce.21.cloned.1.call-update) | async-done | bytes 2359312 | tf_op jit(solution)/shard_map/psum | solution.py:545
  99.7 2.6 multiply_reduce_fusion.5
  103.2 1.6 pad_maximum_fusion.n2
  104.8 228.5 %shard_map.238 = (bf16[768,1536]{1,0:T(8,128)(2,1)}, bf16[768,1536]{1,0:T(8,128)(2,1)}, f32[4,192,1792]{2,1,0:T(8,128)}, bf16[21,4,192,256]{3,2,1,0:T(8,128)(2,1)}, bf16[21,4,192,256]{3,2,1,0:T(8,128)(2,1)}) custom-call(bf16[768,1536]{1,0:T(8,128)(2,1)} %pad_maximum_fusion.n2, bf16[768,1536]{1,0:T(8,128)(2,1)} %pad_maximum_fusion.1.g, ...), custom_call_target="tpu_custom_call" | custom-call | tf_op jit(solution)/shard_map/pallas_call | solution.py:439
  333.6 57.4 %all-reduce.17.cloned.1.call-done = bf16[768,1536]{1,0:T(8,128)(2,1)} async-done(((bf16[768,1536]{1,0:T(8,128)(2,1)}), bf16[768,1536]{1,0:T(8,128)(2,1)}) %all-reduce.17.cloned.1.call-update) | async-done | bytes 2359312 | tf_op jit(solution)/shard_map/psum | solution.py:561
  391.0 2.4 convert_element_type.241
  393.5 3.3 multiply_reduce_fusion.1
  396.8 1.8 multiply_add_fusion.1
  400.8 2.0 fusion.15
  402.9 2.8 fusion.45
  407.4 4.2 collective-permute-start.2
  417.9 2.1 fusion.13
  422.3 1.4 fusion.41
  429.4 1.9 fusion.11
  432.1 1.8 fusion.10
  436.0 2.1 fusion.14
  438.2 4.3 slice_bitcast_fusion
  444.3 2.1 fusion.12
  446.4 20.7 %reduce-scatter.11.cloned.1.call-done = bf16[384,192]{0,1:T(8,128)(2,1)} async-done(((bf16[384,1536]{0,1:T(8,128)(2,1)}), bf16[384,192]{0,1:T(8,128)(2,1)}) %reduce-scatter.11.cloned.1.call-update) | async-done | bytes 147472 | tf_op jit(solution)/shard_map/reduce_scatter | solution.py:639
  467.1 1.6 convert_element_type.264
  468.8 64.7 %reduce-scatter.7.cloned.1.call-done = bf16[192,384]{1,0:T(8,128)(2,1)} async-done(((bf16[1536,384]{1,0:T(8,128)(2,1)}), bf16[192,384]{1,0:T(8,128)(2,1)}) %reduce-scatter.7.cloned.1.call-update) | async-done | bytes 147472 | tf_op jit(solution)/shard_map/reduce_scatter | solution.py:637
  533.5 1.6 convert_element_type.260
  535.1 94.0 %all-reduce.19.cloned.1.call-done = (bf16[768,1536]{1,0:T(8,128)(2,1)}, bf16[384,1536]{1,0:T(8,128)(2,1)}, bf16[384,1536]{1,0:T(8,128)(2,1)}) async-done(((bf16[768,1536]{1,0:T(8,128)(2,1)}, bf16[384,1536]{1,0:T(8,128)(2,1)}, bf16[384,1536]{1,0:T(8,128)(2,1)}), (bf16[768,1536]{1,0:T(8,128)(2,1)}, bf16[384,1536]{1,0:T(8,128)(2,1)}, bf16[384,1536]{1,0:T(8,128)(2,1)})) %all-reduce.19.cloned.1.call-update) | async-done | bytes 4718608 | tf_op jit(solution)/shard_map/psum | solution.py:560
  629.2 3.8 fusion.24
  633.0 2.8 convert_element_type.237
  636.4 60.2 %reduce-scatter.9.cloned.1.call-done = bf16[192,384]{1,0:T(8,128)(2,1)} async-done(((bf16[1536,384]{1,0:T(8,128)(2,1)}), bf16[192,384]{1,0:T(8,128)(2,1)}) %reduce-scatter.9.cloned.1.call-update) | async-done | bytes 147472 | tf_op jit(solution)/shard_map/reduce_scatter | solution.py:638
  696.6 1.6 convert_element_type.262
  698.2 35.9 %all-reduce.10 = (f32[1536]{0:T(1024)}, f32[3,384]{1,0:T(4,128)}, f32[1536]{0:T(1024)}) all-reduce(f32[1536]{0:T(1024)} %add.311, f32[3,384]{1,0:T(4,128)} %maximum_add_fusion, f32[1536]{0:T(1024)S(1)} %add.317), channel_id=1, replica_groups=mesh['seq'=8,'tp'=4] {'seq'}, use_global_device_ids=true, to_apply=%region_20.21 | all-reduce | flops 4224 | bytes 33792 | tf_op jit(solution)/shard_map/psum | solution.py:641
  735.5 5.9 fusion.36
  741.4 1.6 pad_maximum_fusion.3
  743.0 1.6 pad_maximum_fusion.2
  744.6 18.5 %reduce-scatter.5.cloned.1.call-done = bf16[192,384]{1,0:T(8,128)(2,1)} async-done(((bf16[1536,384]{1,0:T(8,128)(2,1)}), bf16[192,384]{1,0:T(8,128)(2,1)}) %reduce-scatter.5.cloned.1.call-update) | async-done | bytes 147472 | tf_op jit(solution)/shard_map/reduce_scatter | solution.py:636
  763.1 1.6 convert_element_type.258
  (272 shorter events, 45.1 us)
Async XLA Ops:
  7.2 32.6 %copy-start = (bf16[384,1536]{1,0:T(8,128)(2,1)S(1)}, bf16[384,1536]{1,0:T(8,128)(2,1)}, u32[]{:S(2)}) copy-start(bf16[384,1536]{1,0:T(8,128)(2,1)} %param.21) | copy-start | bytes 3538948
  7.2 92.4 %all-reduce.21.cloned.1.call-start = ((), (), s32[]{:S(2)}) async-start(), calls=%async_computation.10 | async-start | bytes 4718592 | tf_op jit(solution)/shard_map/psum | solution.py:545
  9.6 3.9 copy-start.77
  9.6 8.4 %copy-start.73 = (f32[384]{0:T(512)}, f32[384]{0:T(512)S(1)}, u32[]{:S(2)}) copy-start(f32[384]{0:T(512)S(1)} %get-tuple-element.114) | copy-start | bytes 4612
  11.9 5.3 copy-start.19
  13.5 6.1 copy-start.53
  14.2 16.2 %collective-permute-start = (bf16[3,2,384]{2,1,0:T(2,128)(2,1)}, bf16[3,2,384]{2,1,0:T(2,128)(2,1)}, u32[]{:S(2)}, u32[]{:S(2)}) collective-permute-start(bf16[3,2,384]{2,1,0:T(2,128)(2,1)} %slice.148), channel_id=1, source_target_pairs={{28,0},{0,4},{4,8},{8,12},{12,16},{16,20},{20,24},{24,28},{29,1},{... | collective-permute-start | bytes 13832 | tf_op jit(solution)/shard_map/ppermute | solution.py:474
  21.0 11.3 %collective-permute-start.1 = (bf16[3,2,384]{2,1,0:T(2,128)(2,1)}, bf16[3,2,384]{2,1,0:T(2,128)(2,1)}, u32[]{:S(2)}, u32[]{:S(2)}) collective-permute-start(bf16[3,2,384]{2,1,0:T(2,128)(2,1)} %slice.154), channel_id=1, source_target_pairs={{28,0},{0,4},{4,8},{8,12},{12,16},{16,20},{20,24},{24,28},{29,1},{... | collective-permute-start | bytes 13832 | tf_op jit(solution)/shard_map/ppermute | solution.py:474
  29.6 5.2 copy-start.65
  29.6 5.3 copy-start.67
  29.6 5.2 copy-start.69
  29.6 5.2 copy-start.71
  30.4 4.5 copy-start.55
  37.5 4.1 copy-start.39
  43.4 347.5 %all-reduce.17.cloned.1.call-start = ((), (), s32[]{:S(2)}) async-start(), calls=%async_computation.4 | async-start | bytes 4718592 | tf_op jit(solution)/shard_map/psum | solution.py:561
  62.0 3.4 copy-start.30
  333.3 133.8 %reduce-scatter.11.cloned.1.call-start = ((), (), s32[]{:S(2)}) async-start(), calls=%async_computation.8 | async-start | bytes 1327104 | tf_op jit(solution)/shard_map/reduce_scatter | solution.py:639
  393.4 3.3 copy-start.16
  393.5 3.3 copy-start.18
  402.9 130.6 %reduce-scatter.7.cloned.1.call-start = ((), (), s32[]{:S(2)}) async-start(), calls=%async_computation.6 | async-start | bytes 1327104 | tf_op jit(solution)/shard_map/reduce_scatter | solution.py:637
  405.8 11.0 %copy-start.31 = (bf16[384,384]{1,0:T(8,128)(2,1)}, bf16[384,384]{1,0:T(8,128)(2,1)S(1)}, u32[]{:S(2)}) copy-start(bf16[384,384]{1,0:T(8,128)(2,1)S(1)} %get-tuple-element.76) | copy-start | bytes 884740
  405.8 5.9 copy-start.5
  405.8 5.8 copy-start.28
  405.8 5.8 copy-start.51
  407.4 12.9 %collective-permute-start.2 = (f32[3,2,384]{2,1,0:T(2,128)}, f32[3,2,384]{2,1,0:T(2,128)}, u32[]{:S(2)}, u32[]{:S(2)}) collective-permute-start(f32[3,2,384]{2,1,0:T(2,128)} %pad_add_fusion.3), channel_id=1, source_target_pairs={{4,0},{8,4},{12,8},{16,12},{20,16},{24,20},{28,24},{0,28},{5,1},{9... | collective-permute-start | bytes 27656 | tf_op jit(solution)/shard_map/ppermute | solution.py:474
  412.5 5.3 copy-start.33
  414.3 6.9 collective-permute-start.3
  417.9 3.4 copy-start.88
  417.9 3.4 copy-start.89
  417.9 4.3 copy-start.25
  420.0 209.2 %all-reduce.19.cloned.1.call-start = ((), (), s32[]{:S(2)}) async-start(), calls=%async_computation.9 | async-start | bytes 9437184 | tf_op jit(solution)/shard_map/psum | solution.py:560
  423.7 8.4 %copy-start.35 = (bf16[384,384]{1,0:T(8,128)(2,1)}, bf16[384,384]{1,0:T(8,128)(2,1)S(1)}, u32[]{:S(2)}) copy-start(bf16[384,384]{1,0:T(8,128)(2,1)S(1)} %get-tuple-element.74) | copy-start | bytes 884740
  425.3 3.7 copy-start.37
  434.0 262.6 %reduce-scatter.9.cloned.1.call-start = ((), (), s32[]{:S(2)}) async-start(), calls=%async_computation.7 | async-start | bytes 1327104 | tf_op jit(solution)/shard_map/reduce_scatter | solution.py:638
  438.1 325.0 %reduce-scatter.5.cloned.1.call-start = ((), (), s32[]{:S(2)}) async-start(), calls=%async_computation.5 | async-start | bytes 1327104 | tf_op jit(solution)/shard_map/reduce_scatter | solution.py:636
  438.1 4.4 copy-start.83
  438.1 4.4 copy-start.82
  438.1 4.4 copy-start.81
  438.1 4.5 copy-start.86
  438.1 4.5 copy-start.85
  438.2 4.5 copy-start.84
  438.2 4.5 copy-start.59
  438.2 4.5 copy-start.60
  438.2 5.1 copy-start.44
  438.2 5.1 copy-start.80
  629.2 3.8 copy-start.26
  633.0 102.5 %copy-start.8 = (bf16[384,1536]{1,0:T(8,128)(2,1)S(1)}, bf16[384,1536]{1,0:T(8,128)(2,1)}, u32[]{:S(2)}) copy-start(bf16[384,1536]{1,0:T(8,128)(2,1)} %get-tuple-element.51) | copy-start | bytes 3538948
  743.0 21.7 %copy-start.1 = (bf16[384,1536]{1,0:T(8,128)(2,1)S(1)}, bf16[384,1536]{1,0:T(8,128)(2,1)}, u32[]{:S(2)}) copy-start(bf16[384,1536]{1,0:T(8,128)(2,1)} %param.21) | copy-start | bytes 3538948
  (56 other events, 110.3 us)
Sparse Core Ops, SparseCore 0:
  43.5 56.0 all-reduce.20
  333.4 57.4 all-reduce.16
  403.0 64.1 reduce-scatter.10
  470.4 63.0 reduce-scatter.6
  535.8 93.3 all-reduce.18
  632.4 64.1 reduce-scatter.8
  700.0 63.0 reduce-scatter.4

commit v3 on v1

v3 whole, which is shorter than its diff:
```python
import functools
import jax
import jax.numpy as jnp
from jax import lax
from jax.experimental import pallas as pl
from jax.experimental.pallas import tpu as pltpu
from jax.sharding import PartitionSpec as P

SPAN = 128
MICRO = 2
EPSILON = 1e-05
MESH = pl.DeviceIdType.MESH
TILE = 256
BLOCK = 32
f32 = jnp.float32
bf16 = jnp.bfloat16


def dot_nn(a, b):
    return jnp.dot(a, b, preferred_element_type=f32)


def dot_nt(a, b):
    return lax.dot_general(a, b, (((1,), (1,)), ((), ())), preferred_element_type=f32)


def dot_tn(a, b):
    return lax.dot_general(a, b, (((0,), (0,)), ((), ())), preferred_element_type=f32)


def send_to(src, dst, send_sem, recv_sem, device):
    return pltpu.make_async_remote_copy(
        src_ref=src,
        dst_ref=dst,
        send_sem=send_sem,
        recv_sem=recv_sem,
        device_id=device,
        device_id_type=MESH,
    )


def rows_at(start, size):
    return pl.ds(pl.multiple_of(start, 16), size)


class Place:
    def __init__(self, line):
        self.line = line
        self.s = lax.axis_index("seq")
        self.t = lax.axis_index("tp")
        self.a = lax.div(self.s, 2)
        self.b = lax.rem(self.s, 2)
        self.h = lax.rem(self.t, 2)
        count = 2 * line
        self.pair = (self.a * 2 + 1 - self.b, self.t)
        self.up = (lax.rem(self.a + 1, line) * 2 + self.b, self.t)
        self.down = (lax.rem(self.a + line - 1, line) * 2 + self.b, self.t)
        self.after = lax.rem(self.s + 1, count)
        self.before = lax.rem(self.s + count - 1, count)
        self.next = (self.after, self.t)
        self.last = (self.before, self.t)
        self.core = (self.s, self.t + 1 - 2 * self.h)
        self.across = (self.s, lax.rem(self.t + 2, 4))


class Scatter:
    NAMES = (
        "stage", "zin", "fetch", "yfetch", "final", "stage_sem", "ysend_sem", "yrecv_sem", "zsend_sem", "zin_sem",
        "fetch_sem", "yfetch_sem", "final_sem",
    )

    def __init__(self, place, n_tiles, ffn_tiles, rows, sbuf, obuf, ybuf, out, scratch):
        self.place, self.a, self.b, self.line = place, place.a, place.b, place.line
        self.n, self.ffn_tiles, self.rows = n_tiles, ffn_tiles, rows
        self.sbuf, self.obuf, self.ybuf, self.out = sbuf, obuf, ybuf, out
        for name, ref in zip(self.NAMES, scratch):
            setattr(self, name, ref)
        self.slots = self.zin.shape[0]

    @staticmethod
    def scratch(n_tiles, line, rows):
        slots = min(n_tiles, line + 1)
        dma = pltpu.SemaphoreType.DMA
        return [
            pltpu.VMEM((2, 2, line, rows, TILE), bf16),
            pltpu.VMEM((slots, line + 1, rows, TILE), bf16),
            pltpu.VMEM((2, line, rows, TILE), bf16),
            pltpu.VMEM((2, line, rows, TILE), bf16),
            pltpu.VMEM((2, rows, TILE), f32),
            dma((2, 2)),
            dma((n_tiles,)),
            dma((n_tiles,)),
            dma((2, line)),
            dma((slots, line + 1)),
            dma((2, line)),
            dma((2, line)),
            dma((2,)),
        ]

    def local(self, k):
        slot = lax.rem(k, 2)
        return (
            pltpu.make_async_copy(self.stage.at[slot, 1 - self.b], self.sbuf.at[k], self.stage_sem.at[slot, 0]),
            pltpu.make_async_copy(self.stage.at[slot, self.b], self.obuf.at[k], self.stage_sem.at[slot, 1]),
        )

    def swap(self, k):
        return send_to(
            self.sbuf.at[k], self.ybuf.at[k], self.ysend_sem.at[k], self.yrecv_sem.at[k], self.place.pair
        )

    def flush(self, k):
        for copy in self.local(k):
            copy.wait()
        self.swap(k).start()

    def produce(self, k, parts):
        @pl.when(jnp.logical_and(k != 0, k != self.ffn_tiles))
        def _():
            self.flush(k - 1)

        slot = lax.rem(k, 2)
        for offset, value in parts:
            width = value.shape[1]
            for c in range(self.line):
                for half in range(2):
                    row = (2 * c + half) * self.rows
                    self.stage[slot, half, c, :, offset : offset + width] = value[row : row + self.rows].astype(bf16)
        for copy in self.local(k):
            copy.start()

    def tile_of(self, i, c):
        lag = jnp.where(c > self.a, self.a, jnp.where(c < self.a, self.line - 1 - self.a, jnp.maximum(self.a, self.line - 1 - self.a)))
        return i - lag

    def valid(self, i, c):
        k = self.tile_of(i, c)
        return jnp.logical_and(k >= 0, k < self.n)

    def fetching(self, i, c):
        slot = lax.rem(i, 2)
        k = jnp.clip(self.tile_of(i, c), 0, self.n - 1)
        return (
            pltpu.make_async_copy(self.obuf.at[k, c], self.fetch.at[slot, c], self.fetch_sem.at[slot, c]),
            pltpu.make_async_copy(self.ybuf.at[k, c], self.yfetch.at[slot, c], self.yfetch_sem.at[slot, c]),
        )

    def onward(self, i, c, upward):
        slot = lax.rem(i, 2)
        k = jnp.clip(self.tile_of(i, c), 0, self.n - 1)
        at = lax.rem(k, self.slots)
        place = c + 1 if upward else c
        return send_to(
            self.fetch.at[slot, c],
            self.zin.at[at, place],
            self.zsend_sem.at[slot, c],
            self.zin_sem.at[at, place],
            self.place.up if upward else self.place.down,
        )

    def drain(self, i):
        @pl.loop(0, self.line)
        def _(c):
            @pl.when(jnp.logical_and(self.valid(i, c), c != self.a))
            def _():
                self.onward(i, c, False).wait_send()

    def storing(self, k):
        slot = lax.rem(k, 2)
        is_ffn = k < self.ffn_tiles
        kind = jnp.where(is_ffn, lax.rem(k, 3), 3)
        column = jnp.where(is_ffn, lax.div(k, 3), k - self.ffn_tiles)
        return pltpu.make_async_copy(
            self.final.at[slot],
            self.out.at[kind, :, pl.ds(pl.multiple_of(column * TILE, TILE), TILE)],
            self.final_sem.at[slot],
        )

    def advance(self, i):
        line, a = self.line, self.a

        @pl.when(i >= 2)
        def _():
            self.drain(i - 2)

        first = i - jnp.minimum(a, line - 1 - a)

        @pl.when(jnp.logical_and(first >= 0, first < self.n))
        def _():
            self.swap(first).wait_recv()

        @pl.loop(0, line)
        def _(c):
            @pl.when(self.valid(i, c))
            def _():
                for copy in self.fetching(i, c):
                    copy.start()

        slot = lax.rem(i, 2)

        @pl.loop(0, line)
        def _(c):
            @pl.when(self.valid(i, c))
            def _():
                k = self.tile_of(i, c)
                at = lax.rem(k, self.slots)

                def arrival(where, device):
                    send_to(
                        self.fetch.at[slot, c],
                        self.zin.at[at, where],
                        self.zsend_sem.at[slot, c],
                        self.zin_sem.at[at, where],
                        device,
                    ).wait_recv()

                for copy in self.fetching(i, c):
                    copy.wait()

                @pl.when(jnp.logical_and(c >= a, a > 0))
                def _():
                    arrival(c + 1, self.place.down)

                @pl.when(jnp.logical_and(c <= a, a < line - 1))
                def _():
                    arrival(c, self.place.up)

                def base():
                    return self.fetch[slot, c].astype(f32) + self.yfetch[slot, c].astype(f32)

                @pl.when(c != a)
                def _():
                    @pl.when(jnp.logical_and(c > a, a > 0))
                    def _():
                        self.fetch[slot, c] = (base() + self.zin[at, c + 1].astype(f32)).astype(bf16)

                    @pl.when(jnp.logical_and(c < a, a < line - 1))
                    def _():
                        self.fetch[slot, c] = (base() + self.zin[at, c].astype(f32)).astype(bf16)

                    @pl.when(
                        jnp.logical_or(jnp.logical_and(c > a, a == 0), jnp.logical_and(c < a, a == line - 1))
                    )
                    def _():
                        self.fetch[slot, c] = base().astype(bf16)

                    @pl.when(c > a)
                    def _():
                        self.onward(i, c, True).start()

                    @pl.when(c < a)
                    def _():
                        self.onward(i, c, False).start()

                @pl.when(c == a)
                def _():
                    fslot = lax.rem(k, 2)

                    @pl.when(k >= 2)
                    def _():
                        self.storing(k - 2).wait()

                    @pl.when(jnp.logical_and(a > 0, a < line - 1))
                    def _():
                        self.final[fslot] = base() + self.zin[at, c].astype(f32) + self.zin[at, c + 1].astype(f32)

                    @pl.when(a == 0)
                    def _():
                        self.final[fslot] = base() + self.zin[at, c].astype(f32)

                    @pl.when(a == line - 1)
                    def _():
                        self.final[fslot] = base() + self.zin[at, c + 1].astype(f32)

                    self.storing(k).start()

    def pump(self, low, high):
        @pl.loop(low, high)
        def _(i):
            self.advance(i)

    def finish(self):
        steps = self.n + self.line - 1
        self.drain(steps - 2)
        self.drain(steps - 1)
        self.storing(self.n - 2).wait()
        self.storing(self.n - 1).wait()

        @pl.loop(0, self.n)
        def _(k):
            self.swap(k).wait_send()


class Sum:
    def __init__(self, place, which, term, inbox, across, sems):
        self.place, self.which, self.term, self.inbox, self.across, self.sems = place, which, term, inbox, across, sems
        self.half = inbox.shape[1]

    def own(self, m):
        return rows_at((2 * m + self.place.h) * self.half, self.half)

    def other(self, m):
        return rows_at((2 * m + 1 - self.place.h) * self.half, self.half)

    def first(self, m):
        return send_to(
            self.term.at[self.other(m)], self.inbox.at[m], self.sems.at[self.which, m, 0], self.sems.at[self.which, m, 1],
            self.place.core,
        )

    def second(self, m):
        return send_to(
            self.term.at[self.own(m)], self.across.at[m], self.sems.at[self.which, m, 2], self.sems.at[self.which, m, 3],
            self.place.across,
        )

    def start(self, m):
        self.first(m).start()

    def relay(self, m):
        self.first(m).wait_recv()
        base = (2 * m + self.place.h) * self.half

        @pl.loop(0, self.half // BLOCK)
        def _(r):
            at = rows_at(base + r * BLOCK, BLOCK)
            took = self.inbox[m, rows_at(r * BLOCK, BLOCK), :].astype(f32)
            self.term[at, :] = (self.term[at, :].astype(f32) + took).astype(bf16)

        self.second(m).start()

    def ready(self, m):
        self.second(m).wait_recv()

    def total(self, m, r):
        at = rows_at((2 * m + self.place.h) * self.half + r * BLOCK, BLOCK)
        return self.term[at, :].astype(f32) + self.across[m, rows_at(r * BLOCK, BLOCK), :].astype(f32)

    def settle(self, m):
        self.first(m).wait_send()
        self.second(m).wait_send()

    def spread(self, m, buffer):
        at = self.own(m)
        return send_to(
            buffer.at[at], buffer.at[at], self.sems.at[self.which, m, 4], self.sems.at[self.which, m, 5], self.place.core
        )

    def publish(self, m, staged, out):
        at = rows_at(self.place.h * self.half, self.half)
        return (
            pltpu.make_async_copy(staged.at[m], out.at[m, at], self.sems.at[self.which, m, 6]),
            send_to(
                staged.at[m], out.at[m, at], self.sems.at[self.which, m, 4], self.sems.at[self.which, m, 5],
                self.place.core,
            ),
        )


def normal(values):
    scale = lax.rsqrt(jnp.mean(values * values, axis=-1, keepdims=True) + EPSILON)
    return scale, values * scale


def fold(values):
    return jnp.sum(values.reshape(values.shape[0] // 8, 8, values.shape[1]), axis=0)


def kernel(line, rows, n_ffn, names, *refs):
    v = dict(zip(names, refs))
    (lengths, order, mask, mix_gain, ffn_gain, taps_in) = (
        v[n] for n in ("lengths", "order", "mask", "mix_gain", "ffn_gain", "taps")
    )
    place = Place(line)
    n1, n2, g, term0, term1, r1h = (v[n] for n in ("n1", "n2", "g", "term0", "term1", "r1h"))
    inbox0, inbox1, across0, across1, across2 = (v[n] for n in ("inbox0", "inbox1", "across0", "across1", "across2"))
    pb, pc, px, po = (v[n] for n in ("pb", "pc", "px", "po"))
    bs, cs, xs, bx, ym, cat = (v[n] for n in ("bs", "cs", "xs", "bx", "ym", "cat"))
    sums, load = v["sums"], v["load"]
    tokens, width = n1.shape
    local = tokens // MICRO
    half = local // 2
    spans = local // SPAN
    chan = bs.shape[1]
    units = v["w_down"].shape[0]
    full = units // TILE
    rest = units - full * TILE
    docs = lengths.shape[1]
    rs = Scatter(
        place, 3 * n_ffn + 6, 3 * n_ffn, rows, v["sbuf"], v["obuf"], v["ybuf"], v["grads"],
        [v[n] for n in Scatter.NAMES],
    )
    branch = Sum(place, 0, term0, inbox0, across0, sums)
    second = Sum(place, 1, term1, inbox1, across1, sums)
    feed = Sum(place, 2, term0, inbox0, across2, sums)
    first = Sum(place, 3, term0, inbox1, across0, sums)

    barrier = pltpu.get_barrier_semaphore()
    for device in (place.pair, place.next, place.last, place.core, place.across):
        pl.semaphore_signal(barrier, inc=1, device_id=device, device_id_type=MESH)

    @pl.loop(0, line)
    def _(c):
        @pl.when(c != place.a)
        def _():
            pl.semaphore_signal(barrier, inc=1, device_id=(c * 2 + place.b, place.t), device_id_type=MESH)

    def loading(which, src, dst):
        return pltpu.make_async_copy(src, dst, load.at[which])

    projections = [
        loading(2, v["proj_b"], pb),
        loading(3, v["proj_x"], px),
        loading(4, v["proj_c"], pc),
        loading(5, v["proj_out"], po),
    ]
    cot_load = [loading(6 + m, v["cotangent"].at[m], g.at[m * local : (m + 1) * local]) for m in range(MICRO)]
    wgb, wub, wdb = v["wgb"], v["wub"], v["wdb"]

    def weights(j, slot):
        at = pl.ds(pl.multiple_of(j * TILE, TILE), TILE)
        return [
            pltpu.make_async_copy(v[src].at[at], dst.at[slot], v["wsem"].at[slot, q])
            for q, (src, dst) in enumerate((("w_gate", wgb), ("w_up", wub), ("w_down", wdb)))
        ]

    def rest_weights():
        slot = full % 2
        return [
            pltpu.make_async_copy(v[src].at[full * TILE :], dst.at[slot, 0:rest], v["wsem"].at[slot, q])
            for q, (src, dst) in enumerate((("w_gate", wgb), ("w_up", wub), ("w_down", wdb)))
        ]

    taps = taps_in[...].astype(f32)
    row_ids = lax.broadcasted_iota(jnp.int32, (SPAN, 1), 0)
    tap = [taps[k : k + 1, :] for k in range(3)]

    def span_facts(m, q):
        mine = order[m, place.s * spans + q]
        position = mine * SPAN + row_ids
        near = position >= 0
        far = position >= 0
        begin = jnp.int32(0)
        for n in range(docs):
            near = jnp.logical_and(near, position != begin)
            far = jnp.logical_and(far, position != begin + 1)
            begin = begin + lengths[m, n]
        return mine, near, jnp.logical_and(near, far)

    def terms(m, q, near, far, mine):
        here = bx[pl.ds(m * local + q * SPAN, SPAN), :].astype(f32)
        older = jnp.zeros((1, chan), f32)
        newer = jnp.zeros((1, chan), f32)
        for k in range(spans):
            took = order[m, place.before * spans + k] == mine - 1
            tail = v["halo_in"][m, k].astype(f32)
            older = older + jnp.where(took, tail[14:15], 0.0)
            newer = newer + jnp.where(took, tail[15:16], 0.0)
        far_term = pltpu.roll(here, 2, 0)
        far_term = jnp.where(row_ids == 0, older, jnp.where(row_ids == 1, newer, far_term))
        near_term = jnp.where(row_ids == 0, newer, pltpu.roll(here, 1, 0))
        return jnp.where(far, far_term, 0.0), jnp.where(near, near_term, 0.0), here

    def halo(m):
        return send_to(
            v["halo_out"].at[m], v["halo_in"].at[m], v["hsem"].at[0, m], v["hsem"].at[1, m], place.next
        )

    def halo_back(m):
        return send_to(
            v["back_out"].at[m], v["back_in"].at[m], v["hsem"].at[2, m], v["hsem"].at[3, m], place.last
        )

    def mixer_half(m, x):
        base = m * local

        @pl.loop(0, local // BLOCK)
        def _(r):
            at = rows_at(base + r * BLOCK, BLOCK)
            _, unit = normal(x[at, :].astype(f32))
            n1[at, :] = (unit * mix_gain[...]).astype(bf16)

        at = pl.ds(base, local)
        if m == 0:
            projections[0].wait()
        bs[at, :] = dot_nn(n1[at, :], pb[...])
        if m == 0:
            projections[1].wait()
        xs[at, :] = dot_nn(n1[at, :], px[...])
        for q in range(spans):
            rows_q = pl.ds(base + q * SPAN, SPAN)
            product = (bs[rows_q, :] * xs[rows_q, :]).astype(bf16)
            bx[rows_q, :] = product
            v["halo_out"][m, q] = product[SPAN - 16 :, :]

    def mixer_rest(m):
        base = m * local
        at = pl.ds(base, local)
        if m == 0:
            projections[2].wait()
        cs[at, :] = dot_nn(n1[at, :], pc[...])
        halo(m).wait_recv()
        for q in range(spans):
            rows_q = pl.ds(base + q * SPAN, SPAN)
            mine, near, far = span_facts(m, q)
            far_term, near_term, here = terms(m, q, near, far, mine)
            conv = tap[0] * far_term + tap[1] * near_term + tap[2] * here
            ym[rows_q, :] = (cs[rows_q, :] * conv).astype(bf16)
        if m == 0:
            projections[3].wait()
        term0[at, :] = dot_nn(ym[at, :], po[...]).astype(bf16)
        branch.start(m)

    def middle(m, x):
        branch.ready(m)

        @pl.loop(0, half // BLOCK)
        def _(r):
            at = rows_at(m * local + place.h * half + r * BLOCK, BLOCK)
            value = x[at, :].astype(f32) + branch.total(m, r)
            r1h[rows_at(m * half + r * BLOCK, BLOCK), :] = value
            _, unit = normal(value)
            n2[at, :] = (unit * ffn_gain[...]).astype(bf16)

        branch.spread(m, n2).start()

    def masked(m):
        cot_load[m].wait()
        for q in range(spans):
            kept = mask[m : m + 1, q * SPAN : (q + 1) * SPAN].astype(f32)
            kept = jnp.transpose(jnp.broadcast_to(kept, (SPAN, SPAN)))
            rows_q = pl.ds(m * local + q * SPAN, SPAN)
            for c in range(width // SPAN):
                cols = pl.ds(c * SPAN, SPAN)
                g[rows_q, cols] = (g[rows_q, cols].astype(f32) * kept).astype(bf16)

    def mixer_forward(x):
        x_load = [loading(m, v["tokens"].at[m], x.at[m * local : (m + 1) * local]) for m in range(MICRO)]
        for copy in [x_load[0]] + projections[:2] + [x_load[1]] + projections[2:] + cot_load + weights(0, 0):
            copy.start()
        x_load[0].wait()
        mixer_half(0, x)
        pl.semaphore_wait(barrier, 5 + line - 1)
        halo(0).start()
        x_load[1].wait()
        mixer_rest(0)
        mixer_half(1, x)
        halo(1).start()
        branch.relay(0)
        mixer_rest(1)
        masked(0)
        branch.relay(1)
        masked(1)
        middle(0, x)
        middle(1, x)
        for m in range(MICRO):
            branch.spread(m, n2).wait()
            branch.settle(m)

    pl.run_scoped(mixer_forward, pltpu.VMEM((tokens, width), bf16))

    def feed_forward(oacc, dacc, gs, us, ds, hb, dgb, dub):
        oacc[...] = jnp.zeros_like(oacc)
        dacc[...] = jnp.zeros_like(dacc)

        @pl.loop(0, n_ffn)
        def _(j):
            slot = lax.rem(j, 2)

            @pl.when(j < full)
            def _():
                for copy in weights(jnp.minimum(j, full - 1), slot):
                    copy.wait()

            if rest:

                @pl.when(j == full)
                def _():
                    for copy in rest_weights():
                        copy.wait()

            @pl.when(j + 1 < full)
            def _():
                for copy in weights(jnp.minimum(j + 1, full - 1), 1 - slot):
                    copy.start()

            if rest:

                @pl.when(j + 1 == full)
                def _():
                    for buffer in (wgb, wub, wdb):
                        buffer[full % 2, rest:, :] = jnp.zeros((TILE - rest, width), bf16)
                    for copy in rest_weights():
                        copy.start()

            gs[...] = dot_nt(n2[...], wgb[slot])
            us[...] = dot_nt(n2[...], wub[slot])
            ds[...] = dot_nt(g[...], wdb[slot])

            @pl.loop(0, tokens // 64)
            def _(r):
                at = rows_at(r * 64, 64)
                gate, up, back = gs[at, :], us[at, :], ds[at, :]
                sigma = jax.nn.sigmoid(gate)
                silu = gate * sigma
                hb[at, :] = (silu * up).astype(bf16)
                dgb[at, :] = (back * up * sigma * (1.0 + gate * (1.0 - sigma))).astype(bf16)
                dub[at, :] = (back * silu).astype(bf16)

            rs.produce(3 * j, [(0, dot_tn(g[...], hb[...]))])
            rs.produce(3 * j + 1, [(0, dot_tn(n2[...], dgb[...]))])
            rs.produce(3 * j + 2, [(0, dot_tn(n2[...], dub[...]))])
            oacc[...] += dot_nn(hb[...], wdb[slot])
            dacc[...] += dot_nn(dgb[...], wgb[slot])
            dacc[...] += dot_nn(dub[...], wub[slot])

        rs.flush(3 * n_ffn - 1)
        for m in range(MICRO):
            at = pl.ds(m * local, local)
            term1[at, :] = dacc[at, :].astype(bf16)
            second.start(m)
        for m in range(MICRO):
            at = pl.ds(m * local, local)
            term0[at, :] = oacc[at, :].astype(bf16)
            feed.start(m)

    pl.run_scoped(
        feed_forward,
        pltpu.VMEM((tokens, width), f32),
        pltpu.VMEM((tokens, width), f32),
        pltpu.VMEM((tokens, TILE), f32),
        pltpu.VMEM((tokens, TILE), f32),
        pltpu.VMEM((tokens, TILE), f32),
        pltpu.VMEM((tokens, TILE), bf16),
        pltpu.VMEM((tokens, TILE), bf16),
        pltpu.VMEM((tokens, TILE), bf16),
    )

    def backward(dr1, xh, dym, dbx, gain_one, gain_two, tap_rows):
        x_load = [
            loading(m, v["tokens"].at[m, rows_at(place.h * half, half)], xh.at[m * half : (m + 1) * half])
            for m in range(MICRO)
        ]
        for copy in x_load:
            copy.start()
        for m in range(MICRO):
            second.relay(m)
        for m in range(MICRO):
            feed.relay(m)
        gain_one[...] = jnp.zeros_like(gain_one)
        gain_two[...] = jnp.zeros_like(gain_two)
        rs.pump(0, 4)

        for m in range(MICRO):
            second.ready(m)

            @pl.loop(0, half // BLOCK)
            def _(r):
                at = rows_at(m * local + place.h * half + r * BLOCK, BLOCK)
                here = rows_at(m * half + r * BLOCK, BLOCK)
                grad = second.total(m, r)
                scale, unit = normal(r1h[here, :])
                gain_two[...] += fold(grad * unit)
                weighted = grad * ffn_gain[...]
                inner = jnp.mean(weighted * unit, axis=-1, keepdims=True)
                value = g[at, :].astype(f32) + scale * (weighted - unit * inner)
                dr1[here, :] = value
                n2[at, :] = value.astype(bf16)

            second.spread(m, n2).start()

        rs.pump(4, 8)
        for m in range(MICRO):
            feed.ready(m)

            @pl.loop(0, half // BLOCK)
            def _(r):
                here = rows_at(m * half + r * BLOCK, BLOCK)
                at = rows_at(r * BLOCK, BLOCK)
                across2[m, at, :] = (r1h[here, :] + feed.total(m, r)).astype(bf16)

            for copy in feed.publish(m, across2, v["block_out"]):
                copy.start()

        for m in range(MICRO):
            second.spread(m, n2).wait()
            second.settle(m)
        dym[...] = dot_nt(n2[...], po[...])
        tap_sums = [jnp.zeros((8, chan), f32) for _ in range(3)]
        for m in range(MICRO):
            for q in range(spans):
                rows_q = pl.ds(m * local + q * SPAN, SPAN)
                mine, near, far = span_facts(m, q)
                far_term, near_term, here = terms(m, q, near, far, mine)
                grad = dym[rows_q, :]
                cat[rows_q, chan : 2 * chan] = (
                    grad * (tap[0] * far_term + tap[1] * near_term + tap[2] * here)
                ).astype(bf16)
                grad = grad * cs[rows_q, :]
                for k, other in enumerate((far_term, near_term, here)):
                    tap_sums[k] = tap_sums[k] + fold(grad * other)
                old = jnp.where(far, tap[0] * grad, 0.0)
                mid = jnp.where(near, tap[1] * grad, 0.0)
                dbx[rows_q, :] = (
                    tap[2] * grad
                    + jnp.where(row_ids < SPAN - 1, pltpu.roll(mid, SPAN - 1, 0), 0.0)
                    + jnp.where(row_ids < SPAN - 2, pltpu.roll(old, SPAN - 2, 0), 0.0)
                )
                top_ids = row_ids[:8]
                v["back_out"][m, q] = jnp.where(top_ids < 2, old[:8], 0.0) + jnp.where(
                    top_ids == 1, mid[0:1], 0.0
                )
            halo_back(m).start()
        for k in range(3):
            tap_rows[k] = tap_sums[k]
        for m in range(MICRO):
            halo_back(m).wait_recv()
            for q in range(spans):
                rows_q = pl.ds(m * local + q * SPAN, SPAN)
                mine = order[m, place.s * spans + q]
                from_next = jnp.zeros((8, chan), f32)
                for k in range(spans):
                    took = order[m, place.after * spans + k] == mine + 1
                    from_next = from_next + jnp.where(took, v["back_in"][m, k], 0.0)
                value = dbx[rows_q, :]
                value = (
                    value
                    + jnp.where(row_ids == SPAN - 2, from_next[0:1], 0.0)
                    + jnp.where(row_ids == SPAN - 1, from_next[1:2], 0.0)
                )
                cat[rows_q, 0:chan] = (value * xs[rows_q, :]).astype(bf16)
                cat[rows_q, 2 * chan :] = (value * bs[rows_q, :]).astype(bf16)
        k0 = 3 * n_ffn
        wide = 3 * chan
        whole = wide // TILE
        for k in range(whole):
            rs.produce(k0 + k, [(0, dot_tn(n1[...], cat[:, k * TILE : (k + 1) * TILE]))])
        left = wide - whole * TILE
        rs.produce(
            k0 + whole,
            [
                (0, dot_tn(n1[...], cat[:, whole * TILE :])),
                (left, dot_tn(n2[...], ym[:, 0 : TILE - left])),
            ],
        )
        rs.produce(k0 + whole + 1, [(0, dot_tn(n2[...], ym[:, TILE - left :]))])
        rs.flush(k0 + whole + 1)

        for m in range(MICRO):
            feed.settle(m)
            at = pl.ds(m * local, local)
            term0[at, :] = (
                dot_nt(cat[at, 0:chan], pb[...])
                + dot_nt(cat[at, chan : 2 * chan], pc[...])
                + dot_nt(cat[at, 2 * chan :], px[...])
            ).astype(bf16)
            first.start(m)
        for m in range(MICRO):
            first.relay(m)
        rs.pump(8, 14)
        for m in range(MICRO):
            x_load[m].wait()
            first.ready(m)

            @pl.loop(0, half // BLOCK)
            def _(r):
                here = rows_at(m * half + r * BLOCK, BLOCK)
                at = rows_at(r * BLOCK, BLOCK)
                grad = first.total(m, r)
                scale, unit = normal(xh[here, :].astype(f32))
                gain_one[...] += fold(grad * unit)
                weighted = grad * mix_gain[...]
                inner = jnp.mean(weighted * unit, axis=-1, keepdims=True)
                across0[m, at, :] = (dr1[here, :] + scale * (weighted - unit * inner)).astype(bf16)

            for copy in first.publish(m, across0, v["d_tokens"]):
                copy.start()

        small, gather = v["small"], v["gather"]
        ssem = v["ssem"]
        small[0] = jnp.zeros((8, width), f32)
        small[0, 0:1, :] = jnp.sum(gain_one[...], axis=0, keepdims=True)
        small[0, 1:2, :] = jnp.sum(gain_two[...], axis=0, keepdims=True)
        for k in range(3):
            small[0, 2:3, k * chan : (k + 1) * chan] = jnp.sum(tap_rows[k], axis=0, keepdims=True)
        core = send_to(small.at[0], gather.at[0], ssem.at[0], ssem.at[1], place.core)
        core.start()
        core.wait_recv()
        small[1] = small[0] + jnp.where(lax.broadcasted_iota(jnp.int32, (8, 1), 0) < 2, gather[0], 0.0)
        pair = send_to(small.at[1], gather.at[1], ssem.at[2], ssem.at[3], place.pair)
        pair.start()
        pair.wait_recv()
        small[2] = small[1] + gather[1]

        def along(c, slot):
            return send_to(
                small.at[2], gather.at[2 + slot], ssem.at[4 + c], ssem.at[4 + line + slot], (c * 2 + place.b, place.t)
            )

        @pl.loop(0, line)
        def _(c):
            @pl.when(c != place.a)
            def _():
                along(c, place.a).start()

        gather[2 + place.a] = small[2]

        rs.pump(14, rs.n + line - 1)

        @pl.loop(0, line)
        def _(c):
            @pl.when(c != place.a)
            def _():
                along(c, c).wait_recv()
                along(c, place.a).wait_send()

        total = gather[2]
        for c in range(1, line):
            total = total + gather[2 + c]
        v["small_out"][...] = total
        core.wait_send()
        pair.wait_send()
        for m in range(MICRO):
            halo(m).wait_send()
            halo_back(m).wait_send()
            first.settle(m)
            for each, staged, out in ((feed, across2, v["block_out"]), (first, across0, v["d_tokens"])):
                for copy in each.publish(m, staged, out):
                    copy.wait()
        rs.finish()

    pl.run_scoped(
        backward,
        pltpu.VMEM((tokens // 2, width), f32),
        pltpu.VMEM((tokens // 2, width), bf16),
        pltpu.VMEM((tokens, chan), f32),
        pltpu.VMEM((tokens, chan), f32),
        pltpu.VMEM((8, width), f32),
        pltpu.VMEM((8, width), f32),
        pltpu.VMEM((3, 8, chan), f32),
    )


def body(
    seq_count,
    tokens,
    mix_gain,
    proj_b,
    proj_c,
    proj_x,
    conv_taps,
    proj_out,
    ffn_gain,
    w_gate,
    w_up,
    w_down,
    cotangent,
    seq_lengths,
    span_order,
    keep_mask,
):
    local, width = tokens.shape[1:]
    total = MICRO * local
    half = local // 2
    chan = proj_b.shape[1]
    units = w_gate.shape[1]
    n_ffn = pl.cdiv(units, TILE)
    line = seq_count // 2
    rows = width // seq_count
    n_tiles = 3 * n_ffn + 6
    spans = local // SPAN
    dma = pltpu.SemaphoreType.DMA
    vmem = pl.BlockSpec(memory_space=pltpu.VMEM)
    smem = pl.BlockSpec(memory_space=pltpu.SMEM)
    hbm = pl.BlockSpec(memory_space=pl.ANY)
    shape = jax.ShapeDtypeStruct
    inputs = [
        ("lengths", seq_lengths, smem),
        ("order", span_order, smem),
        ("mask", keep_mask, vmem),
        ("mix_gain", mix_gain.reshape(1, width), vmem),
        ("ffn_gain", ffn_gain.reshape(1, width), vmem),
        ("taps", conv_taps, vmem),
        ("tokens", tokens, hbm),
        ("cotangent", cotangent, hbm),
        ("proj_b", proj_b, hbm),
        ("proj_c", proj_c, hbm),
        ("proj_x", proj_x, hbm),
        ("proj_out", proj_out, hbm),
        ("w_gate", w_gate.T, hbm),
        ("w_up", w_up.T, hbm),
        ("w_down", w_down, hbm),
    ]
    piece = shape((n_tiles, line, rows, TILE), bf16)
    outputs = [
        ("block_out", shape(tokens.shape, bf16), hbm),
        ("d_tokens", shape(tokens.shape, bf16), hbm),
        ("grads", shape((4, rows, n_ffn * TILE), f32), hbm),
        ("small_out", shape((8, width), f32), vmem),
        ("sbuf", piece, hbm),
        ("obuf", piece, hbm),
        ("ybuf", piece, hbm),
    ]
    scratch = [
        ("n1", pltpu.VMEM((total, width), bf16)),
        ("n2", pltpu.VMEM((total, width), bf16)),
        ("g", pltpu.VMEM((total, width), bf16)),
        ("term0", pltpu.VMEM((total, width), bf16)),
        ("term1", pltpu.VMEM((total, width), bf16)),
        ("r1h", pltpu.VMEM((total // 2, width), f32)),
        ("inbox0", pltpu.VMEM((MICRO, half, width), bf16)),
        ("inbox1", pltpu.VMEM((MICRO, half, width), bf16)),
        ("across0", pltpu.VMEM((MICRO, half, width), bf16)),
        ("across1", pltpu.VMEM((MICRO, half, width), bf16)),
        ("across2", pltpu.VMEM((MICRO, half, width), bf16)),
        ("pb", pltpu.VMEM((width, chan), bf16)),
        ("pc", pltpu.VMEM((width, chan), bf16)),
        ("px", pltpu.VMEM((width, chan), bf16)),
        ("po", pltpu.VMEM((chan, width), bf16)),
        ("bs", pltpu.VMEM((total, chan), f32)),
        ("cs", pltpu.VMEM((total, chan), f32)),
        ("xs", pltpu.VMEM((total, chan), f32)),
        ("bx", pltpu.VMEM((total, chan), bf16)),
        ("ym", pltpu.VMEM((total, chan), bf16)),
        ("cat", pltpu.VMEM((total, 3 * chan), bf16)),
        ("wgb", pltpu.VMEM((2, TILE, width), bf16)),
        ("wub", pltpu.VMEM((2, TILE, width), bf16)),
        ("wdb", pltpu.VMEM((2, TILE, width), bf16)),
        ("halo_out", pltpu.VMEM((MICRO, spans, 16, chan), bf16)),
        ("halo_in", pltpu.VMEM((MICRO, spans, 16, chan), bf16)),
        ("back_out", pltpu.VMEM((MICRO, spans, 8, chan), f32)),
        ("back_in", pltpu.VMEM((MICRO, spans, 8, chan), f32)),
        ("small", pltpu.VMEM((3, 8, width), f32)),
        ("gather", pltpu.VMEM((2 + line, 8, width), f32)),
        ("load", dma((8,))),
        ("wsem", dma((2, 3))),
        ("sums", dma((4, MICRO, 7))),
        ("hsem", dma((4, MICRO))),
        ("ssem", dma((4 + 2 * line,))),
    ]
    scratch += list(zip(Scatter.NAMES, Scatter.scratch(n_tiles, line, rows)))
    names = [n for n, _, _ in inputs] + [n for n, _, _ in outputs] + [n for n, _ in scratch]
    results = pl.pallas_call(
        functools.partial(kernel, line, rows, n_ffn, names),
        out_shape=tuple(s for _, s, _ in outputs),
        in_specs=[s for _, _, s in inputs],
        out_specs=tuple(s for _, _, s in outputs),
        scratch_shapes=[s for _, s in scratch],
        compiler_params=pltpu.CompilerParams(
            collective_id=0, has_side_effects=True, vmem_limit_bytes=62 * 2**20 - 2**19
        ),
    )(*[a for _, a, _ in inputs])
    block_out, d_tokens, grads, small = results[:4]
    return (
        block_out,
        d_tokens,
        small[0],
        grads[3, :, 0:chan],
        grads[3, :, chan : 2 * chan],
        grads[3, :, 2 * chan : 3 * chan],
        small[2, : 3 * chan].reshape(3, chan),
        grads[3, :, 3 * chan : 4 * chan].T,
        small[1],
        grads[1, :, :units],
        grads[2, :, :units],
        grads[0, :, :units].T,
    )


def solution(mesh):
    placed = (
        P(None, "seq", None),
        P(),
        P(None, "tp"),
        P(None, "tp"),
        P(None, "tp"),
        P(None, "tp"),
        P("tp", None),
        P(),
        P(None, "tp"),
        P(None, "tp"),
        P("tp", None),
        P(None, "seq", None),
        P(),
        P(),
        P(None, "seq"),
    )
    return jax.shard_map(
        functools.partial(body, mesh.shape["seq"]),
        mesh=mesh,
        in_specs=placed,
        out_specs=(
            P(None, "seq", None),
            P(None, "seq", None),
            P(),
            P("seq", "tp"),
            P("seq", "tp"),
            P("seq", "tp"),
            P(None, "tp"),
            P("tp", "seq"),
            P(),
            P("seq", "tp"),
            P("seq", "tp"),
            P("tp", "seq"),
        ),
        check_vma=False,
    )
```

time: 918 us -> 408 us (0.44)
  waiting for transfers between devices: 654 us -> 0 us
  Pallas kernels: 0 us -> 390 us
  matrix products: 123 us -> 0 us
  other arithmetic: 57.6 us -> 0 us
  blocking collectives: 37.4 us -> 0 us
  between operations: 16.1 us -> 0.66 us
  starting transfers between devices: 10.9 us -> 0 us
    reduce_scatter x7 -> x0, waiting for transfers between devices: 461 us -> none  [the longest x1 108 us: body(): lax.psum_scatter(pending[5].astype(bf16), 'seq', scatter_dimension=0, til...]
    pallas_call x0 -> x1, Pallas kernels: none -> 390 us  [body(): pl.pallas_call(functools.partial(kernel, line, rows, n_ffn, names), out_s...]
    psum x3 -> x0, waiting for transfers between devices: 193 us -> none  [the longest x1 94.4 us: body(): lax.psum(feed_terms.astype(bf16), 'tp').astype(f32)]
    dot_general x46 -> x0, matrix products: 123 us -> none  [the longest x2 12.2 us: body(): feed_terms = jnp.dot(hidden, w_down, preferred_element_type=f32)]
    psum x1 -> x0, blocking collectives: 37.4 us -> none  [body(): small = lax.psum((gain_one, gain_two, taps_grad), 'seq')]
    convert_element_type x15 -> x0, other arithmetic: 18.8 us -> none  [the longest x1 2.36 us: body(): lax.psum_scatter(pending[6].astype(bf16), 'seq', scatter_dimension=1, til...]
    reduce_sum x6 -> x0, other arithmetic: 15.5 us -> none  [the longest x1 4.83 us: body(): gain_two = gain_two + jnp.sum(grad_second * normal_two, axis=0)]
    another operation x6 -> x0, other arithmetic: 11.2 us -> none  [the longest x2 6.93 us: body(): jnp.stack(input_grads)]
  transfers between devices with their start and end apart: 14 -> 0, of which waited for: 9 -> 0; matrix products, arithmetic and copies ran while one was open for 12% -> 0% of each run, Pallas kernels for 0% -> 0%
where the time goes in v3:
time: 408 us; the launch traced here: 407 us
  Pallas kernels  390 us (96%)
  local copies, waits for them, and re-layouts  16.1 us (4%)
    pallas_call x1, Pallas kernels, body(): pl.pallas_call(functools.partial(kernel, line, rows, n_ffn, names), out_s...  390 us

profile of v3, /device:TPU:0, one launch (start us, length us, event | category | flops | bytes accessed | tf_op | source)
XLA Modules:
  0.0 406.6 jit_solution(18063626348420369537)
XLA Ops:
  0.6 1.3 reshape.30.refs_3_
  1.9 1.3 reshape.31.refs_4_
  3.2 389.8 %shard_map.238 = (bf16[2,384,1536]{2,1,0:T(8,128)(2,1)}, bf16[2,384,1536]{2,1,0:T(8,128)(2,1)}, f32[4,192,1792]{2,1,0:T(8,128)}, f32[8,1536]{1,0:T(8,128)}, bf16...) custom-call(s32[2,6]{1,0:T(2,128)} %refs_0_.1, ...), custom_call_target="tpu_custom_call" | custom-call | tf_op jit(solution)/shard_map/pallas_call | solution.py:943
  393.1 0.8 slice_reduce_fusion.2
  393.9 1.5 slice_reduce_fusion
  395.4 0.6 reshape_squeeze.3
  396.0 2.3 slice_bitcast_fusion.3
  398.2 0.0 copy-start.1
  398.2 4.4 %slice_bitcast_fusion = (f32[1728,192]{0,1:T(8,128)}, f32[192,1728]{1,0:T(8,128)}, f32[192,1728]{1,0:T(8,128)}) fusion(f32[4,192,1792]{2,1,0:T(8,128)} %get-tuple-element.19), kind=kLoop, calls=%fused_computation | loop fusion | bytes 7962624 | tf_op jit(solution)/shard_map/transpose | solution.py:966
  402.6 0.0 copy-done.1
  402.6 0.0 copy-start
  402.6 1.4 copy.29
  404.0 1.1 copy-done
  405.2 1.4 copy.30
Async XLA Ops:
  398.2 4.4 %copy-start.1 = (bf16[2,384,1536]{2,1,0:T(8,128)(2,1)S(1)}, bf16[2,384,1536]{2,1,0:T(8,128)(2,1)}, u32[]{:S(2)}) copy-start(bf16[2,384,1536]{2,1,0:T(8,128)(2,1)} %get-tuple-element.41) | copy-start | bytes 7077892
  402.6 2.5 copy-start

commit v4 on v3

--- a/solution.py
+++ b/solution.py
@@ -12,6 +12,7 @@
 MESH = pl.DeviceIdType.MESH
 TILE = 256
 BLOCK = 32
+ROWS = 384
 f32 = jnp.float32
 bf16 = jnp.bfloat16
 
@@ -65,28 +66,44 @@
 
 class Scatter:
     NAMES = (
-        "stage", "zin", "fetch", "yfetch", "final", "stage_sem", "ysend_sem", "yrecv_sem", "zsend_sem", "zin_sem",
-        "fetch_sem", "yfetch_sem", "final_sem",
+        "stage", "zin", "fetch", "yfetch", "acc", "final", "swap_out", "swap_in", "swap_sum",
+        "stage_sem", "ysend_sem", "yrecv_sem", "zsend_sem", "zin_sem", "fetch_sem", "yfetch_sem", "final_sem",
+        "swap_sem", "sum_sem",
     )
-
-    def __init__(self, place, n_tiles, ffn_tiles, rows, sbuf, obuf, ybuf, out, scratch):
+    GROUP = 6
+
+    def __init__(self, place, n_tiles, ffn_tiles, rows, wbuf, ybuf, out, scratch):
         self.place, self.a, self.b, self.line = place, place.a, place.b, place.line
         self.n, self.ffn_tiles, self.rows = n_tiles, ffn_tiles, rows
-        self.sbuf, self.obuf, self.ybuf, self.out = sbuf, obuf, ybuf, out
+        self.wbuf, self.ybuf, self.out = wbuf, ybuf, out
         for name, ref in zip(self.NAMES, scratch):
             setattr(self, name, ref)
         self.slots = self.zin.shape[0]
-
-    @staticmethod
-    def scratch(n_tiles, line, rows):
-        slots = min(n_tiles, line + 1)
+        self.items = self.count(n_tiles)
+        self.steps = self.items + self.line - 1
+        self.swaps = self.swap_sum.shape[0]
+
+    @classmethod
+    def count(cls, n_tiles):
+        left = n_tiles % cls.GROUP
+        assert left != 1
+        return n_tiles // cls.GROUP * (cls.GROUP + 1) + (left + 1 if left else 0)
+
+    @classmethod
+    def scratch(cls, n_tiles, line, rows):
+        slots = line + 1
+        swaps = (n_tiles + cls.GROUP - 2) // cls.GROUP
         dma = pltpu.SemaphoreType.DMA
         return [
             pltpu.VMEM((2, 2, line, rows, TILE), bf16),
             pltpu.VMEM((slots, line + 1, rows, TILE), bf16),
             pltpu.VMEM((2, line, rows, TILE), bf16),
             pltpu.VMEM((2, line, rows, TILE), bf16),
+            pltpu.VMEM((rows, TILE), f32),
             pltpu.VMEM((2, rows, TILE), f32),
+            pltpu.VMEM((swaps, rows, TILE), bf16),
+            pltpu.VMEM((swaps, rows, TILE), bf16),
+            pltpu.VMEM((swaps, rows, TILE), f32),
             dma((2, 2)),
             dma((n_tiles,)),
             dma((n_tiles,)),
@@ -95,24 +112,33 @@
             dma((2, line)),
             dma((2, line)),
             dma((2,)),
+            dma((2, swaps)),
+            dma((swaps,)),
         ]
+
 
     def local(self, k):
         slot = lax.rem(k, 2)
         return (
-            pltpu.make_async_copy(self.stage.at[slot, 1 - self.b], self.sbuf.at[k], self.stage_sem.at[slot, 0]),
-            pltpu.make_async_copy(self.stage.at[slot, self.b], self.obuf.at[k], self.stage_sem.at[slot, 1]),
+            pltpu.make_async_copy(self.stage.at[slot, 1 - self.b], self.wbuf.at[k, 0], self.stage_sem.at[slot, 0]),
+            pltpu.make_async_copy(self.stage.at[slot, self.b], self.wbuf.at[k, 1], self.stage_sem.at[slot, 1]),
         )
 
-    def swap(self, k):
+    def halved(self, k):
+        return lax.rem(k, self.GROUP) != 1
+
+    def halve(self, k):
         return send_to(
-            self.sbuf.at[k], self.ybuf.at[k], self.ysend_sem.at[k], self.yrecv_sem.at[k], self.place.pair
+            self.wbuf.at[k, 0], self.ybuf.at[k], self.ysend_sem.at[k], self.yrecv_sem.at[k], self.place.pair
         )
 
     def flush(self, k):
         for copy in self.local(k):
             copy.wait()
-        self.swap(k).start()
+
+        @pl.when(self.halved(k))
+        def _():
+            self.halve(k).start()
 
     def produce(self, k, parts):
         @pl.when(jnp.logical_and(k != 0, k != self.ffn_tiles))
@@ -120,90 +146,124 @@
             self.flush(k - 1)
 
         slot = lax.rem(k, 2)
-        for offset, value in parts:
-            width = value.shape[1]
-            for c in range(self.line):
-                for half in range(2):
-                    row = (2 * c + half) * self.rows
-                    self.stage[slot, half, c, :, offset : offset + width] = value[row : row + self.rows].astype(bf16)
+        for offset, left, right in parts:
+            width = right().shape[1]
+            for start in range(0, left.shape[1], ROWS):
+                value = dot_tn(left[:, start : start + ROWS], right())
+                for n in range(ROWS // self.rows):
+                    c, half = divmod(start // self.rows + n, 2)
+                    self.stage[slot, half, c, :, offset : offset + width] = value[
+                        n * self.rows : (n + 1) * self.rows
+                    ].astype(bf16)
         for copy in self.local(k):
             copy.start()
 
-    def tile_of(self, i, c):
-        lag = jnp.where(c > self.a, self.a, jnp.where(c < self.a, self.line - 1 - self.a, jnp.maximum(self.a, self.line - 1 - self.a)))
-        return i - lag
-
-    def valid(self, i, c):
-        k = self.tile_of(i, c)
-        return jnp.logical_and(k >= 0, k < self.n)
+
+    def item_of(self, i, c):
+        a, far = self.a, self.line - 1 - self.a
+        return i - jnp.where(c > a, a, jnp.where(c < a, far, jnp.maximum(a, far)))
+
+    def inside(self, q):
+        return jnp.logical_and(q >= 0, q < self.items)
+
+    def item(self, q):
+        q = jnp.clip(q, 0, self.items - 1)
+        group = lax.div(q, self.GROUP + 1)
+        e = lax.rem(q, self.GROUP + 1)
+        tile = self.GROUP * group + jnp.where(e < 2, 1, jnp.where(e == 2, 0, e - 1))
+        return group, tile, jnp.minimum(e, 2)
+
+    def block(self, n):
+        return jnp.where(n < self.a, n, self.line - 1 - (n - self.a))
 
     def fetching(self, i, c):
         slot = lax.rem(i, 2)
-        k = jnp.clip(self.tile_of(i, c), 0, self.n - 1)
-        return (
-            pltpu.make_async_copy(self.obuf.at[k, c], self.fetch.at[slot, c], self.fetch_sem.at[slot, c]),
-            pltpu.make_async_copy(self.ybuf.at[k, c], self.yfetch.at[slot, c], self.yfetch_sem.at[slot, c]),
+        _, tile, kind = self.item(self.item_of(i, c))
+        side = jnp.where(kind == 0, 0, 1)
+        return pltpu.make_async_copy(
+            self.wbuf.at[tile, side, c], self.fetch.at[slot, c], self.fetch_sem.at[slot, c]
         )
+
+    def yfetching(self, i, c):
+        slot = lax.rem(i, 2)
+        _, tile, _ = self.item(self.item_of(i, c))
+        return pltpu.make_async_copy(self.ybuf.at[tile, c], self.yfetch.at[slot, c], self.yfetch_sem.at[slot, c])
 
     def onward(self, i, c, upward):
         slot = lax.rem(i, 2)
-        k = jnp.clip(self.tile_of(i, c), 0, self.n - 1)
-        at = lax.rem(k, self.slots)
-        place = c + 1 if upward else c
+        at = lax.rem(jnp.clip(self.item_of(i, c), 0, self.items - 1), self.slots)
+        where = c + 1 if upward else c
         return send_to(
             self.fetch.at[slot, c],
-            self.zin.at[at, place],
+            self.zin.at[at, where],
             self.zsend_sem.at[slot, c],
-            self.zin_sem.at[at, place],
+            self.zin_sem.at[at, where],
             self.place.up if upward else self.place.down,
         )
 
     def drain(self, i):
         @pl.loop(0, self.line)
         def _(c):
-            @pl.when(jnp.logical_and(self.valid(i, c), c != self.a))
+            @pl.when(jnp.logical_and(self.inside(self.item_of(i, c)), c != self.a))
             def _():
                 self.onward(i, c, False).wait_send()
 
-    def storing(self, k):
-        slot = lax.rem(k, 2)
-        is_ffn = k < self.ffn_tiles
-        kind = jnp.where(is_ffn, lax.rem(k, 3), 3)
-        column = jnp.where(is_ffn, lax.div(k, 3), k - self.ffn_tiles)
-        return pltpu.make_async_copy(
-            self.final.at[slot],
-            self.out.at[kind, :, pl.ds(pl.multiple_of(column * TILE, TILE), TILE)],
-            self.final_sem.at[slot],
+    def storing(self, q):
+        slot = lax.rem(q, 2)
+        _, tile, _ = self.item(q)
+        return pltpu.make_async_copy(self.final.at[slot], self.place_of(tile), self.final_sem.at[slot])
+
+    def place_of(self, tile):
+        is_ffn = tile < self.ffn_tiles
+        kind = jnp.where(is_ffn, lax.rem(tile, 3), 3)
+        column = jnp.where(is_ffn, lax.div(tile, 3), tile - self.ffn_tiles)
+        return self.out.at[kind, :, pl.ds(pl.multiple_of(column * TILE, TILE), TILE)]
+
+    def swapping(self, group):
+        return send_to(
+            self.swap_out.at[group], self.swap_in.at[group], self.swap_sem.at[0, group], self.swap_sem.at[1, group],
+            self.place.pair,
         )
 
-    def advance(self, i):
-        line, a = self.line, self.a
-
+    def begin(self, i):
         @pl.when(i >= 2)
         def _():
             self.drain(i - 2)
 
-        first = i - jnp.minimum(a, line - 1 - a)
-
-        @pl.when(jnp.logical_and(first >= 0, first < self.n))
+        q = i - jnp.minimum(self.a, self.line - 1 - self.a)
+        _, tile, kind = self.item(q)
+
+        @pl.when(jnp.logical_and(self.inside(q), kind == 2))
         def _():
-            self.swap(first).wait_recv()
+            self.halve(tile).wait_recv()
+
+        @pl.loop(0, self.line)
+        def _(n):
+            c = self.block(n)
+            q = self.item_of(i, c)
+            _, _, kind = self.item(q)
+
+            @pl.when(self.inside(q))
+            def _():
+                self.fetching(i, c).start()
+
+            @pl.when(jnp.logical_and(self.inside(q), kind == 2))
+            def _():
+                self.yfetching(i, c).start()
+
+    def complete(self, i):
+        line, a, acc = self.line, self.a, self.acc
+        slot = lax.rem(i, 2)
 
         @pl.loop(0, line)
-        def _(c):
-            @pl.when(self.valid(i, c))
-            def _():
-                for copy in self.fetching(i, c):
-                    copy.start()
-
-        slot = lax.rem(i, 2)
-
-        @pl.loop(0, line)
-        def _(c):
-            @pl.when(self.valid(i, c))
-            def _():
-                k = self.tile_of(i, c)
-                at = lax.rem(k, self.slots)
+        def _(n):
+            c = self.block(n)
+            q = self.item_of(i, c)
+
+            @pl.when(self.inside(q))
+            def _():
+                group, _, kind = self.item(q)
+                at = lax.rem(q, self.slots)
 
                 def arrival(where, device):
                     send_to(
@@ -213,9 +273,15 @@
                         self.zin_sem.at[at, where],
                         device,
                     ).wait_recv()
-
-                for copy in self.fetching(i, c):
-                    copy.wait()
+                    acc[...] += self.zin[at, where].astype(f32)
+
+                self.fetching(i, c).wait()
+                acc[...] = self.fetch[slot, c].astype(f32)
+
+                @pl.when(kind == 2)
+                def _():
+                    self.yfetching(i, c).wait()
+                    acc[...] += self.yfetch[slot, c].astype(f32)
 
                 @pl.when(jnp.logical_and(c >= a, a > 0))
                 def _():
@@ -225,24 +291,9 @@
                 def _():
                     arrival(c, self.place.up)
 
-                def base():
-                    return self.fetch[slot, c].astype(f32) + self.yfetch[slot, c].astype(f32)
-
                 @pl.when(c != a)
                 def _():
-                    @pl.when(jnp.logical_and(c > a, a > 0))
-                    def _():
-                        self.fetch[slot, c] = (base() + self.zin[at, c + 1].astype(f32)).astype(bf16)
-
-                    @pl.when(jnp.logical_and(c < a, a < line - 1))
-                    def _():
-                        self.fetch[slot, c] = (base() + self.zin[at, c].astype(f32)).astype(bf16)
-
-                    @pl.when(
-                        jnp.logical_or(jnp.logical_and(c > a, a == 0), jnp.logical_and(c < a, a == line - 1))
-                    )
-                    def _():
-                        self.fetch[slot, c] = base().astype(bf16)
+                    self.fetch[slot, c] = acc[...].astype(bf16)
 
                     @pl.when(c > a)
                     def _():
@@ -254,41 +305,60 @@
 
                 @pl.when(c == a)
                 def _():
-                    fslot = lax.rem(k, 2)
-
-                    @pl.when(k >= 2)
+                    _, _, older = self.item(q - 2)
+
+                    @pl.when(jnp.logical_and(q >= 2, older == 2))
                     def _():
-                        self.storing(k - 2).wait()
-
-                    @pl.when(jnp.logical_and(a > 0, a < line - 1))
+                        self.storing(q - 2).wait()
+
+                    @pl.when(kind == 0)
                     def _():
-                        self.final[fslot] = base() + self.zin[at, c].astype(f32) + self.zin[at, c + 1].astype(f32)
-
-                    @pl.when(a == 0)
+                        self.swap_out[group] = acc[...].astype(bf16)
+                        self.swapping(group).start()
+
+                    @pl.when(kind == 1)
                     def _():
-                        self.final[fslot] = base() + self.zin[at, c].astype(f32)
-
-                    @pl.when(a == line - 1)
+                        self.swap_sum[group] = acc[...]
+
+                    @pl.when(kind == 2)
                     def _():
-                        self.final[fslot] = base() + self.zin[at, c + 1].astype(f32)
-
-                    self.storing(k).start()
+                        self.final[lax.rem(q, 2)] = acc[...]
+                        self.storing(q).start()
 
     def pump(self, low, high):
         @pl.loop(low, high)
         def _(i):
-            self.advance(i)
+            self.begin(i)
+            self.complete(i)
 
     def finish(self):
-        steps = self.n + self.line - 1
-        self.drain(steps - 2)
-        self.drain(steps - 1)
-        self.storing(self.n - 2).wait()
-        self.storing(self.n - 1).wait()
+        def summed(group):
+            return pltpu.make_async_copy(
+                self.swap_sum.at[group], self.place_of(group * self.GROUP + 1), self.sum_sem.at[group]
+            )
+
+        @pl.loop(0, self.swaps)
+        def _(group):
+            self.swapping(group).wait_recv()
+            self.swap_sum[group] += self.swap_in[group].astype(f32)
+            summed(group).start()
+
+        self.drain(self.steps - 2)
+        self.drain(self.steps - 1)
+        for q in (self.items - 2, self.items - 1):
+            assert q % (self.GROUP + 1) >= 2
+            self.storing(q).wait()
+
+        @pl.loop(0, self.swaps)
+        def _(group):
+            self.swapping(group).wait_send()
+            summed(group).wait()
 
         @pl.loop(0, self.n)
         def _(k):
-            self.swap(k).wait_send()
+            @pl.when(self.halved(k))
+            def _():
+                self.halve(k).wait_send()
 
 
 class Sum:
@@ -347,14 +417,18 @@
         )
 
     def publish(self, m, staged, out):
-        at = rows_at(self.place.h * self.half, self.half)
+        target = out.at[rows_at((2 * m + self.place.h) * self.half, self.half)]
         return (
-            pltpu.make_async_copy(staged.at[m], out.at[m, at], self.sems.at[self.which, m, 6]),
+            pltpu.make_async_copy(staged.at[m], target, self.sems.at[self.which, m, 6]),
             send_to(
-                staged.at[m], out.at[m, at], self.sems.at[self.which, m, 4], self.sems.at[self.which, m, 5],
+                staged.at[m], target, self.sems.at[self.which, m, 4], self.sems.at[self.which, m, 5],
                 self.place.core,
             ),
         )
+
+
+def gain_row(gain):
+    return gain[...].reshape(1, gain.shape[0])
 
 
 def normal(values):
@@ -379,15 +453,16 @@
     sums, load = v["sums"], v["load"]
     tokens, width = n1.shape
     local = tokens // MICRO
-    half = local // 2
     spans = local // SPAN
+    pieces = MICRO * spans
+    half = SPAN // 2
     chan = bs.shape[1]
     units = v["w_down"].shape[0]
     full = units // TILE
     rest = units - full * TILE
     docs = lengths.shape[1]
     rs = Scatter(
-        place, 3 * n_ffn + 6, 3 * n_ffn, rows, v["sbuf"], v["obuf"], v["ybuf"], v["grads"],
+        place, 3 * n_ffn + 6, 3 * n_ffn, rows, v["wbuf"], v["ybuf"], v["grads"],
         [v[n] for n in Scatter.NAMES],
     )
     branch = Sum(place, 0, term0, inbox0, across0, sums)
@@ -415,20 +490,28 @@
         loading(5, v["proj_out"], po),
     ]
     cot_load = [loading(6 + m, v["cotangent"].at[m], g.at[m * local : (m + 1) * local]) for m in range(MICRO)]
-    wgb, wub, wdb = v["wgb"], v["wub"], v["wdb"]
+    wgu, wdb = v["wgu"], v["wdb"]
 
     def weights(j, slot):
         at = pl.ds(pl.multiple_of(j * TILE, TILE), TILE)
         return [
-            pltpu.make_async_copy(v[src].at[at], dst.at[slot], v["wsem"].at[slot, q])
-            for q, (src, dst) in enumerate((("w_gate", wgb), ("w_up", wub), ("w_down", wdb)))
+            pltpu.make_async_copy(v[src].at[at], dst, v["wsem"].at[slot, q])
+            for q, (src, dst) in enumerate(
+                (("w_gate", wgu.at[slot, 0:TILE]), ("w_up", wgu.at[slot, TILE:]), ("w_down", wdb.at[slot]))
+            )
         ]
 
     def rest_weights():
         slot = full % 2
         return [
-            pltpu.make_async_copy(v[src].at[full * TILE :], dst.at[slot, 0:rest], v["wsem"].at[slot, q])
-            for q, (src, dst) in enumerate((("w_gate", wgb), ("w_up", wub), ("w_down", wdb)))
+            pltpu.make_async_copy(v[src].at[full * TILE :], dst, v["wsem"].at[slot, q])
+            for q, (src, dst) in enumerate(
+                (
+                    ("w_gate", wgu.at[slot, 0:rest]),
+                    ("w_up", wgu.at[slot, TILE : TILE + rest]),
+                    ("w_down", wdb.at[slot, 0:rest]),
+                )
+            )
         ]
 
     taps = taps_in[...].astype(f32)
@@ -478,7 +561,7 @@
         def _(r):
             at = rows_at(base + r * BLOCK, BLOCK)
             _, unit = normal(x[at, :].astype(f32))
-            n1[at, :] = (unit * mix_gain[...]).astype(bf16)
+            n1[at, :] = (unit * gain_row(mix_gain)).astype(bf16)
 
         at = pl.ds(base, local)
         if m == 0:
@@ -506,23 +589,26 @@
             far_term, near_term, here = terms(m, q, near, far, mine)
             conv = tap[0] * far_term + tap[1] * near_term + tap[2] * here
             ym[rows_q, :] = (cs[rows_q, :] * conv).astype(bf16)
-        if m == 0:
-            projections[3].wait()
-        term0[at, :] = dot_nn(ym[at, :], po[...]).astype(bf16)
-        branch.start(m)
-
-    def middle(m, x):
-        branch.ready(m)
+            if m == 0 and q == 0:
+                projections[3].wait()
+            term0[rows_q, :] = dot_nn(ym[rows_q, :], po[...]).astype(bf16)
+            piece = m * spans + q
+            branch.start(piece)
+            if piece > 0:
+                branch.relay(piece - 1)
+
+    def middle(p, x):
+        branch.ready(p)
 
         @pl.loop(0, half // BLOCK)
         def _(r):
-            at = rows_at(m * local + place.h * half + r * BLOCK, BLOCK)
-            value = x[at, :].astype(f32) + branch.total(m, r)
-            r1h[rows_at(m * half + r * BLOCK, BLOCK), :] = value
+            at = rows_at((2 * p + place.h) * half + r * BLOCK, BLOCK)
+            value = x[at, :].astype(f32) + branch.total(p, r)
+            r1h[rows_at(p * half + r * BLOCK, BLOCK), :] = value
             _, unit = normal(value)
-            n2[at, :] = (unit * ffn_gain[...]).astype(bf16)
-
-        branch.spread(m, n2).start()
+            n2[at, :] = (unit * gain_row(ffn_gain)).astype(bf16)
+
+        branch.spread(p, n2).start()
 
     def masked(m):
         cot_load[m].wait()
@@ -546,20 +632,22 @@
         mixer_rest(0)
         mixer_half(1, x)
         halo(1).start()
-        branch.relay(0)
         mixer_rest(1)
         masked(0)
-        branch.relay(1)
+        branch.relay(pieces - 1)
         masked(1)
-        middle(0, x)
-        middle(1, x)
-        for m in range(MICRO):
-            branch.spread(m, n2).wait()
-            branch.settle(m)
+        for p in range(pieces):
+            middle(p, x)
+        for p in range(pieces):
+            branch.spread(p, n2).wait()
+            branch.settle(p)
 
     pl.run_scoped(mixer_forward, pltpu.VMEM((tokens, width), bf16))
 
-    def feed_forward(oacc, dacc, gs, us, ds, hb, dgb, dub):
+    def steps_by(j):
+        return jnp.where(j < 0, 0, 2 * j - jnp.where(j >= 3, 1, 0) - jnp.where(j >= 4, 1, 0))
+
+    def feed_forward(oacc, dacc, hb, dgu):
         oacc[...] = jnp.zeros_like(oacc)
         dacc[...] = jnp.zeros_like(dacc)
 
@@ -588,103 +676,119 @@
 
                 @pl.when(j + 1 == full)
                 def _():
-                    for buffer in (wgb, wub, wdb):
-                        buffer[full % 2, rest:, :] = jnp.zeros((TILE - rest, width), bf16)
+                    blank = jnp.zeros((TILE - rest, width), bf16)
+                    wgu[full % 2, rest:TILE, :] = blank
+                    wgu[full % 2, TILE + rest :, :] = blank
+                    wdb[full % 2, rest:, :] = blank
                     for copy in rest_weights():
                         copy.start()
 
-            gs[...] = dot_nt(n2[...], wgb[slot])
-            us[...] = dot_nt(n2[...], wub[slot])
-            ds[...] = dot_nt(g[...], wdb[slot])
-
-            @pl.loop(0, tokens // 64)
-            def _(r):
-                at = rows_at(r * 64, 64)
-                gate, up, back = gs[at, :], us[at, :], ds[at, :]
+            step = steps_by(j - 1)
+            one = steps_by(j) > step
+            two = steps_by(j) > step + 1
+
+            @pl.when(one)
+            def _():
+                rs.begin(step)
+
+            for m in range(MICRO):
+                at = slice(m * local, (m + 1) * local)
+                both = dot_nt(n2[at, :], wgu[slot])
+                back = dot_nt(g[at, :], wdb[slot])
+                gate, up = both[:, :TILE], both[:, TILE:]
                 sigma = jax.nn.sigmoid(gate)
                 silu = gate * sigma
                 hb[at, :] = (silu * up).astype(bf16)
-                dgb[at, :] = (back * up * sigma * (1.0 + gate * (1.0 - sigma))).astype(bf16)
-                dub[at, :] = (back * silu).astype(bf16)
-
-            rs.produce(3 * j, [(0, dot_tn(g[...], hb[...]))])
-            rs.produce(3 * j + 1, [(0, dot_tn(n2[...], dgb[...]))])
-            rs.produce(3 * j + 2, [(0, dot_tn(n2[...], dub[...]))])
+                dgu[at, :TILE] = (back * up * sigma * (1.0 + gate * (1.0 - sigma))).astype(bf16)
+                dgu[at, TILE:] = (back * silu).astype(bf16)
+
+            @pl.when(one)
+            def _():
+                rs.complete(step)
+
+            @pl.when(two)
+            def _():
+                rs.begin(step + 1)
+
+            rs.produce(3 * j, [(0, g, lambda: hb[...])])
             oacc[...] += dot_nn(hb[...], wdb[slot])
-            dacc[...] += dot_nn(dgb[...], wgb[slot])
-            dacc[...] += dot_nn(dub[...], wub[slot])
+
+            @pl.when(two)
+            def _():
+                rs.complete(step + 1)
+
+            rs.produce(3 * j + 1, [(0, n2, lambda: dgu[:, :TILE])])
+            dacc[...] += dot_nn(dgu[...], wgu[slot])
+            rs.produce(3 * j + 2, [(0, n2, lambda: dgu[:, TILE:])])
 
         rs.flush(3 * n_ffn - 1)
-        for m in range(MICRO):
-            at = pl.ds(m * local, local)
+        for p in range(pieces):
+            at = pl.ds(p * SPAN, SPAN)
             term1[at, :] = dacc[at, :].astype(bf16)
-            second.start(m)
-        for m in range(MICRO):
-            at = pl.ds(m * local, local)
+            second.start(p)
+            if p > 1:
+                second.relay(p - 2)
+        for p in range(pieces):
+            at = pl.ds(p * SPAN, SPAN)
             term0[at, :] = oacc[at, :].astype(bf16)
-            feed.start(m)
+            feed.start(p)
+            if p < 2:
+                second.relay(pieces - 2 + p)
 
     pl.run_scoped(
         feed_forward,
         pltpu.VMEM((tokens, width), f32),
         pltpu.VMEM((tokens, width), f32),
-        pltpu.VMEM((tokens, TILE), f32),
-        pltpu.VMEM((tokens, TILE), f32),
-        pltpu.VMEM((tokens, TILE), f32),
         pltpu.VMEM((tokens, TILE), bf16),
-        pltpu.VMEM((tokens, TILE), bf16),
-        pltpu.VMEM((tokens, TILE), bf16),
+        pltpu.VMEM((tokens, 2 * TILE), bf16),
     )
+    taken = [2 * (n_ffn - 1) - 2]
+
+    def pump(count):
+        rs.pump(taken[0], taken[0] + count)
+        taken[0] += count
 
     def backward(dr1, xh, dym, dbx, gain_one, gain_two, tap_rows):
         x_load = [
-            loading(m, v["tokens"].at[m, rows_at(place.h * half, half)], xh.at[m * half : (m + 1) * half])
-            for m in range(MICRO)
+            loading(
+                8 + p,
+                v["tokens"].at[p // spans, rows_at(p % spans * SPAN + place.h * half, half)],
+                xh.at[p * half : (p + 1) * half],
+            )
+            for p in range(pieces)
         ]
         for copy in x_load:
             copy.start()
-        for m in range(MICRO):
-            second.relay(m)
-        for m in range(MICRO):
-            feed.relay(m)
         gain_one[...] = jnp.zeros_like(gain_one)
         gain_two[...] = jnp.zeros_like(gain_two)
-        rs.pump(0, 4)
-
-        for m in range(MICRO):
-            second.ready(m)
+        pump(3)
+        for p in range(pieces):
+            feed.relay(p)
+        pump(1)
+
+        for p in range(pieces):
+            second.ready(p)
 
             @pl.loop(0, half // BLOCK)
             def _(r):
-                at = rows_at(m * local + place.h * half + r * BLOCK, BLOCK)
-                here = rows_at(m * half + r * BLOCK, BLOCK)
-                grad = second.total(m, r)
+                at = rows_at((2 * p + place.h) * half + r * BLOCK, BLOCK)
+                here = rows_at(p * half + r * BLOCK, BLOCK)
+                grad = second.total(p, r)
                 scale, unit = normal(r1h[here, :])
                 gain_two[...] += fold(grad * unit)
-                weighted = grad * ffn_gain[...]
+                weighted = grad * gain_row(ffn_gain)
                 inner = jnp.mean(weighted * unit, axis=-1, keepdims=True)
                 value = g[at, :].astype(f32) + scale * (weighted - unit * inner)
                 dr1[here, :] = value
                 n2[at, :] = value.astype(bf16)
 
-            second.spread(m, n2).start()
-
-        rs.pump(4, 8)
-        for m in range(MICRO):
-            feed.ready(m)
-
-            @pl.loop(0, half // BLOCK)
-            def _(r):
-                here = rows_at(m * half + r * BLOCK, BLOCK)
-                at = rows_at(r * BLOCK, BLOCK)
-                across2[m, at, :] = (r1h[here, :] + feed.total(m, r)).astype(bf16)
-
-            for copy in feed.publish(m, across2, v["block_out"]):
-                copy.start()
-
-        for m in range(MICRO):
-            second.spread(m, n2).wait()
-            second.settle(m)
+            second.spread(p, n2).start()
+            if p % 3 == 2:
+                pump(2)
+
+        for p in range(pieces):
+            second.spread(p, n2).wait()
+            second.settle(p)
         dym[...] = dot_nt(n2[...], po[...])
         tap_sums = [jnp.zeros((8, chan), f32) for _ in range(3)]
         for m in range(MICRO):
@@ -711,6 +815,7 @@
                     top_ids == 1, mid[0:1], 0.0
                 )
             halo_back(m).start()
+            pump(1)
         for k in range(3):
             tap_rows[k] = tap_sums[k]
         for m in range(MICRO):
@@ -734,59 +839,82 @@
         wide = 3 * chan
         whole = wide // TILE
         for k in range(whole):
-            rs.produce(k0 + k, [(0, dot_tn(n1[...], cat[:, k * TILE : (k + 1) * TILE]))])
+            rs.produce(k0 + k, [(0, n1, lambda k=k: cat[:, k * TILE : (k + 1) * TILE])])
+            if k == 1:
+                pump(1)
         left = wide - whole * TILE
         rs.produce(
             k0 + whole,
             [
-                (0, dot_tn(n1[...], cat[:, whole * TILE :])),
-                (left, dot_tn(n2[...], ym[:, 0 : TILE - left])),
+                (0, n1, lambda: cat[:, whole * TILE :]),
+                (left, n2, lambda: ym[:, 0 : TILE - left]),
             ],
         )
-        rs.produce(k0 + whole + 1, [(0, dot_tn(n2[...], ym[:, TILE - left :]))])
+        rs.produce(k0 + whole + 1, [(0, n2, lambda: ym[:, TILE - left :])])
         rs.flush(k0 + whole + 1)
-
+        pump(2)
+
+        for p in range(pieces):
+            feed.ready(p)
+
+            @pl.loop(0, half // BLOCK)
+            def _(r):
+                here = rows_at(p * half + r * BLOCK, BLOCK)
+                at = rows_at(r * BLOCK, BLOCK)
+                across2[p, at, :] = (r1h[here, :] + feed.total(p, r)).astype(bf16)
+
+            for copy in feed.publish(p, across2, v["block_out"]):
+                copy.start()
+            feed.settle(p)
+        pump(1)
         for m in range(MICRO):
-            feed.settle(m)
             at = pl.ds(m * local, local)
             term0[at, :] = (
                 dot_nt(cat[at, 0:chan], pb[...])
                 + dot_nt(cat[at, chan : 2 * chan], pc[...])
                 + dot_nt(cat[at, 2 * chan :], px[...])
             ).astype(bf16)
-            first.start(m)
-        for m in range(MICRO):
-            first.relay(m)
-        rs.pump(8, 14)
-        for m in range(MICRO):
-            x_load[m].wait()
-            first.ready(m)
+            for p in range(m * spans, (m + 1) * spans):
+                first.start(p)
+            pump(1)
+        for p in range(pieces):
+            first.relay(p)
+        pump(2)
+        for p in range(pieces):
+            x_load[p].wait()
+            first.ready(p)
 
             @pl.loop(0, half // BLOCK)
             def _(r):
-                here = rows_at(m * half + r * BLOCK, BLOCK)
+                here = rows_at(p * half + r * BLOCK, BLOCK)
                 at = rows_at(r * BLOCK, BLOCK)
-                grad = first.total(m, r)
+                grad = first.total(p, r)
                 scale, unit = normal(xh[here, :].astype(f32))
                 gain_one[...] += fold(grad * unit)
-                weighted = grad * mix_gain[...]
+                weighted = grad * gain_row(mix_gain)
                 inner = jnp.mean(weighted * unit, axis=-1, keepdims=True)
-                across0[m, at, :] = (dr1[here, :] + scale * (weighted - unit * inner)).astype(bf16)
-
-            for copy in first.publish(m, across0, v["d_tokens"]):
+                across0[p, at, :] = (dr1[here, :] + scale * (weighted - unit * inner)).astype(bf16)
+
+            for copy in first.publish(p, across0, v["d_tokens"]):
                 copy.start()
+            if p % 3 == 2:
+                pump(1)
 
         small, gather = v["small"], v["gather"]
         ssem = v["ssem"]
-        small[0] = jnp.zeros((8, width), f32)
-        small[0, 0:1, :] = jnp.sum(gain_one[...], axis=0, keepdims=True)
-        small[0, 1:2, :] = jnp.sum(gain_two[...], axis=0, keepdims=True)
+        side = width // 2
+        small[0] = jnp.zeros((8, side), f32)
+        for n, gain in enumerate((gain_one, gain_two)):
+            row = jnp.sum(gain[...], axis=0, keepdims=True)
+            small[0, 2 * n : 2 * n + 1, :] = row[:, :side]
+            small[0, 2 * n + 1 : 2 * n + 2, :] = row[:, side:]
         for k in range(3):
-            small[0, 2:3, k * chan : (k + 1) * chan] = jnp.sum(tap_rows[k], axis=0, keepdims=True)
+            at = k % 2 * chan
+            small[0, 4 + k // 2 : 5 + k // 2, at : at + chan] = jnp.sum(tap_rows[k], axis=0, keepdims=True)
         core = send_to(small.at[0], gather.at[0], ssem.at[0], ssem.at[1], place.core)
         core.start()
         core.wait_recv()
-        small[1] = small[0] + jnp.where(lax.broadcasted_iota(jnp.int32, (8, 1), 0) < 2, gather[0], 0.0)
+        small[1] = small[0] + jnp.where(lax.broadcasted_iota(jnp.int32, (8, 1), 0) < 4, gather[0], 0.0)
         pair = send_to(small.at[1], gather.at[1], ssem.at[2], ssem.at[3], place.pair)
         pair.start()
         pair.wait_recv()
@@ -805,7 +933,7 @@
 
         gather[2 + place.a] = small[2]
 
-        rs.pump(14, rs.n + line - 1)
+        rs.pump(taken[0], rs.steps)
 
         @pl.loop(0, line)
         def _(c):
@@ -823,6 +951,7 @@
         for m in range(MICRO):
             halo(m).wait_send()
             halo_back(m).wait_send()
+        for m in range(pieces):
             first.settle(m)
             for each, staged, out in ((feed, across2, v["block_out"]), (first, across0, v["d_tokens"])):
                 for copy in each.publish(m, staged, out):
@@ -861,7 +990,7 @@
 ):
     local, width = tokens.shape[1:]
     total = MICRO * local
-    half = local // 2
+    half = SPAN // 2
     chan = proj_b.shape[1]
     units = w_gate.shape[1]
     n_ffn = pl.cdiv(units, TILE)
@@ -869,6 +998,7 @@
     rows = width // seq_count
     n_tiles = 3 * n_ffn + 6
     spans = local // SPAN
+    pieces = MICRO * spans
     dma = pltpu.SemaphoreType.DMA
     vmem = pl.BlockSpec(memory_space=pltpu.VMEM)
     smem = pl.BlockSpec(memory_space=pltpu.SMEM)
@@ -878,8 +1008,8 @@
         ("lengths", seq_lengths, smem),
         ("order", span_order, smem),
         ("mask", keep_mask, vmem),
-        ("mix_gain", mix_gain.reshape(1, width), vmem),
-        ("ffn_gain", ffn_gain.reshape(1, width), vmem),
+        ("mix_gain", mix_gain, vmem),
+        ("ffn_gain", ffn_gain, vmem),
         ("taps", conv_taps, vmem),
         ("tokens", tokens, hbm),
         ("cotangent", cotangent, hbm),
@@ -891,15 +1021,13 @@
         ("w_up", w_up.T, hbm),
         ("w_down", w_down, hbm),
     ]
-    piece = shape((n_tiles, line, rows, TILE), bf16)
     outputs = [
-        ("block_out", shape(tokens.shape, bf16), hbm),
-        ("d_tokens", shape(tokens.shape, bf16), hbm),
+        ("block_out", shape((total, width), bf16), hbm),
+        ("d_tokens", shape((total, width), bf16), hbm),
         ("grads", shape((4, rows, n_ffn * TILE), f32), hbm),
-        ("small_out", shape((8, width), f32), vmem),
-        ("sbuf", piece, hbm),
-        ("obuf", piece, hbm),
-        ("ybuf", piece, hbm),
+        ("small_out", shape((8, width // 2), f32), vmem),
+        ("wbuf", shape((n_tiles, 2, line, rows, TILE), bf16), hbm),
+        ("ybuf", shape((n_tiles, line, rows, TILE), bf16), hbm),
     ]
     scratch = [
         ("n1", pltpu.VMEM((total, width), bf16)),
@@ -908,11 +1036,11 @@
         ("term0", pltpu.VMEM((total, width), bf16)),
         ("term1", pltpu.VMEM((total, width), bf16)),
         ("r1h", pltpu.VMEM((total // 2, width), f32)),
-        ("inbox0", pltpu.VMEM((MICRO, half, width), bf16)),
-        ("inbox1", pltpu.VMEM((MICRO, half, width), bf16)),
-        ("across0", pltpu.VMEM((MICRO, half, width), bf16)),
-        ("across1", pltpu.VMEM((MICRO, half, width), bf16)),
-        ("across2", pltpu.VMEM((MICRO, half, width), bf16)),
+        ("inbox0", pltpu.VMEM((pieces, half, width), bf16)),
+        ("inbox1", pltpu.VMEM((pieces, half, width), bf16)),
+        ("across0", pltpu.VMEM((pieces, half, width), bf16)),
+        ("across1", pltpu.VMEM((pieces, half, width), bf16)),
+        ("across2", pltpu.VMEM((pieces, half, width), bf16)),
         ("pb", pltpu.VMEM((width, chan), bf16)),
         ("pc", pltpu.VMEM((width, chan), bf16)),
         ("px", pltpu.VMEM((width, chan), bf16)),
@@ -923,18 +1051,17 @@
         ("bx", pltpu.VMEM((total, chan), bf16)),
         ("ym", pltpu.VMEM((total, chan), bf16)),
         ("cat", pltpu.VMEM((total, 3 * chan), bf16)),
-        ("wgb", pltpu.VMEM((2, TILE, width), bf16)),
-        ("wub", pltpu.VMEM((2, TILE, width), bf16)),
+        ("wgu", pltpu.VMEM((2, 2 * TILE, width), bf16)),
         ("wdb", pltpu.VMEM((2, TILE, width), bf16)),
         ("halo_out", pltpu.VMEM((MICRO, spans, 16, chan), bf16)),
         ("halo_in", pltpu.VMEM((MICRO, spans, 16, chan), bf16)),
         ("back_out", pltpu.VMEM((MICRO, spans, 8, chan), f32)),
         ("back_in", pltpu.VMEM((MICRO, spans, 8, chan), f32)),
-        ("small", pltpu.VMEM((3, 8, width), f32)),
-        ("gather", pltpu.VMEM((2 + line, 8, width), f32)),
-        ("load", dma((8,))),
+        ("small", pltpu.VMEM((3, 8, width // 2), f32)),
+        ("gather", pltpu.VMEM((2 + line, 8, width // 2), f32)),
+        ("load", dma((8 + pieces,))),
         ("wsem", dma((2, 3))),
-        ("sums", dma((4, MICRO, 7))),
+        ("sums", dma((4, pieces, 7))),
         ("hsem", dma((4, MICRO))),
         ("ssem", dma((4 + 2 * line,))),
     ]
@@ -952,15 +1079,15 @@
     )(*[a for _, a, _ in inputs])
     block_out, d_tokens, grads, small = results[:4]
     return (
-        block_out,
-        d_tokens,
-        small[0],
+        block_out.reshape(tokens.shape),
+        d_tokens.reshape(tokens.shape),
+        small[0:2].reshape(width),
         grads[3, :, 0:chan],
         grads[3, :, chan : 2 * chan],
         grads[3, :, 2 * chan : 3 * chan],
-        small[2, : 3 * chan].reshape(3, chan),
+        small[4:6].reshape(4, chan)[:3],
         grads[3, :, 3 * chan : 4 * chan].T,
-        small[1],
+        small[2:4].reshape(width),
         grads[1, :, :units],
         grads[2, :, :units],
         grads[0, :, :units].T,

time: 408 us -> 310 us (0.76)
  Pallas kernels: 390 us -> 295 us
    pallas_call x1, Pallas kernels: 390 us -> 295 us  [body(): pl.pallas_call(functools.partial(kernel, line, rows, n_ffn, names), out_s...]
where the time goes in v4:
time: 310 us; the launch traced here: 309 us
  Pallas kernels  295 us (95%)
  local copies, waits for them, and re-layouts  13.3 us (4%)
    pallas_call x1, Pallas kernels, body(): pl.pallas_call(functools.partial(kernel, line, rows, n_ffn, names), out_s...  295 us

profile of v4, /device:TPU:0, one launch (start us, length us, event | category | flops | bytes accessed | tf_op | source)
XLA Modules:
  0.0 308.9 jit_solution(3830622483280116078)
XLA Ops:
  0.7 294.9 %shard_map.238 = (bf16[768,1536]{1,0:T(8,128)(2,1)}, bf16[768,1536]{1,0:T(8,128)(2,1)}, f32[4,192,1792]{2,1,0:T(8,128)}, f32[8,768]{1,0:T(8,128)}, bf16[27,2,4,1...) custom-call(s32[2,6]{1,0:T(2,128)} %refs_0_.1, s32[2,24]{1,0:T(2,128)} %refs_1_.1, s32[2,384]{1,0:T(2,128)} %refs_2_.1, ...), custom_call_target="tpu_custom_call" | custom-call | tf_op jit(solution)/shard_map/pallas_call | solution.py:1070
  295.6 0.9 fusion
  296.5 0.6 reshape.43
  297.1 0.6 reshape.42
  297.7 0.6 reshape.41
  298.3 2.3 slice_bitcast_fusion.3
  300.5 0.0 copy-start.1
  300.5 4.4 %slice_bitcast_fusion = (f32[1728,192]{0,1:T(8,128)}, f32[192,1728]{1,0:T(8,128)}, f32[192,1728]{1,0:T(8,128)}) fusion(f32[4,192,1792]{2,1,0:T(8,128)} %get-tuple-element.19), kind=kLoop, calls=%fused_computation | loop fusion | bytes 7962624 | tf_op jit(solution)/shard_map/transpose | solution.py:1093
  304.9 0.0 copy-done.1
  304.9 0.0 copy-start
  304.9 1.4 copy.29
  306.3 1.1 copy-done
  307.4 1.4 copy.30
Async XLA Ops:
  300.5 4.4 %copy-start.1 = (bf16[768,1536]{1,0:T(8,128)(2,1)S(1)}, bf16[768,1536]{1,0:T(8,128)(2,1)}, u32[]{:S(2)}) copy-start(bf16[768,1536]{1,0:T(8,128)(2,1)} %get-tuple-element.16) | copy-start | bytes 7077892
  304.9 2.5 copy-start

commit v5 on v4

--- a/solution.py
+++ b/solution.py
@@ -70,7 +70,8 @@
         "stage_sem", "ysend_sem", "yrecv_sem", "zsend_sem", "zin_sem", "fetch_sem", "yfetch_sem", "final_sem",
         "swap_sem", "sum_sem",
     )
-    GROUP = 6
+    EARLY = 4
+    AHEAD = 7
 
     def __init__(self, place, n_tiles, ffn_tiles, rows, wbuf, ybuf, out, scratch):
         self.place, self.a, self.b, self.line = place, place.a, place.b, place.line
@@ -79,25 +80,26 @@
         for name, ref in zip(self.NAMES, scratch):
             setattr(self, name, ref)
         self.slots = self.zin.shape[0]
-        self.items = self.count(n_tiles)
-        self.steps = self.items + self.line - 1
+        self.items = n_tiles + self.EARLY
+        self.hop = self.hop_of(self.line)
+        self.held = self.fetch.shape[0]
+        self.steps = self.items + self.hop * (self.line - 1)
         self.swaps = self.swap_sum.shape[0]
 
-    @classmethod
-    def count(cls, n_tiles):
-        left = n_tiles % cls.GROUP
-        assert left != 1
-        return n_tiles // cls.GROUP * (cls.GROUP + 1) + (left + 1 if left else 0)
+    @staticmethod
+    def hop_of(line):
+        return 2 if line <= 4 else 1
 
     @classmethod
     def scratch(cls, n_tiles, line, rows):
-        slots = line + 1
-        swaps = (n_tiles + cls.GROUP - 2) // cls.GROUP
+        slots = cls.hop_of(line) * line + 1
+        held = 2 * cls.hop_of(line)
+        swaps = cls.EARLY
         dma = pltpu.SemaphoreType.DMA
         return [
             pltpu.VMEM((2, 2, line, rows, TILE), bf16),
             pltpu.VMEM((slots, line + 1, rows, TILE), bf16),
-            pltpu.VMEM((2, line, rows, TILE), bf16),
+            pltpu.VMEM((held, line, rows, TILE), bf16),
             pltpu.VMEM((2, line, rows, TILE), bf16),
             pltpu.VMEM((rows, TILE), f32),
             pltpu.VMEM((2, rows, TILE), f32),
@@ -107,9 +109,9 @@
             dma((2, 2)),
             dma((n_tiles,)),
             dma((n_tiles,)),
-            dma((2, line)),
+            dma((held, line)),
             dma((slots, line + 1)),
-            dma((2, line)),
+            dma((held, line)),
             dma((2, line)),
             dma((2,)),
             dma((2, swaps)),
@@ -125,7 +127,11 @@
         )
 
     def halved(self, k):
-        return lax.rem(k, self.GROUP) != 1
+        return jnp.logical_or(lax.rem(k, 3) == 0, k > self.early_tile(self.EARLY - 1))
+
+    @staticmethod
+    def early_tile(n):
+        return n + 1 + n // 2 if isinstance(n, int) else n + 1 + lax.div(n, 2)
 
     def halve(self, k):
         return send_to(
@@ -136,9 +142,11 @@
         for copy in self.local(k):
             copy.wait()
 
-        @pl.when(self.halved(k))
-        def _():
-            self.halve(k).start()
+    def halved_tile(self, n):
+        return jnp.where(n < 2, 3 * n, n + self.EARLY)
+
+    def start_halving(self, n):
+        self.halve(self.halved_tile(n)).start()
 
     def produce(self, k, parts):
         @pl.when(jnp.logical_and(k != 0, k != self.ffn_tiles))
@@ -161,24 +169,27 @@
 
     def item_of(self, i, c):
         a, far = self.a, self.line - 1 - self.a
-        return i - jnp.where(c > a, a, jnp.where(c < a, far, jnp.maximum(a, far)))
+        return i - self.hop * jnp.where(c > a, a, jnp.where(c < a, far, jnp.maximum(a, far)))
 
     def inside(self, q):
         return jnp.logical_and(q >= 0, q < self.items)
 
     def item(self, q):
         q = jnp.clip(q, 0, self.items - 1)
-        group = lax.div(q, self.GROUP + 1)
-        e = lax.rem(q, self.GROUP + 1)
-        tile = self.GROUP * group + jnp.where(e < 2, 1, jnp.where(e == 2, 0, e - 1))
-        return group, tile, jnp.minimum(e, 2)
+        early = q < 2 * self.EARLY
+        n = q - 2 * self.EARLY
+        tile = self.halved_tile(n)
+        return (
+            jnp.where(early, self.early_tile(lax.div(q, 2)), tile),
+            jnp.where(early, lax.rem(q, 2), 2),
+        )
 
     def block(self, n):
         return jnp.where(n < self.a, n, self.line - 1 - (n - self.a))
 
     def fetching(self, i, c):
-        slot = lax.rem(i, 2)
-        _, tile, kind = self.item(self.item_of(i, c))
+        slot = lax.rem(i, self.held)
+        tile, kind = self.item(self.item_of(i, c))
         side = jnp.where(kind == 0, 0, 1)
         return pltpu.make_async_copy(
             self.wbuf.at[tile, side, c], self.fetch.at[slot, c], self.fetch_sem.at[slot, c]
@@ -186,11 +197,11 @@
 
     def yfetching(self, i, c):
         slot = lax.rem(i, 2)
-        _, tile, _ = self.item(self.item_of(i, c))
+        tile, _ = self.item(self.item_of(i, c))
         return pltpu.make_async_copy(self.ybuf.at[tile, c], self.yfetch.at[slot, c], self.yfetch_sem.at[slot, c])
 
     def onward(self, i, c, upward):
-        slot = lax.rem(i, 2)
+        slot = lax.rem(i, self.held)
         at = lax.rem(jnp.clip(self.item_of(i, c), 0, self.items - 1), self.slots)
         where = c + 1 if upward else c
         return send_to(
@@ -210,7 +221,7 @@
 
     def storing(self, q):
         slot = lax.rem(q, 2)
-        _, tile, _ = self.item(q)
+        tile, _ = self.item(q)
         return pltpu.make_async_copy(self.final.at[slot], self.place_of(tile), self.final_sem.at[slot])
 
     def place_of(self, tile):
@@ -226,12 +237,19 @@
         )
 
     def begin(self, i):
-        @pl.when(i >= 2)
+        @pl.when(i >= self.held)
         def _():
-            self.drain(i - 2)
-
-        q = i - jnp.minimum(self.a, self.line - 1 - self.a)
-        _, tile, kind = self.item(q)
+            self.drain(i - self.held)
+
+        ahead = lax.div(3 * i, 4)
+        fresh = jnp.logical_and(ahead > lax.div(3 * i - 3, 4), i >= self.AHEAD)
+
+        @pl.when(jnp.logical_and(fresh, ahead + 2 < self.n - self.EARLY))
+        def _():
+            self.start_halving(ahead + 2)
+
+        q = i - self.hop * jnp.minimum(self.a, self.line - 1 - self.a)
+        tile, kind = self.item(q)
 
         @pl.when(jnp.logical_and(self.inside(q), kind == 2))
         def _():
@@ -241,7 +259,7 @@
         def _(n):
             c = self.block(n)
             q = self.item_of(i, c)
-            _, _, kind = self.item(q)
+            _, kind = self.item(q)
 
             @pl.when(self.inside(q))
             def _():
@@ -253,7 +271,8 @@
 
     def complete(self, i):
         line, a, acc = self.line, self.a, self.acc
-        slot = lax.rem(i, 2)
+        slot = lax.rem(i, self.held)
+        yslot = lax.rem(i, 2)
 
         @pl.loop(0, line)
         def _(n):
@@ -262,7 +281,8 @@
 
             @pl.when(self.inside(q))
             def _():
-                group, _, kind = self.item(q)
+                _, kind = self.item(q)
+                group = jnp.minimum(lax.div(q, 2), self.EARLY - 1)
                 at = lax.rem(q, self.slots)
 
                 def arrival(where, device):
@@ -281,7 +301,7 @@
                 @pl.when(kind == 2)
                 def _():
                     self.yfetching(i, c).wait()
-                    acc[...] += self.yfetch[slot, c].astype(f32)
+                    acc[...] += self.yfetch[yslot, c].astype(f32)
 
                 @pl.when(jnp.logical_and(c >= a, a > 0))
                 def _():
@@ -305,7 +325,7 @@
 
                 @pl.when(c == a)
                 def _():
-                    _, _, older = self.item(q - 2)
+                    _, older = self.item(q - 2)
 
                     @pl.when(jnp.logical_and(q >= 2, older == 2))
                     def _():
@@ -334,7 +354,7 @@
     def finish(self):
         def summed(group):
             return pltpu.make_async_copy(
-                self.swap_sum.at[group], self.place_of(group * self.GROUP + 1), self.sum_sem.at[group]
+                self.swap_sum.at[group], self.place_of(self.early_tile(group)), self.sum_sem.at[group]
             )
 
         @pl.loop(0, self.swaps)
@@ -343,10 +363,10 @@
             self.swap_sum[group] += self.swap_in[group].astype(f32)
             summed(group).start()
 
-        self.drain(self.steps - 2)
-        self.drain(self.steps - 1)
+        for n in range(self.held):
+            self.drain(self.steps - 1 - n)
         for q in (self.items - 2, self.items - 1):
-            assert q % (self.GROUP + 1) >= 2
+            assert q >= 2 * self.EARLY
             self.storing(q).wait()
 
         @pl.loop(0, self.swaps)
@@ -644,8 +664,7 @@
 
     pl.run_scoped(mixer_forward, pltpu.VMEM((tokens, width), bf16))
 
-    def steps_by(j):
-        return jnp.where(j < 0, 0, 2 * j - jnp.where(j >= 3, 1, 0) - jnp.where(j >= 4, 1, 0))
+    early = n_ffn - 1
 
     def feed_forward(oacc, dacc, hb, dgu):
         oacc[...] = jnp.zeros_like(oacc)
@@ -683,9 +702,8 @@
                     for copy in rest_weights():
                         copy.start()
 
-            step = steps_by(j - 1)
-            one = steps_by(j) > step
-            two = steps_by(j) > step + 1
+            step = jnp.maximum(j - 1, 0)
+            one = jnp.logical_and(j >= 1, j <= early)
 
             @pl.when(one)
             def _():
@@ -706,18 +724,11 @@
             def _():
                 rs.complete(step)
 
-            @pl.when(two)
-            def _():
-                rs.begin(step + 1)
-
             rs.produce(3 * j, [(0, g, lambda: hb[...])])
             oacc[...] += dot_nn(hb[...], wdb[slot])
 
-            @pl.when(two)
-            def _():
-                rs.complete(step + 1)
-
             rs.produce(3 * j + 1, [(0, n2, lambda: dgu[:, :TILE])])
+            rs.start_halving(j)
             dacc[...] += dot_nn(dgu[...], wgu[slot])
             rs.produce(3 * j + 2, [(0, n2, lambda: dgu[:, TILE:])])
 
@@ -742,7 +753,7 @@
         pltpu.VMEM((tokens, TILE), bf16),
         pltpu.VMEM((tokens, 2 * TILE), bf16),
     )
-    taken = [2 * (n_ffn - 1) - 2]
+    taken = [early]
 
     def pump(count):
         rs.pump(taken[0], taken[0] + count)
@@ -761,7 +772,7 @@
             copy.start()
         gain_one[...] = jnp.zeros_like(gain_one)
         gain_two[...] = jnp.zeros_like(gain_two)
-        pump(3)
+        pump(2)
         for p in range(pieces):
             feed.relay(p)
         pump(1)
@@ -783,7 +794,7 @@
                 n2[at, :] = value.astype(bf16)
 
             second.spread(p, n2).start()
-            if p % 3 == 2:
+            if p == 2:
                 pump(2)
 
         for p in range(pieces):
@@ -815,7 +826,7 @@
                     top_ids == 1, mid[0:1], 0.0
                 )
             halo_back(m).start()
-            pump(1)
+        pump(2)
         for k in range(3):
             tap_rows[k] = tap_sums[k]
         for m in range(MICRO):
@@ -840,7 +851,7 @@
         whole = wide // TILE
         for k in range(whole):
             rs.produce(k0 + k, [(0, n1, lambda k=k: cat[:, k * TILE : (k + 1) * TILE])])
-            if k == 1:
+            if k % 2 == 1:
                 pump(1)
         left = wide - whole * TILE
         rs.produce(
@@ -852,7 +863,8 @@
         )
         rs.produce(k0 + whole + 1, [(0, n2, lambda: ym[:, TILE - left :])])
         rs.flush(k0 + whole + 1)
-        pump(2)
+        assert taken[0] < rs.AHEAD + 13
+        pump(1)
 
         for p in range(pieces):
             feed.ready(p)
@@ -876,7 +888,6 @@
             ).astype(bf16)
             for p in range(m * spans, (m + 1) * spans):
                 first.start(p)
-            pump(1)
         for p in range(pieces):
             first.relay(p)
         pump(2)
@@ -897,7 +908,7 @@
 
             for copy in first.publish(p, across0, v["d_tokens"]):
                 copy.start()
-            if p % 3 == 2:
+            if p % 2 == 1:
                 pump(1)
 
         small, gather = v["small"], v["gather"]
@@ -913,10 +924,12 @@
             small[0, 4 + k // 2 : 5 + k // 2, at : at + chan] = jnp.sum(tap_rows[k], axis=0, keepdims=True)
         core = send_to(small.at[0], gather.at[0], ssem.at[0], ssem.at[1], place.core)
         core.start()
+        pump(1)
         core.wait_recv()
         small[1] = small[0] + jnp.where(lax.broadcasted_iota(jnp.int32, (8, 1), 0) < 4, gather[0], 0.0)
         pair = send_to(small.at[1], gather.at[1], ssem.at[2], ssem.at[3], place.pair)
         pair.start()
+        pump(3)
         pair.wait_recv()
         small[2] = small[1] + gather[1]
 
@@ -1077,21 +1090,93 @@
             collective_id=0, has_side_effects=True, vmem_limit_bytes=62 * 2**20 - 2**19
         ),
     )(*[a for _, a, _ in inputs])
-    block_out, d_tokens, grads, small = results[:4]
+    done = finish_call(results[:4], total, width, chan, units, rows)
     return (
-        block_out.reshape(tokens.shape),
-        d_tokens.reshape(tokens.shape),
-        small[0:2].reshape(width),
-        grads[3, :, 0:chan],
-        grads[3, :, chan : 2 * chan],
-        grads[3, :, 2 * chan : 3 * chan],
-        small[4:6].reshape(4, chan)[:3],
-        grads[3, :, 3 * chan : 4 * chan].T,
-        small[2:4].reshape(width),
-        grads[1, :, :units],
-        grads[2, :, :units],
-        grads[0, :, :units].T,
+        done[0].reshape(tokens.shape),
+        done[1].reshape(tokens.shape),
+        done[2],
+        done[3],
+        done[4],
+        done[5],
+        done[6],
+        done[7].T,
+        done[8],
+        done[9],
+        done[10],
+        done[11].T,
     )
+
+
+def finish_kernel(
+    block_in, tokens_in, grads, small, block_out, d_tokens, d_mixgain, d_b, d_c, d_x, d_taps, d_out, d_ffngain, d_gate, d_up, d_down
+):
+    chan, units = d_b.shape[1], d_gate.shape[1]
+    side = small.shape[1]
+    block_out[...] = block_in[...]
+    d_tokens[...] = tokens_in[...]
+    for n, out in enumerate((d_b, d_c, d_x, d_out)):
+        out[...] = grads[3, :, n * chan : (n + 1) * chan]
+    for n, out in enumerate((d_down, d_gate, d_up)):
+        out[...] = grads[n, :, :units]
+
+    @pl.when(pl.program_id(0) == 0)
+    def _():
+        for n, out in enumerate((d_mixgain, d_ffngain)):
+            out[0:side] = small[2 * n : 2 * n + 1, :].reshape(side)
+            out[side:] = small[2 * n + 1 : 2 * n + 2, :].reshape(side)
+        for k in range(3):
+            at = k % 2 * chan
+            d_taps[k : k + 1, :] = small[4 + k // 2 : 5 + k // 2, at : at + chan]
+
+
+def finish_call(arrays, tokens, width, chan, units, rows):
+    cuts = 6
+    shape = jax.ShapeDtypeStruct
+
+    def by_rows(count, columns):
+        return pl.BlockSpec((count // cuts, columns), lambda i: (i, 0))
+
+    def whole(*sizes):
+        return pl.BlockSpec(sizes, lambda i: (0,) * len(sizes))
+
+    return pl.pallas_call(
+        finish_kernel,
+        grid=(cuts,),
+        in_specs=[
+            by_rows(tokens, width),
+            by_rows(tokens, width),
+            pl.BlockSpec((4, rows // cuts, arrays[2].shape[2]), lambda i: (0, i, 0)),
+            whole(*arrays[3].shape),
+        ],
+        out_shape=(
+            shape((tokens, width), bf16),
+            shape((tokens, width), bf16),
+            shape((width,), f32),
+            shape((rows, chan), f32),
+            shape((rows, chan), f32),
+            shape((rows, chan), f32),
+            shape((3, chan), f32),
+            shape((rows, chan), f32),
+            shape((width,), f32),
+            shape((rows, units), f32),
+            shape((rows, units), f32),
+            shape((rows, units), f32),
+        ),
+        out_specs=(
+            by_rows(tokens, width),
+            by_rows(tokens, width),
+            whole(width),
+            by_rows(rows, chan),
+            by_rows(rows, chan),
+            by_rows(rows, chan),
+            whole(3, chan),
+            by_rows(rows, chan),
+            whole(width),
+            by_rows(rows, units),
+            by_rows(rows, units),
+            by_rows(rows, units),
+        ),
+    )(*arrays)
 
 
 def solution(mesh):

time: 310 us -> 287 us (0.926)
  local copies, waits for them, and re-layouts: 13.3 us -> 0 us
  Pallas kernels: 295 us -> 284 us
    pallas_call x1, Pallas kernels: 295 us -> 275 us  [body(): pl.pallas_call(functools.partial(kernel, line, rows, n_ffn, names), out_s...]
    pallas_call x0 -> x1, Pallas kernels: none -> 8.93 us  [finish_call(): pl.pallas_call(finish_kernel, grid=(cuts,), in_specs=[by_rows(tokens, wid...]
    transpose x2 -> x0, local copies, waits for them, and re-layouts: 6.65 us -> none  [the longest x1 4.39 us: body(): grads[0, :, :units]]
    unnamed x6 -> x0, local copies, waits for them, and re-layouts: 3.92 us -> none
where the time goes in v5:
time: 287 us; the launch traced here: 285 us
  Pallas kernels  284 us (99%)
    pallas_call x1, Pallas kernels, body(): pl.pallas_call(functools.partial(kernel, line, rows, n_ffn, names), out_s...  275 us
    pallas_call x1, Pallas kernels, finish_call(): pl.pallas_call(finish_kernel, grid=(cuts,), in_specs=[by_rows(tokens, wid...  8.93 us

profile of v5, /device:TPU:0, one launch (start us, length us, event | category | flops | bytes accessed | tf_op | source)
XLA Modules:
  0.0 285.1 jit_solution(13335082382483142450)
XLA Ops:
  0.7 275.3 %shard_map.238 = (bf16[768,1536]{1,0:T(8,128)(2,1)}, bf16[768,1536]{1,0:T(8,128)(2,1)}, f32[4,192,1792]{2,1,0:T(8,128)}, f32[8,768]{1,0:T(8,128)}, bf16[27,2,4,1...) custom-call(s32[2,6]{1,0:T(2,128)} %refs_0_.1, s32[2,24]{1,0:T(2,128)} %refs_1_.1, s32[2,384]{1,0:T(2,128)} %refs_2_.1, ...), custom_call_target="tpu_custom_call" | custom-call | tf_op jit(solution)/shard_map/pallas_call | solution.py:1083
  276.0 8.9 %shard_map.239 = (bf16[768,1536]{1,0:T(8,128)(2,1)}, bf16[768,1536]{1,0:T(8,128)(2,1)}, f32[1536]{0:T(1024)}, f32[192,384]{1,0:T(8,128)}, f32[192,384]{1,0:T(8,1...) custom-call(bf16[768,1536]{1,0:T(8,128)(2,1)} %get-tuple-element.28., ...), custom_call_target="tpu_custom_call" | custom-call | tf_op jit(solution)/shard_map/pallas_call | solution.py:1142

commit v6 on v5

--- a/solution.py
+++ b/solution.py
@@ -143,15 +143,17 @@
             copy.wait()
 
     def halved_tile(self, n):
-        return jnp.where(n < 2, 3 * n, n + self.EARLY)
+        return jnp.where(n <= self.EARLY // 2, 3 * n, n + self.EARLY)
 
     def start_halving(self, n):
         self.halve(self.halved_tile(n)).start()
 
-    def produce(self, k, parts):
-        @pl.when(jnp.logical_and(k != 0, k != self.ffn_tiles))
-        def _():
-            self.flush(k - 1)
+    def produce(self, k, parts, flushed=False):
+        if not flushed:
+
+            @pl.when(jnp.logical_and(k != 0, k != self.ffn_tiles))
+            def _():
+                self.flush(k - 1)
 
         slot = lax.rem(k, 2)
         for offset, left, right in parts:
@@ -470,6 +472,7 @@
     inbox0, inbox1, across0, across1, across2 = (v[n] for n in ("inbox0", "inbox1", "across0", "across1", "across2"))
     pb, pc, px, po = (v[n] for n in ("pb", "pc", "px", "po"))
     bs, cs, xs, bx, ym, cat = (v[n] for n in ("bs", "cs", "xs", "bx", "ym", "cat"))
+    hb, dgu = v["hb"], v["dgu"]
     sums, load = v["sums"], v["load"]
     tokens, width = n1.shape
     local = tokens // MICRO
@@ -584,17 +587,14 @@
             n1[at, :] = (unit * gain_row(mix_gain)).astype(bf16)
 
         at = pl.ds(base, local)
-        if m == 0:
-            projections[0].wait()
         bs[at, :] = dot_nn(n1[at, :], pb[...])
-        if m == 0:
-            projections[1].wait()
         xs[at, :] = dot_nn(n1[at, :], px[...])
         for q in range(spans):
             rows_q = pl.ds(base + q * SPAN, SPAN)
             product = (bs[rows_q, :] * xs[rows_q, :]).astype(bf16)
             bx[rows_q, :] = product
-            v["halo_out"][m, q] = product[SPAN - 16 :, :]
+            if m:
+                v["halo_out"][m, q] = product[SPAN - 16 :, :]
 
     def mixer_rest(m):
         base = m * local
@@ -640,14 +640,33 @@
                 cols = pl.ds(c * SPAN, SPAN)
                 g[rows_q, cols] = (g[rows_q, cols].astype(f32) * kept).astype(bf16)
 
-    def mixer_forward(x):
+    def front(slot, m):
+        at = slice(m * local, (m + 1) * local)
+        both = dot_nt(n2[at, :], wgu[slot])
+        back = dot_nt(g[at, :], wdb[slot])
+        gate, up = both[:, :TILE], both[:, TILE:]
+        sigma = jax.nn.sigmoid(gate)
+        silu = gate * sigma
+        hb[at, :] = (silu * up).astype(bf16)
+        dgu[at, :TILE] = (back * up * sigma * (1.0 + gate * (1.0 - sigma))).astype(bf16)
+        dgu[at, TILE:] = (back * silu).astype(bf16)
+
+    def mixer_forward(x, tails):
         x_load = [loading(m, v["tokens"].at[m], x.at[m * local : (m + 1) * local]) for m in range(MICRO)]
         for copy in [x_load[0]] + projections[:2] + [x_load[1]] + projections[2:] + cot_load + weights(0, 0):
             copy.start()
         x_load[0].wait()
-        mixer_half(0, x)
+        for q in range(spans):
+            _, unit = normal(x[(q + 1) * SPAN - 16 : (q + 1) * SPAN, :].astype(f32))
+            tails[q * 16 : (q + 1) * 16, :] = (unit * gain_row(mix_gain)).astype(bf16)
+        projections[0].wait()
+        projections[1].wait()
+        ends = (dot_nn(tails[...], pb[...]) * dot_nn(tails[...], px[...])).astype(bf16)
+        for q in range(spans):
+            v["halo_out"][0, q] = ends[q * 16 : (q + 1) * 16]
         pl.semaphore_wait(barrier, 5 + line - 1)
         halo(0).start()
+        mixer_half(0, x)
         x_load[1].wait()
         mixer_rest(0)
         mixer_half(1, x)
@@ -656,17 +675,20 @@
         masked(0)
         branch.relay(pieces - 1)
         masked(1)
-        for p in range(pieces):
-            middle(p, x)
-        for p in range(pieces):
-            branch.spread(p, n2).wait()
-            branch.settle(p)
-
-    pl.run_scoped(mixer_forward, pltpu.VMEM((tokens, width), bf16))
-
-    early = n_ffn - 1
-
-    def feed_forward(oacc, dacc, hb, dgu):
+        for m in range(MICRO):
+            for p in range(m * spans, (m + 1) * spans):
+                middle(p, x)
+            for p in range(m * spans, (m + 1) * spans):
+                branch.spread(p, n2).wait()
+                branch.settle(p)
+            if m == 0:
+                for copy in weights(0, 0):
+                    copy.wait()
+                front(0, 0)
+
+    pl.run_scoped(mixer_forward, pltpu.VMEM((tokens, width), bf16), pltpu.VMEM((16 * spans, width), bf16))
+
+    def feed_forward(oacc, dacc):
         oacc[...] = jnp.zeros_like(oacc)
         dacc[...] = jnp.zeros_like(dacc)
 
@@ -674,7 +696,7 @@
         def _(j):
             slot = lax.rem(j, 2)
 
-            @pl.when(j < full)
+            @pl.when(jnp.logical_and(j > 0, j < full))
             def _():
                 for copy in weights(jnp.minimum(j, full - 1), slot):
                     copy.wait()
@@ -702,35 +724,24 @@
                     for copy in rest_weights():
                         copy.start()
 
-            step = jnp.maximum(j - 1, 0)
-            one = jnp.logical_and(j >= 1, j <= early)
-
-            @pl.when(one)
+            @pl.when(j > 0)
             def _():
-                rs.begin(step)
-
-            for m in range(MICRO):
-                at = slice(m * local, (m + 1) * local)
-                both = dot_nt(n2[at, :], wgu[slot])
-                back = dot_nt(g[at, :], wdb[slot])
-                gate, up = both[:, :TILE], both[:, TILE:]
-                sigma = jax.nn.sigmoid(gate)
-                silu = gate * sigma
-                hb[at, :] = (silu * up).astype(bf16)
-                dgu[at, :TILE] = (back * up * sigma * (1.0 + gate * (1.0 - sigma))).astype(bf16)
-                dgu[at, TILE:] = (back * silu).astype(bf16)
-
-            @pl.when(one)
+                front(slot, 0)
+                front(slot, 1)
+
+            @pl.when(j == 0)
             def _():
-                rs.complete(step)
+                front(0, 1)
 
             rs.produce(3 * j, [(0, g, lambda: hb[...])])
             oacc[...] += dot_nn(hb[...], wdb[slot])
-
-            rs.produce(3 * j + 1, [(0, n2, lambda: dgu[:, :TILE])])
+            rs.flush(3 * j)
             rs.start_halving(j)
+            rs.produce(3 * j + 1, [(0, n2, lambda: dgu[:, :TILE])], flushed=True)
+            rs.produce(3 * j + 2, [(0, n2, lambda: dgu[:, TILE:])])
+            rs.begin(j)
             dacc[...] += dot_nn(dgu[...], wgu[slot])
-            rs.produce(3 * j + 2, [(0, n2, lambda: dgu[:, TILE:])])
+            rs.complete(j)
 
         rs.flush(3 * n_ffn - 1)
         for p in range(pieces):
@@ -750,10 +761,8 @@
         feed_forward,
         pltpu.VMEM((tokens, width), f32),
         pltpu.VMEM((tokens, width), f32),
-        pltpu.VMEM((tokens, TILE), bf16),
-        pltpu.VMEM((tokens, 2 * TILE), bf16),
     )
-    taken = [early]
+    taken = [n_ffn]
 
     def pump(count):
         rs.pump(taken[0], taken[0] + count)
@@ -1066,6 +1075,8 @@
         ("cat", pltpu.VMEM((total, 3 * chan), bf16)),
         ("wgu", pltpu.VMEM((2, 2 * TILE, width), bf16)),
         ("wdb", pltpu.VMEM((2, TILE, width), bf16)),
+        ("hb", pltpu.VMEM((total, TILE), bf16)),
+        ("dgu", pltpu.VMEM((total, 2 * TILE), bf16)),
         ("halo_out", pltpu.VMEM((MICRO, spans, 16, chan), bf16)),
         ("halo_in", pltpu.VMEM((MICRO, spans, 16, chan), bf16)),
         ("back_out", pltpu.VMEM((MICRO, spans, 8, chan), f32)),
@@ -1130,7 +1141,7 @@
 
 
 def finish_call(arrays, tokens, width, chan, units, rows):
-    cuts = 6
+    cuts = 3
     shape = jax.ShapeDtypeStruct
 
     def by_rows(count, columns):

time: 287 us -> 286 us (level)
  no operation moved by 1% of the time
where the time goes in v6:
time: 286 us; the launch traced here: 284 us
  Pallas kernels  283 us (99%)
    pallas_call x1, Pallas kernels, body(): pl.pallas_call(functools.partial(kernel, line, rows, n_ffn, names), out_s...  275 us
    pallas_call x1, Pallas kernels, finish_call(): pl.pallas_call(finish_kernel, grid=(cuts,), in_specs=[by_rows(tokens, wid...  8.69 us

profile of v6, /device:TPU:0, one launch (start us, length us, event | category | flops | bytes accessed | tf_op | source)
XLA Modules:
  0.0 284.2 jit_solution(11500092380065431701)
XLA Ops:
  0.7 274.7 %shard_map.238 = (bf16[768,1536]{1,0:T(8,128)(2,1)}, bf16[768,1536]{1,0:T(8,128)(2,1)}, f32[4,192,1792]{2,1,0:T(8,128)}, f32[8,768]{1,0:T(8,128)}, bf16[27,2,4,1...) custom-call(s32[2,6]{1,0:T(2,128)} %refs_0_.1, s32[2,24]{1,0:T(2,128)} %refs_1_.1, s32[2,384]{1,0:T(2,128)} %refs_2_.1, ...), custom_call_target="tpu_custom_call" | custom-call | tf_op jit(solution)/shard_map/pallas_call | solution.py:1094
  275.3 8.7 %shard_map.239 = (bf16[768,1536]{1,0:T(8,128)(2,1)}, bf16[768,1536]{1,0:T(8,128)(2,1)}, f32[1536]{0:T(1024)}, f32[192,384]{1,0:T(8,128)}, f32[192,384]{1,0:T(8,1...) custom-call(bf16[768,1536]{1,0:T(8,128)(2,1)} %get-tuple-element.28., ...), custom_call_target="tpu_custom_call" | custom-call | tf_op jit(solution)/shard_map/pallas_call | solution.py:1153

commit v7 on v6

--- a/solution.py
+++ b/solution.py
@@ -1101,30 +1101,28 @@
             collective_id=0, has_side_effects=True, vmem_limit_bytes=62 * 2**20 - 2**19
         ),
     )(*[a for _, a, _ in inputs])
-    done = finish_call(results[:4], total, width, chan, units, rows)
+    done = finish_call(results[2:4], width, chan, units, rows)
     return (
-        done[0].reshape(tokens.shape),
-        done[1].reshape(tokens.shape),
+        results[0].reshape(tokens.shape),
+        results[1].reshape(tokens.shape),
+        done[0],
+        done[1],
         done[2],
         done[3],
         done[4],
-        done[5],
+        done[5].T,
         done[6],
-        done[7].T,
+        done[7],
         done[8],
-        done[9],
-        done[10],
-        done[11].T,
+        done[9].T,
     )
 
 
 def finish_kernel(
-    block_in, tokens_in, grads, small, block_out, d_tokens, d_mixgain, d_b, d_c, d_x, d_taps, d_out, d_ffngain, d_gate, d_up, d_down
+    grads, small, d_mixgain, d_b, d_c, d_x, d_taps, d_out, d_ffngain, d_gate, d_up, d_down
 ):
     chan, units = d_b.shape[1], d_gate.shape[1]
     side = small.shape[1]
-    block_out[...] = block_in[...]
-    d_tokens[...] = tokens_in[...]
     for n, out in enumerate((d_b, d_c, d_x, d_out)):
         out[...] = grads[3, :, n * chan : (n + 1) * chan]
     for n, out in enumerate((d_down, d_gate, d_up)):
@@ -1140,7 +1138,7 @@
             d_taps[k : k + 1, :] = small[4 + k // 2 : 5 + k // 2, at : at + chan]
 
 
-def finish_call(arrays, tokens, width, chan, units, rows):
+def finish_call(arrays, width, chan, units, rows):
     cuts = 3
     shape = jax.ShapeDtypeStruct
 
@@ -1154,14 +1152,10 @@
         finish_kernel,
         grid=(cuts,),
         in_specs=[
-            by_rows(tokens, width),
-            by_rows(tokens, width),
-            pl.BlockSpec((4, rows // cuts, arrays[2].shape[2]), lambda i: (0, i, 0)),
-            whole(*arrays[3].shape),
+            pl.BlockSpec((4, rows // cuts, arrays[0].shape[2]), lambda i: (0, i, 0)),
+            whole(*arrays[1].shape),
         ],
         out_shape=(
-            shape((tokens, width), bf16),
-            shape((tokens, width), bf16),
             shape((width,), f32),
             shape((rows, chan), f32),
             shape((rows, chan), f32),
@@ -1174,8 +1168,6 @@
             shape((rows, units), f32),
         ),
         out_specs=(
-            by_rows(tokens, width),
-            by_rows(tokens, width),
             whole(width),
             by_rows(rows, chan),
             by_rows(rows, chan),

time: 286 us -> 287 us (level)
  local copies, waits for them, and re-layouts: 0 us -> 3.92 us
    unnamed x0 -> x6, local copies, waits for them, and re-layouts: none -> 3.92 us
where the time goes in v7:
time: 287 us; the launch traced here: 285 us
  Pallas kernels  281 us (98%)
  local copies, waits for them, and re-layouts  3.92 us (1%)
    pallas_call x1, Pallas kernels, body(): pl.pallas_call(functools.partial(kernel, line, rows, n_ffn, names), out_s...  275 us
    pallas_call x1, Pallas kernels, finish_call(): pl.pallas_call(finish_kernel, grid=(cuts,), in_specs=[pl.BlockSpec((4, ro...  6.02 us

profile of v7, /device:TPU:0, one launch (start us, length us, event | category | flops | bytes accessed | tf_op | source)
XLA Modules:
  0.0 285.4 jit_solution(15925727711031580503)
XLA Ops:
  0.7 274.7 %shard_map.238 = (bf16[768,1536]{1,0:T(8,128)(2,1)}, bf16[768,1536]{1,0:T(8,128)(2,1)}, f32[4,192,1792]{2,1,0:T(8,128)}, f32[8,768]{1,0:T(8,128)}, bf16[27,2,4,1...) custom-call(s32[2,6]{1,0:T(2,128)} %refs_0_.1, s32[2,24]{1,0:T(2,128)} %refs_1_.1, s32[2,384]{1,0:T(2,128)} %refs_2_.1, ...), custom_call_target="tpu_custom_call" | custom-call | tf_op jit(solution)/shard_map/pallas_call | solution.py:1094
  275.4 0.0 copy-start.1
  275.4 6.0 %shard_map.239 = (f32[1536]{0:T(1024)}, f32[192,384]{1,0:T(8,128)}, f32[192,384]{1,0:T(8,128)}, f32[192,384]{1,0:T(8,128)}, f32[3,384]{1,0:T(4,128)}, /*index=5*...) custom-call(f32[4,192,1792]{2,1,0:T(8,128)} %get-tuple-element.28.grads, ...), custom_call_target="tpu_custom_call" | custom-call | tf_op jit(solution)/shard_map/pallas_call | solution.py:1151
  281.4 0.0 copy-done.1
  281.4 0.0 copy-start
  281.4 1.4 copy.29
  282.8 1.1 copy-done
  283.9 1.4 copy.30
Async XLA Ops:
  275.4 6.0 %copy-start.1 = (bf16[768,1536]{1,0:T(8,128)(2,1)S(1)}, bf16[768,1536]{1,0:T(8,128)(2,1)}, u32[]{:S(2)}) copy-start(bf16[768,1536]{1,0:T(8,128)(2,1)} %get-tuple-element.26) | copy-start | bytes 7077892
  281.4 2.5 copy-start
